TPU v7x, 32 devices: a whole 2x2x4 slice. The times are simulated.
32 devices in a mesh: group: 2 (over x), space: 16 (over z, y, core).
Axes of the slice: x: 2, y: 2, z: 4, core: 2. Of those that a mesh axis runs over, the one named last changes fastest.
Arguments:
- node_feat: bfloat16 [8192, 512], P(('group', 'space')), parts along dimension 0, may hold values from -6 to 6
- edge_feat: bfloat16 [32768, 512], P(('group', 'space')), parts along dimension 0, may hold values from -6 to 6
- grad_nodes: bfloat16 [8192, 512], P(('group', 'space')), parts along dimension 0, may hold values from -6 to 6
- grad_edges: bfloat16 [32768, 512], P(('group', 'space')), parts along dimension 0, may hold values from -6 to 6
- edge_first: bfloat16 [1536, 512], replicated, may hold values from -0.15625 to 0.15625
- edge_second: bfloat16 [512, 512], replicated, may hold values from -0.25 to 0.25
- node_first: bfloat16 [1024, 512], replicated, may hold values from -0.1875 to 0.1875
- node_second: bfloat16 [512, 512], replicated, may hold values from -0.25 to 0.25
- gains: float32 [2, 512], replicated, may hold values from 0.1 to 1.9
- edge_peer: int32 [32768], P(('group', 'space')), parts along dimension 0, may hold values from 0 to 15, as said below
- edge_slot: int32 [32768], P(('group', 'space')), parts along dimension 0, may hold values from 0 to 255, as said below
- edge_recv: int32 [32768], P(('group', 'space')), parts along dimension 0, may hold values from 0 to 255
- send_index: int32 [32, 16, 8], P(('group', 'space')), parts along dimension 0, may hold values from 0 to 255
- live_blocks: int32 [32], P(('group', 'space')), parts along dimension 0, may hold values from 1 to 8, as said below
Outputs:
- grad_node_feat: bfloat16 [8192, 512], P(('group', 'space')), parts along dimension 0
- grad_edge_feat: bfloat16 [32768, 512], P(('group', 'space')), parts along dimension 0
- grad_edge_first: float32 [3072, 512], P(('group', 'space')), parts along dimension 0
- grad_edge_second: float32 [1024, 512], P(('group', 'space')), parts along dimension 0
- grad_node_first: float32 [2048, 512], P(('group', 'space')), parts along dimension 0
- grad_node_second: float32 [1024, 512], P(('group', 'space')), parts along dimension 0
- grad_gains: float32 [4, 512], P('group'), parts along dimension 0
There are 2 independent parts, one for each index of `group`. A program takes and returns all parts, laid end to end along the dimension named above; an argument that names none is the same for every part. Nothing has to cross between parts.
Inputs may be any that keep to these rules, and one draw needn't show every extreme that they name: `edge_peer`: the rows of device d name d itself or another device. `edge_slot`: where edge_peer names the edge's own device the value is a local row; else it is a slot below 8. `live_blocks`: some device has all 8 blocks live.
All inputs are finite; a program needn't handle non-finite values.
Results may differ from a plain program's by a relative error of at most 0.008.
Values may be sent and summed in bfloat16 or wider, within the bound.
No kernel may reach another device: no remote copies, remote signals or barrier semaphores. Data moves between devices by JAX's collectives and lax.ppermute only.
A program may use at most 128 MiB of HBM per device.

v0:
```python
import jax
import jax.numpy as jnp
from jax import lax
from jax.sharding import PartitionSpec as P

EDGE_BLOCK = 128


EPS = 1e-05


def times_transposed(left, right):
    return lax.dot_general(
        left, right, (((1,), (1,)), ((), ())), preferred_element_type=jnp.float32
    )


def transposed_times(left, right):
    return lax.dot_general(
        left, right, (((0,), (0,)), ((), ())), preferred_element_type=jnp.float32
    )


def silu_slope(pre_act):
    sigmoid_val = jax.nn.sigmoid(pre_act)
    return sigmoid_val * (1.0 + pre_act * (1.0 - sigmoid_val))


def mlp_forward(inputs, first_weight, second, gain_row):
    pre_act = jnp.dot(inputs, first_weight, preferred_element_type=jnp.float32)
    hidden = jax.nn.silu(pre_act).astype(jnp.bfloat16)
    post_act = jnp.dot(hidden, second, preferred_element_type=jnp.float32)
    centred = post_act - jnp.mean(post_act, axis=-1, keepdims=True)
    inv_std = lax.rsqrt(jnp.mean(centred * centred, axis=-1, keepdims=True) + EPS)
    normed = centred * inv_std
    return (pre_act, hidden, normed, inv_std, normed * gain_row)


def mlp_backward(grad_out, inputs, first_weight, second, gain_row, saved):
    pre_act, hidden, normed, inv_std = saved
    grad_gain = jnp.sum(grad_out * normed, axis=0)
    grad_normed = grad_out * gain_row
    grad_post = inv_std * (
        grad_normed
        - jnp.mean(grad_normed, axis=-1, keepdims=True)
        - normed * jnp.mean(grad_normed * normed, axis=-1, keepdims=True)
    )
    grad_post = grad_post.astype(jnp.bfloat16)
    grad_hidden = times_transposed(grad_post, second)
    grad_pre = (grad_hidden * silu_slope(pre_act)).astype(jnp.bfloat16)
    grad_in = times_transposed(grad_pre, first_weight)
    return (
        grad_in,
        transposed_times(inputs, grad_pre),
        transposed_times(hidden, grad_post),
        grad_gain,
    )


def shards(
    node_feat,
    edge_feat,
    grad_nodes,
    grad_edges,
    edge_first,
    edge_second,
    node_first,
    node_second,
    gains,
    edge_peer,
    edge_slot,
    edge_recv,
    send_index,
    live_blocks,
):
    node_rows, feat_width = node_feat.shape
    edge_rows = edge_feat.shape[0]
    devices = lax.axis_size("space")
    own_index = lax.axis_index("space")
    send_table = send_index[0]
    capacity = send_table.shape[1]
    lookup_rows = node_rows + devices * capacity
    outgoing = node_feat[send_table.reshape(-1)].reshape(devices, capacity, feat_width)
    incoming_rows = lax.all_to_all(outgoing, "space", split_axis=0, concat_axis=0, tiled=True)
    lookup = jnp.concatenate(
        [node_feat, incoming_rows.reshape(devices * capacity, feat_width)], axis=0
    )
    senders = jnp.where(
        edge_peer == own_index, edge_slot, node_rows + edge_peer * capacity + edge_slot
    )
    block_count = live_blocks[0]
    live_count = block_count * EDGE_BLOCK

    def edge_ids(row_start, row_count):
        live_now = row_start + jnp.arange(row_count, dtype=jnp.int32) < live_count
        return (senders, edge_recv, live_now)

    def over_edges(step, running):
        return step(running, 0, edge_rows)

    def forward_step(running, row_start, row_count):
        aggregate, stored = running
        sender_ids, receiver_ids, live_now = edge_ids(row_start, row_count)
        inputs = jnp.concatenate([lookup[sender_ids], node_feat[receiver_ids], edge_feat], axis=1)
        outputs = mlp_forward(inputs, edge_first, edge_second, gains[0])
        aggregate = aggregate.at[receiver_ids].add(jnp.where(live_now[:, None], outputs[4], 0.0))
        pieces = (inputs, outputs[0], outputs[1], outputs[2], outputs[3])
        stored = tuple((piece for piece in pieces))
        return (aggregate, stored)

    empty_store = (
        jnp.zeros((edge_rows, 3 * feat_width), jnp.bfloat16),
        jnp.zeros((edge_rows, feat_width), jnp.float32),
        jnp.zeros((edge_rows, feat_width), jnp.bfloat16),
        jnp.zeros((edge_rows, feat_width), jnp.float32),
        jnp.zeros((edge_rows, 1), jnp.float32),
    )
    aggregate, stored = over_edges(
        forward_step, (jnp.zeros((node_rows, feat_width), jnp.float32), empty_store)
    )
    node_inputs = jnp.concatenate([node_feat, aggregate.astype(jnp.bfloat16)], axis=1)
    node_fwd = mlp_forward(node_inputs, node_first, node_second, gains[1])
    node_grad_in, grad_node_first, grad_node_second, node_gain = mlp_backward(
        grad_nodes.astype(jnp.float32), node_inputs, node_first, node_second, gains[1], node_fwd[:4]
    )
    grad_aggregate = node_grad_in[:, feat_width:].astype(jnp.bfloat16)

    def backward_step(running, row_start, row_count):
        totals, first_sum, second_sum, gain_sum, edge_out = running
        sender_ids, receiver_ids, live_now = edge_ids(row_start, row_count)
        kept = tuple((buffer for buffer in stored))
        inputs = kept[0]
        grad_msg = jnp.where(
            live_now[:, None],
            grad_edges.astype(jnp.float32) + grad_aggregate[receiver_ids].astype(jnp.float32),
            0.0,
        )
        grad_in, first_part, second_part, gain_part = mlp_backward(
            grad_msg, inputs, edge_first, edge_second, gains[0], kept[1:]
        )
        totals = (
            totals.at[sender_ids]
            .add(grad_in[:, :feat_width])
            .at[receiver_ids]
            .add(grad_in[:, feat_width : 2 * feat_width])
        )
        new_rows = (grad_edges.astype(jnp.float32) + grad_in[:, 2 * feat_width :]).astype(
            jnp.bfloat16
        )
        edge_out = new_rows
        return (totals, first_part, second_part, gain_part, edge_out)

    start_state = (
        jnp.zeros((lookup_rows, feat_width), jnp.float32),
        jnp.zeros((3 * feat_width, feat_width), jnp.float32),
        jnp.zeros((feat_width, feat_width), jnp.float32),
        jnp.zeros((feat_width,), jnp.float32),
        grad_edges,
    )
    edge_state = over_edges(backward_step, start_state)
    node_shares = (
        lax.psum_scatter(grad_node_first, "space", scatter_dimension=0, tiled=True),
        lax.psum_scatter(grad_node_second, "space", scatter_dimension=0, tiled=True),
    )
    totals, first_sum, second_sum, gain_sum, grad_edge_feat = edge_state
    returned = lax.all_to_all(
        totals[node_rows:].reshape(devices, capacity, feat_width).astype(jnp.bfloat16),
        "space",
        split_axis=0,
        concat_axis=0,
        tiled=True,
    ).astype(jnp.float32)
    node_totals = (
        totals[:node_rows]
        .at[send_table.reshape(-1)]
        .add(returned.reshape(devices * capacity, feat_width))
    )
    grad_node_feat = (
        grad_nodes.astype(jnp.float32) + node_grad_in[:, :feat_width] + node_totals
    ).astype(jnp.bfloat16)
    edge_shares = (
        lax.psum_scatter(first_sum, "space", scatter_dimension=0, tiled=True),
        lax.psum_scatter(second_sum, "space", scatter_dimension=0, tiled=True),
    )
    gain_totals = lax.psum((gain_sum, node_gain), "space")
    return (
        grad_node_feat,
        grad_edge_feat,
        edge_shares[0],
        edge_shares[1],
        node_shares[0],
        node_shares[1],
        jnp.stack([gain_totals[0], gain_totals[1]]),
    )


def solution(mesh):
    placed = (
        P(("group", "space"), None),
        P(("group", "space"), None),
        P(("group", "space"), None),
        P(("group", "space"), None),
        P(),
        P(),
        P(),
        P(),
        P(),
        P(("group", "space")),
        P(("group", "space")),
        P(("group", "space")),
        P(("group", "space"), None, None),
        P(("group", "space")),
    )
    return jax.shard_map(
        shards,
        mesh=mesh,
        in_specs=placed,
        out_specs=(
            P(("group", "space"), None),
            P(("group", "space"), None),
            P(("group", "space"), None),
            P(("group", "space"), None),
            P(("group", "space"), None),
            P(("group", "space"), None),
            P("group", None),
        ),
        check_vma=False,
    )
```

profile of v0, /device:TPU:0, one launch (start us, length us, event | category | flops | bytes accessed | tf_op | source)
XLA Modules:
  0.0 318.0 jit_solution(7453187925502985612)
XLA Ops:
  8.9 2.5 gather_fusion
  11.4 7.4 %all-to-all-start = ((bf16[16,8,512]{2,1,0:T(8,128)(2,1)}), bf16[16,8,512]{2,1,0:T(8,128)(2,1)S(1)}, u32[]{:S(2)}, u32[]{:S(2)}) async-start(bf16[16,8,512]{2,1,0:T(8,128)(2,1)} %bitcast.2), calls=%async_computation | async-start | bytes 262144 | tf_op jit(solution)/shard_map/all_to_all | solution.py:84
  21.8 5.1 %gather_fusion.2 = bf16[1024,512]{1,0:T(8,128)(2,1)} fusion(bf16[256,512]{1,0:T(8,128)(2,1)S(1)} %copy-done.1, s32[1024]{0:T(1024)S(1)} %get-tuple-element.32), kind=kCustom, calls=%fused_computation.2 | custom fusion | bytes 2101248 | tf_op jit(solution)/shard_map/gather | solution.py:104
  26.9 5.1 %gather_fusion.1 = bf16[1024,512]{1,0:T(8,128)(2,1)} fusion(bf16[384,512]{1,0:T(8,128)(2,1)S(1)} %pad_maximum_fusion.1, s32[1024]{0:T(1024)S(1)} %get-tuple-element.29), kind=kCustom, calls=%fused_computation.1 | custom fusion | bytes 2101248 | tf_op jit(solution)/shard_map/gather | solution.py:104
  34.0 3.4 %multiply_convert_fusion.2 = (bf16[1024,512]{1,0:T(8,128)(2,1)S(1)}, f32[1024,512]{1,0:T(8,128)}) fusion(bf16[1024,1536]{1,0:T(8,128)(2,1)S(1)} %constant_dynamic-update-slice_fusion, bf16[1536,512]{1,0:T(8,128)(2,1)S(1)} %copy-done), kind=kOutput, calls=%fused_computation.22 | convolution fusion | flops 1613234176 | bytes 7864320 | tf_op jit(solution)/shard_map/dot_general | solution.py:30
  39.5 1.7 multiply_select_fusion
  41.2 2.9 copy.27
  44.1 7.4 %scatter_custom_fusion = f32[256,512]{1,0:T(8,128)S(1)} fusion(s32[1024]{0:T(1024)S(1)} %get-tuple-element.33, f32[1024,512]{1,0:T(8,128)} %copy.27, f32[]{:T(128)} %constant.12.clone.1), kind=kCustom, calls=%fused_computation.54 | custom fusion | flops 524288 | bytes 524800 | tf_op jit(solution)/shard_map/scatter-add | solution.py:106
  51.5 1.8 fusion.20
  56.9 1.7 fusion.37
  59.6 5.1 %gather_fusion.3 = bf16[1024,512]{1,0:T(8,128)(2,1)} fusion(bf16[256,512]{1,0:T(8,128)(2,1)S(1)} %slice.64, s32[1024]{0:T(1024)S(1)} %get-tuple-element.32), kind=kCustom, calls=%fused_computation.3 | custom fusion | bytes 2101248 | tf_op jit(solution)/shard_map/gather | solution.py:135
  64.7 2.3 copy.29
  67.1 3.0 multiply_reduce_fusion
  72.0 1.8 fusion.40
  73.8 1.8 fusion.19
  76.7 3.3 %multiply_convert_fusion = bf16[1024,512]{1,0:T(8,128)(2,1)S(1)} fusion(f32[1024,512]{1,0:T(8,128)} %get-tuple-element.37, bf16[1024,512]{0,1:T(8,128)(2,1)} %copy-done.14, bf16[512,512]{1,0:T(8,128)(2,1)S(1)} %copy-done.18), kind=kOutput, calls=%fused_computation.17 | convolution fusion | flops 541589504 | bytes 4718592 | tf_op jit(solution)/shard_map/dot_general | solution.py:13
  80.9 3.6 %fusion.39 = f32[1536,512]{1,0:T(8,128)} fusion(bf16[1024,1536]{1,0:T(8,128)(2,1)S(1)} %copy-done.20, bf16[1024,512]{1,0:T(8,128)(2,1)S(1)} %multiply_convert_fusion), kind=kOutput, calls=%fused_computation.89 | convolution fusion | flops 1610612736 | bytes 7340032 | tf_op jit(solution)/shard_map/dot_general | solution.py:19
  84.5 3.1 fusion.38
  87.7 2.7 copy-done.5
  90.3 1.6 slice.53
  91.9 8.3 %scatter_custom_fusion.1 = f32[384,512]{1,0:T(8,128)} fusion(s32[1024]{0:T(1024)S(1)} %get-tuple-element.30, f32[1024,1536]{1,0:T(8,128)} %copy-done.5, f32[]{:T(128)} %constant.12.clone.1), kind=kCustom, calls=%fused_computation.14 | custom fusion | flops 524288 | bytes 2884096 | tf_op jit(solution)/shard_map/scatter-add | solution.py:143
  100.2 2.9 copy.32
  103.1 2.9 fusion.1
  106.0 2.3 copy.31
  108.3 9.5 %scatter_custom_fusion.2 = f32[384,512]{1,0:T(8,128)} fusion(f32[384,512]{1,0:T(8,128)} %scatter_custom_fusion.1, s32[1024]{0:T(1024)S(1)} %get-tuple-element.31, f32[1024,1536]{1,0:T(8,128)} %copy-done.5), kind=kCustom, calls=%fused_computation.12 | custom fusion | flops 524288 | bytes 2883584 | tf_op jit(solution)/shard_map/scatter-add | solution.py:145
  117.8 1.6 fusion.25
  119.4 6.0 %all-to-all-start.1 = ((bf16[16,8,512]{2,1,0:T(8,128)(2,1)}), bf16[16,8,512]{2,1,0:T(8,128)(2,1)S(1)}, u32[]{:S(2)}, u32[]{:S(2)}) async-start(bf16[16,8,512]{2,1,0:T(8,128)(2,1)} %fusion.25), calls=%async_computation.1 | async-start | bytes 262144 | tf_op jit(solution)/shard_map/all_to_all | solution.py:166
  125.4 33.9 %all-reduce = (f32[1,512]{1,0:T(1,128)S(1)}, f32[1,512]{1,0:T(1,128)S(1)}) all-reduce(f32[1,512]{1,0:T(1,128)S(1)} %bitcast.39, f32[1,512]{1,0:T(1,128)S(1)} %bitcast.40), channel_id=1, replica_groups=mesh['group'=2,'space'=16] {'space'}, use_global_device_ids=true, to_apply=%region_19.20 | all-reduce | flops 1024 | bytes 8192 | tf_op jit(solution)/shard_map/psum | solution.py:185
  161.2 1.6 scatter_custom_fusion.3
  163.5 13.1 %reduce-scatter.7.cloned.1.call-done = f32[32,512]{1,0:T(8,128)} async-done(((f32[512,512]{1,0:T(8,128)}), f32[32,512]{1,0:T(8,128)}) %reduce-scatter.7.cloned.1.call-update) | async-done | bytes 65552 | tf_op jit(solution)/shard_map/reduce_scatter | solution.py:183
  176.6 65.0 %reduce-scatter.9.cloned.1.call-done = f32[64,512]{1,0:T(8,128)} async-done(((f32[1024,512]{1,0:T(8,128)}), f32[64,512]{1,0:T(8,128)}) %reduce-scatter.9.cloned.1.call-update) | async-done | bytes 131088 | tf_op jit(solution)/shard_map/reduce_scatter | solution.py:162
  241.5 69.9 %reduce-scatter.5.cloned.1.call-done = f32[96,512]{1,0:T(8,128)} async-done(((f32[1536,512]{1,0:T(8,128)}), f32[96,512]{1,0:T(8,128)}) %reduce-scatter.5.cloned.1.call-update) | async-done | bytes 196624 | tf_op jit(solution)/shard_map/reduce_scatter | solution.py:182
  (93 shorter events, 19.1 us)
Async XLA Ops:
  7.2 26.8 %copy-start = (bf16[1536,512]{1,0:T(8,128)(2,1)S(1)}, bf16[1536,512]{1,0:T(8,128)(2,1)}, u32[]{:S(2)}) copy-start(bf16[1536,512]{1,0:T(8,128)(2,1)} %param.18) | copy-start | bytes 4718596
  7.2 14.6 %copy-start.1 = (bf16[256,512]{1,0:T(8,128)(2,1)S(1)}, bf16[256,512]{1,0:T(8,128)(2,1)}, u32[]{:S(2)}) copy-start(bf16[256,512]{1,0:T(8,128)(2,1)} %param.14) | copy-start | bytes 786436
  11.4 15.5 %all-to-all-start = ((bf16[16,8,512]{2,1,0:T(8,128)(2,1)}), bf16[16,8,512]{2,1,0:T(8,128)(2,1)S(1)}, u32[]{:S(2)}, u32[]{:S(2)}) async-start(bf16[16,8,512]{2,1,0:T(8,128)(2,1)} %bitcast.2), calls=%async_computation | async-start | bytes 262144 | tf_op jit(solution)/shard_map/all_to_all | solution.py:84
  18.8 144.7 %reduce-scatter.11.cloned.1.call-start = ((), (), s32[]{:S(2)}) async-start(), calls=%async_computation.9 | async-start | bytes 1114112 | tf_op jit(solution)/shard_map/reduce_scatter | solution.py:163
  21.8 5.1 %copy-start.21 = (s32[1024]{0:T(1024)S(1)}, s32[1024]{0:T(1024)}, u32[]{:S(2)}) copy-start(s32[1024]{0:T(1024)} %param.24) | copy-start | bytes 12292
  21.8 5.1 %copy-start.22 = (s32[1024]{0:T(1024)S(1)}, s32[1024]{0:T(1024)}, u32[]{:S(2)}) copy-start(s32[1024]{0:T(1024)} %param.23) | copy-start | bytes 12292
  32.0 1.5 copy-start.6
  32.0 1.9 copy-start.11
  33.9 3.4 %copy-start.19 = (bf16[1024,1536]{1,0:T(8,128)(2,1)}, bf16[1024,1536]{1,0:T(8,128)(2,1)S(1)}, u32[]{:S(2)}) copy-start(bf16[1024,1536]{1,0:T(8,128)(2,1)S(1)} %constant_dynamic-update-slice_fusion) | copy-start | bytes 9437188
  34.0 3.4 %copy-start.17 = (bf16[512,512]{1,0:T(8,128)(2,1)S(1)}, bf16[512,512]{1,0:T(8,128)(2,1)}, u32[]{:S(2)}) copy-start(bf16[512,512]{1,0:T(8,128)(2,1)} %param.19) | copy-start | bytes 1572868
  37.3 1.1 copy-start.12
  38.1 1.4 copy-start.2
  51.5 1.9 copy-start.23
  51.5 2.2 copy-start.15
  53.3 1.0 copy-start.9
  56.7 119.9 %reduce-scatter.7.cloned.1.call-start = ((), (), s32[]{:S(2)}) async-start(), calls=%async_computation.7 | async-start | bytes 1114112 | tf_op jit(solution)/shard_map/reduce_scatter | solution.py:183
  58.6 1.0 copy-start.7
  67.1 3.1 copy-start.3
  67.1 3.1 copy-start.4
  70.1 1.8 copy-start.13
  71.0 1.0 copy-start.14
  72.0 1.9 copy-start.16
  73.8 167.8 %reduce-scatter.9.cloned.1.call-start = ((), (), s32[]{:S(2)}) async-start(), calls=%async_computation.8 | async-start | bytes 2228224 | tf_op jit(solution)/shard_map/reduce_scatter | solution.py:162
  75.6 1.0 copy-start.18
  75.6 235.8 %reduce-scatter.5.cloned.1.call-start = ((), (), s32[]{:S(2)}) async-start(), calls=%async_computation.6 | async-start | bytes 3342336 | tf_op jit(solution)/shard_map/reduce_scatter | solution.py:182
  76.7 4.2 %copy-start.20 = (bf16[1024,1536]{1,0:T(8,128)(2,1)S(1)}, bf16[1024,1536]{1,0:T(8,128)(2,1)}, u32[]{:S(2)}) copy-start(bf16[1024,1536]{1,0:T(8,128)(2,1)} %copy-done.19) | copy-start | bytes 9437188
  79.9 1.0 copy-start.24
  87.6 2.7 copy-start.5
  108.3 51.7 %copy-start.8 = (f32[256,1024]{1,0:T(8,128)S(1)}, f32[256,1024]{1,0:T(8,128)}, u32[]{:S(2)}) copy-start(f32[256,1024]{1,0:T(8,128)} %copy-done.7) | copy-start | bytes 3145732
  108.3 51.7 %copy-start.10 = (bf16[256,512]{1,0:T(8,128)(2,1)S(1)}, bf16[256,512]{1,0:T(8,128)(2,1)}, u32[]{:S(2)}) copy-start(bf16[256,512]{1,0:T(8,128)(2,1)} %param.16) | copy-start | bytes 786436
  119.4 41.8 %all-to-all-start.1 = ((bf16[16,8,512]{2,1,0:T(8,128)(2,1)}), bf16[16,8,512]{2,1,0:T(8,128)(2,1)S(1)}, u32[]{:S(2)}, u32[]{:S(2)}) async-start(bf16[16,8,512]{2,1,0:T(8,128)(2,1)} %fusion.25), calls=%async_computation.1 | async-start | bytes 262144 | tf_op jit(solution)/shard_map/all_to_all | solution.py:166
Sparse Core Ops, SparseCore 0:
  56.8 58.7 reduce-scatter.10
  120.2 56.3 reduce-scatter.6
  180.9 60.5 reduce-scatter.8
  246.3 65.1 reduce-scatter.4
where the time goes:
time: 319 us; the launch traced here: 318 us
  waiting for transfers between devices  148 us (46%)
  local copies, waits for them, and re-layouts  44.5 us (14%)
  other arithmetic  39.4 us (12%)
  blocking collectives  33.9 us (11%)
  matrix products  23.6 us (7%)
  between operations  14.8 us (5%)
  starting transfers between devices  13.8 us (4%)
    reduce_scatter x1, waiting for transfers between devices, shards(): lax.psum_scatter(first_sum, 'space', scatter_dimension=0, tiled=True)  69.9 us
    reduce_scatter x1, waiting for transfers between devices, shards(): lax.psum_scatter(grad_node_first, 'space', scatter_dimension=0, tiled=True)  65 us
    psum x1, blocking collectives, shards(): gain_totals = lax.psum((gain_sum, node_gain), 'space')  33.9 us
    scatter-add x2, other arithmetic, backward_step(): totals = totals.at[sender_ids].add(grad_in[:, :feat_width]).at[receiver_i...  17.8 us
    unnamed x56, local copies, waits for them, and re-layouts  17.3 us
    reduce_scatter x1, waiting for transfers between devices, shards(): lax.psum_scatter(second_sum, 'space', scatter_dimension=0, tiled=True)  13.1 us
    dot_general x4, matrix products, transposed_times(): lax.dot_general(left, right, (((0,), (0,)), ((), ())), preferred_element_...  8.68 us
    dot_general x4, matrix products, times_transposed(): lax.dot_general(left, right, (((1,), (1,)), ((), ())), preferred_element_...  8.57 us
  transfers between devices with their start and end apart: 6, of which 3 were waited for; matrix products, arithmetic and copies ran while one was open for 21% of the time, Pallas kernels for 0%

commit v1 on v0

v1 whole, which is shorter than its diff:
```python
import functools

import jax
import jax.numpy as jnp
from jax import lax
from jax.experimental import pallas as pl
from jax.experimental.pallas import tpu as pltpu
from jax.sharding import PartitionSpec as P

EDGE_BLOCK = 128
CHUNK = 256
EPS = 1e-05
BF16 = jnp.bfloat16
F32 = jnp.float32
INT = jnp.int32
MIB = 1 << 20


def dot(left, right):
    return lax.dot_general(left, right, (((1,), (0,)), ((), ())), preferred_element_type=F32)


def times_transposed(left, right):
    return lax.dot_general(left, right, (((1,), (1,)), ((), ())), preferred_element_type=F32)


def transposed_times(left, right):
    return lax.dot_general(left, right, (((0,), (0,)), ((), ())), preferred_element_type=F32)


def ones_where(mask):
    return jnp.where(mask, 1.0, 0.0).astype(BF16)


def columns(row):
    return jnp.transpose(jnp.broadcast_to(row, (EDGE_BLOCK, EDGE_BLOCK)))


def chosen(rows, width):
    lane = lax.broadcasted_iota(INT, (EDGE_BLOCK, EDGE_BLOCK), 1)
    out = []
    for row in rows:
        col = columns(row)
        out.append(
            jnp.concatenate(
                [ones_where(col == lane + EDGE_BLOCK * j) for j in range(width // EDGE_BLOCK)], axis=1
            )
        )
    return jnp.concatenate(out, axis=0)


def chosen_transposed(rows, width):
    sub = lax.broadcasted_iota(INT, (width, EDGE_BLOCK), 0)
    return jnp.concatenate([ones_where(sub == row) for row in rows], axis=1)


def send_choice(table_ref, node_rows):
    devices, capacity = table_ref.shape[1:]
    eye = lax.broadcasted_iota(INT, (capacity, capacity), 0) == lax.broadcasted_iota(
        INT, (capacity, capacity), 1
    )
    lane = lax.broadcasted_iota(INT, (capacity, node_rows), 1).astype(F32)
    out = []
    for j in range(devices):
        row = table_ref[0, j : j + 1, :].astype(F32)
        col = jnp.sum(
            jnp.where(eye, jnp.broadcast_to(row, (capacity, capacity)), 0.0), axis=1, keepdims=True
        )
        out.append(jnp.where(col == lane, 1.0, 0.0))
    return jnp.concatenate(out, axis=0).astype(BF16)


def block_rows(ref, step, count):
    return [ref[pl.ds(step * count + k, 1), :] for k in range(count)]


def live_rows(rows, step, live):
    return [jnp.where(step * len(rows) + k < live, row, -1) for k, row in enumerate(rows)]


def activation(pre):
    sigmoid = 0.5 * jnp.tanh(0.5 * pre) + 0.5
    hidden = pre * sigmoid
    return hidden.astype(BF16), sigmoid + hidden * (1.0 - sigmoid)


def normalize(post):
    centred = post - jnp.mean(post, axis=-1, keepdims=True)
    inv_std = lax.rsqrt(jnp.mean(centred * centred, axis=-1, keepdims=True) + EPS)
    return centred * inv_std, inv_std


def grad_normalize(grad_out, gain, normed, inv_std):
    grad_normed = grad_out * gain
    return (
        inv_std
        * (
            grad_normed
            - jnp.mean(grad_normed, axis=-1, keepdims=True)
            - normed * jnp.mean(grad_normed * normed, axis=-1, keepdims=True)
        )
    ).astype(BF16)


def pack(keep_ref, send_ref, sources, core):
    chips = keep_ref.shape[0]
    for k in range(chips):
        for ref, place in ((keep_ref, 2 * k + core), (send_ref, 2 * k + 1 - core)):
            pieces = []
            for source in sources:
                share = source.shape[0] // (2 * chips)
                pieces.append(source[pl.ds(pl.multiple_of(place * share, 8), share), :])
            ref[k] = jnp.concatenate(pieces, axis=0).astype(BF16)


def outgoing_kernel(node_ref, table_ref, out_ref):
    out_ref[...] = dot(send_choice(table_ref, node_ref.shape[0]), node_ref[...]).astype(BF16)


def prepare_kernel(
    node_ref, edge_ref, first_ref, node_first_ref, peer_ref, slot_ref, recv_ref, part_ref, node_part_ref, table
):
    step = pl.program_id(0)
    own = lax.axis_index("space")
    nodes, width = node_ref.shape

    @pl.when(step == 0)
    def _():
        node = node_ref[...]
        table[0:nodes] = dot(node, first_ref[0:width]).astype(BF16)
        table[nodes:] = dot(node, first_ref[width : 2 * width]).astype(BF16)
        node_part_ref[...] = dot(node, node_first_ref[...])

    count = CHUNK // EDGE_BLOCK
    peers, slots = block_rows(peer_ref, step, count), block_rows(slot_ref, step, count)
    senders = [jnp.where(peer == own, slot, -1) for peer, slot in zip(peers, slots)]
    choice = jnp.concatenate(
        [chosen(senders, nodes), chosen(block_rows(recv_ref, step, count), nodes)], axis=1
    )
    part_ref[...] = dot(edge_ref[...], first_ref[2 * width :]) + dot(choice, table[...])


def forward_kernel(
    part_ref,
    halo_ref,
    first_ref,
    second_ref,
    gains_ref,
    peer_ref,
    slot_ref,
    recv_ref,
    live_ref,
    node_ref,
    node_part_ref,
    node_first_ref,
    node_second_ref,
    grad_nodes_ref,
    slope_ref,
    hidden_ref,
    normed_ref,
    inv_ref,
    grad_agg_ref,
    node_base_ref,
    keep_ref,
    send_ref,
    gain_ref,
    halo_part,
    total,
    grad_first,
    grad_second,
):
    step = pl.program_id(0)
    own = lax.axis_index("space")
    nodes, width = node_ref.shape
    halo_rows = halo_ref.shape[0]
    capacity = halo_rows // (2 * keep_ref.shape[0])

    @pl.when(step == 0)
    def _():
        halo_part[...] = dot(halo_ref[...], first_ref[...]).astype(BF16)
        total[...] = jnp.zeros_like(total)

    count = CHUNK // EDGE_BLOCK
    peers, slots = block_rows(peer_ref, step, count), block_rows(slot_ref, step, count)
    far = [jnp.where(peer == own, -1, peer * capacity + slot) for peer, slot in zip(peers, slots)]
    pre = part_ref[...] + dot(chosen(far, halo_rows), halo_part[...])
    hidden, slope = activation(pre)
    hidden_ref[...] = hidden
    slope_ref[...] = slope.astype(BF16)
    normed, inv_std = normalize(dot(hidden, second_ref[...]))
    normed_ref[...] = normed.astype(BF16)
    inv_ref[...] = jnp.broadcast_to(inv_std, inv_ref.shape)
    messages = (normed * gains_ref[0:1]).astype(BF16)
    receivers = live_rows(block_rows(recv_ref, step, count), step, live_ref[0])
    total[...] += dot(chosen_transposed(receivers, nodes), messages)

    @pl.when(step == pl.num_programs(0) - 1)
    def _():
        aggregate = total[...].astype(BF16)
        node_pre = node_part_ref[...] + dot(aggregate, node_first_ref[width:])
        node_hidden, node_slope = activation(node_pre)
        node_normed, node_inv = normalize(dot(node_hidden, node_second_ref[...]))
        grad_out = grad_nodes_ref[...].astype(F32)
        gain_ref[...] = jnp.sum(grad_out * node_normed, axis=0, keepdims=True)
        grad_post = grad_normalize(grad_out, gains_ref[1:2], node_normed, node_inv)
        grad_pre = (times_transposed(grad_post, node_second_ref[...]) * node_slope).astype(BF16)
        node_base_ref[...] = grad_out + times_transposed(grad_pre, node_first_ref[0:width])
        grad_agg_ref[...] = times_transposed(grad_pre, node_first_ref[width:]).astype(BF16)
        grad_first[0:width] = transposed_times(node_ref[...], grad_pre)
        grad_first[width:] = transposed_times(aggregate, grad_pre)
        grad_second[...] = transposed_times(node_hidden, grad_post)
        pack(keep_ref, send_ref, (grad_first, grad_second), lax.rem(own, 2))


def backward_kernel(
    grad_edges_ref,
    edge_ref,
    slope_ref,
    hidden_ref,
    normed_ref,
    inv_ref,
    grad_agg_ref,
    node_base_ref,
    node_gain_ref,
    node_ref,
    halo_ref,
    first_ref,
    second_ref,
    gains_ref,
    peer_ref,
    slot_ref,
    recv_ref,
    live_ref,
    edge_out_ref,
    node_total_ref,
    back_ref,
    keep_ref,
    send_ref,
    places,
    grad_first,
    grad_second,
    grad_gain,
):
    step = pl.program_id(0)
    own = lax.axis_index("space")
    nodes, width = node_ref.shape
    halo_rows = halo_ref.shape[0]
    devices = 2 * keep_ref.shape[0]
    capacity = halo_rows // devices

    @pl.when(step == 0)
    def _():
        places[...] = jnp.zeros_like(places)
        grad_first[...] = jnp.zeros_like(grad_first)
        grad_second[...] = jnp.zeros_like(grad_second)
        grad_gain[...] = jnp.zeros_like(grad_gain)

    count = CHUNK // EDGE_BLOCK
    peers, slots = block_rows(peer_ref, step, count), block_rows(slot_ref, step, count)
    receivers = live_rows(block_rows(recv_ref, step, count), step, live_ref[0])
    senders = [
        jnp.where(peer == own, slot, nodes + peer * capacity + slot) for peer, slot in zip(peers, slots)
    ]
    incoming = grad_edges_ref[...].astype(F32)
    live = jnp.concatenate(
        [
            jnp.where(jnp.full((EDGE_BLOCK, 1), step * count + k, INT) < live_ref[0], 1.0, 0.0)
            for k in range(count)
        ],
        axis=0,
    )
    grad_out = incoming * live + dot(chosen(receivers, nodes), grad_agg_ref[...])
    normed = normed_ref[...].astype(F32)
    grad_gain[...] += jnp.sum(grad_out * normed, axis=0, keepdims=True)
    grad_post = grad_normalize(grad_out, gains_ref[0:1], normed, inv_ref[:, 0:1])
    grad_pre = (times_transposed(grad_post, second_ref[...]) * slope_ref[...].astype(F32)).astype(BF16)
    edge_out_ref[...] = (incoming + times_transposed(grad_pre, first_ref[2 * width :])).astype(BF16)
    choice = jnp.concatenate(
        [chosen_transposed(senders, nodes + halo_rows), chosen_transposed(receivers, nodes)], axis=0
    )
    places[...] += dot(choice, grad_pre)
    grad_first[2 * width :] += transposed_times(edge_ref[...], grad_pre)
    grad_second[...] += transposed_times(hidden_ref[...], grad_post)

    @pl.when(step == pl.num_programs(0) - 1)
    def _():
        near = places[0:nodes].astype(BF16)
        far = places[nodes : nodes + halo_rows].astype(BF16)
        received = places[nodes + halo_rows :].astype(BF16)
        node = node_ref[...]
        back = times_transposed(far, first_ref[0:width])
        gains = jnp.concatenate([grad_gain[...], node_gain_ref[...]], axis=0)
        coarse = gains.astype(BF16).astype(F32)
        tail = jnp.concatenate(
            [coarse, gains - coarse, jnp.zeros((4, width), F32)], axis=0
        )
        for k in range(devices):
            back_ref[k] = jnp.concatenate(
                [back[k * capacity : (k + 1) * capacity], tail], axis=0
            ).astype(BF16)
        node_total_ref[...] = (
            node_base_ref[...]
            + times_transposed(near, first_ref[0:width])
            + times_transposed(received, first_ref[width : 2 * width])
        )
        grad_first[0:width] = transposed_times(node, near) + transposed_times(halo_ref[...], far)
        grad_first[width : 2 * width] = transposed_times(node, received)
        pack(keep_ref, send_ref, (grad_first, grad_second), lax.rem(own, 2))


def nodes_kernel(total_ref, returned_ref, table_ref, out_ref, gains_ref):
    devices, capacity = table_ref.shape[1:]
    rows = [returned_ref[k].astype(F32) for k in range(devices)]
    returned = jnp.concatenate([row[0:capacity] for row in rows], axis=0).astype(BF16)
    choice = send_choice(table_ref, total_ref.shape[0])
    out_ref[...] = (total_ref[...] + transposed_times(choice, returned)).astype(BF16)
    tail = rows[0][capacity:]
    for row in rows[1:]:
        tail = tail + row[capacity:]
    gains_ref[...] = tail[0:2] + tail[2:4]


def whole(array):
    zeros = (0,) * array.ndim
    return pl.BlockSpec(array.shape, lambda i: zeros)


def chunked(array):
    return pl.BlockSpec((CHUNK, array.shape[1]), lambda i: (i, 0))


SCALAR = pl.BlockSpec(memory_space=pltpu.SMEM)


def shaped(*shape, dtype=F32):
    return jax.ShapeDtypeStruct(shape, dtype)


def call(body, steps, operands, specs, outs, out_specs, scratch=(), flops=0, name=None):
    moved = sum(a.size * a.dtype.itemsize for a in (*operands, *outs))
    return pl.pallas_call(
        body,
        grid=(steps,),
        in_specs=specs,
        out_specs=out_specs,
        out_shape=outs,
        scratch_shapes=scratch,
        name=name,
        cost_estimate=pl.CostEstimate(flops=flops, bytes_accessed=moved, transcendentals=0),
        compiler_params=pltpu.CompilerParams(vmem_limit_bytes=32 * MIB),
    )(*operands)


def shards(
    node_feat,
    edge_feat,
    grad_nodes,
    grad_edges,
    edge_first,
    edge_second,
    node_first,
    node_second,
    gains,
    edge_peer,
    edge_slot,
    edge_recv,
    send_index,
    live_blocks,
):
    nodes, width = node_feat.shape
    edges = edge_feat.shape[0]
    devices, capacity = send_index.shape[1:]
    chips = devices // 2
    halo_rows = devices * capacity
    steps = edges // CHUNK
    peer, slot, recv = (a.reshape(edges // EDGE_BLOCK, EDGE_BLOCK) for a in (edge_peer, edge_slot, edge_recv))
    other_core = [(i, i ^ 1) for i in range(devices)]
    same_core = [[core + 2 * k for k in range(chips)] for core in range(2)]
    block = width * width * 2

    outgoing = call(
        outgoing_kernel,
        1,
        (node_feat, send_index),
        [whole(node_feat), whole(send_index)],
        [shaped(halo_rows, width, dtype=BF16)],
        [pl.BlockSpec((halo_rows, width), lambda i: (0, 0))],
        name="outgoing",
    )[0].reshape(devices, capacity, width)
    halo = lax.all_to_all(outgoing, "space", split_axis=0, concat_axis=0, tiled=True).reshape(halo_rows, width)

    part, node_part = call(
        prepare_kernel,
        steps,
        (node_feat, edge_feat, edge_first, node_first, peer, slot, recv),
        [
            whole(node_feat),
            chunked(edge_feat),
            whole(edge_first),
            pl.BlockSpec((width, width), lambda i: (0, 0)),
            whole(peer),
            whole(slot),
            whole(recv),
        ],
        [shaped(edges, width), shaped(nodes, width)],
        [pl.BlockSpec((CHUNK, width), lambda i: (i, 0)), pl.BlockSpec((nodes, width), lambda i: (0, 0))],
        [pltpu.VMEM((2 * nodes, width), BF16)],
        flops=block * (2 * edges + 3 * nodes),
        name="prepare",
    )

    node_share = node_first.shape[0] // devices + node_second.shape[0] // devices
    node_packed = shaped(chips, node_share, width, dtype=BF16)
    forward_in = (
        part,
        halo,
        edge_first,
        edge_second,
        gains,
        peer,
        slot,
        recv,
        live_blocks,
        node_feat,
        node_part,
        node_first,
        node_second,
        grad_nodes,
    )
    forward_specs = [whole(a) for a in forward_in]
    forward_specs[0] = chunked(part)
    forward_specs[2] = pl.BlockSpec((width, width), lambda i: (0, 0))
    forward_specs[8] = SCALAR
    rows_out = [
        shaped(edges, width, dtype=BF16),
        shaped(edges, width, dtype=BF16),
        shaped(edges, width, dtype=BF16),
        shaped(edges, 128),
    ]
    forward_out = [
        *rows_out,
        shaped(nodes, width, dtype=BF16),
        shaped(nodes, width),
        node_packed,
        node_packed,
        shaped(1, width),
    ]
    slope, hidden, normed, inv_std, grad_agg, node_base, node_keep, node_send, node_gain = call(
        forward_kernel,
        steps,
        forward_in,
        forward_specs,
        forward_out,
        [*(chunked(a) for a in rows_out), *(whole(a) for a in forward_out[4:])],
        [
            pltpu.VMEM((halo_rows, width), BF16),
            pltpu.VMEM((nodes, width), F32),
            pltpu.VMEM(node_first.shape, F32),
            pltpu.VMEM(node_second.shape, F32),
        ],
        flops=block * (2 * edges + 9 * nodes),
        name="forward",
    )

    def spread(keep, received):
        both = (keep.astype(F32) + received.astype(F32)).astype(BF16)
        return lax.all_to_all(
            both, "space", split_axis=0, concat_axis=0, tiled=True, axis_index_groups=same_core
        )

    node_received = lax.ppermute(node_send, "space", other_core)
    node_spread = spread(node_keep, node_received)

    edge_share = edge_first.shape[0] // devices + edge_second.shape[0] // devices
    edge_packed = shaped(chips, edge_share, width, dtype=BF16)
    backward_in = (
        grad_edges,
        edge_feat,
        slope,
        hidden,
        normed,
        inv_std,
        grad_agg,
        node_base,
        node_gain,
        node_feat,
        halo,
        edge_first,
        edge_second,
        gains,
        peer,
        slot,
        recv,
        live_blocks,
    )
    backward_specs = [*(chunked(a) for a in backward_in[:6]), *(whole(a) for a in backward_in[6:-1]), SCALAR]
    backward_out = [
        shaped(edges, width, dtype=BF16),
        shaped(nodes, width),
        shaped(devices, 2 * capacity, width, dtype=BF16),
        edge_packed,
        edge_packed,
    ]
    grad_edge_feat, node_total, back, edge_keep, edge_send = call(
        backward_kernel,
        steps,
        backward_in,
        backward_specs,
        backward_out,
        [chunked(backward_out[0]), *(whole(a) for a in backward_out[1:])],
        [
            pltpu.VMEM((2 * nodes + halo_rows, width), F32),
            pltpu.VMEM(edge_first.shape, F32),
            pltpu.VMEM(edge_second.shape, F32),
            pltpu.VMEM((1, width), F32),
        ],
        flops=block * (6 * edges),
        name="backward",
    )

    edge_received = lax.ppermute(edge_send, "space", other_core)
    returned = lax.all_to_all(back, "space", split_axis=0, concat_axis=0, tiled=True)
    edge_spread = spread(edge_keep, edge_received)

    node_out = [shaped(nodes, width, dtype=BF16), shaped(2, width)]
    grad_node_feat, gain_totals = call(
        nodes_kernel,
        1,
        (node_total, returned, send_index),
        [whole(node_total), whole(returned), whole(send_index)],
        node_out,
        [whole(a) for a in node_out],
        name="nodes",
    )

    edge_sum = jnp.sum(edge_spread.astype(F32), axis=0)
    node_sum = jnp.sum(node_spread.astype(F32), axis=0)
    edge_cut = edge_first.shape[0] // devices
    node_cut = node_first.shape[0] // devices
    return (
        grad_node_feat,
        grad_edge_feat,
        edge_sum[:edge_cut],
        edge_sum[edge_cut:],
        node_sum[:node_cut],
        node_sum[node_cut:],
        gain_totals,
    )


def solution(mesh):
    placed = (
        P(("group", "space"), None),
        P(("group", "space"), None),
        P(("group", "space"), None),
        P(("group", "space"), None),
        P(),
        P(),
        P(),
        P(),
        P(),
        P(("group", "space")),
        P(("group", "space")),
        P(("group", "space")),
        P(("group", "space"), None, None),
        P(("group", "space")),
    )
    return jax.shard_map(
        shards,
        mesh=mesh,
        in_specs=placed,
        out_specs=(
            P(("group", "space"), None),
            P(("group", "space"), None),
            P(("group", "space"), None),
            P(("group", "space"), None),
            P(("group", "space"), None),
            P(("group", "space"), None),
            P("group", None),
        ),
        check_vma=False,
    )
```

time: 319 us -> 116 us (0.36)
  waiting for transfers between devices: 148 us -> 50.3 us
  other arithmetic: 39.4 us -> 3.78 us
  blocking collectives: 33.9 us -> 0 us
  local copies, waits for them, and re-layouts: 44.5 us -> 18.5 us
  matrix products: 23.6 us -> 0 us
  Pallas kernels: 0 us -> 19.8 us
  between operations: 14.8 us -> 1.45 us
  starting transfers between devices: 13.8 us -> 20.8 us
    reduce_scatter x4 -> x0, waiting for transfers between devices: 148 us -> none  [the longest x1 69.9 us: shards(): lax.psum_scatter(first_sum, 'space', scatter_dimension=0, tiled=True)]
    all_to_all x1 -> x3, waiting for transfers between devices: 0.01 us -> 47.4 us  [the longest x2 39.6 us: spread(): lax.all_to_all(both, 'space', split_axis=0, concat_axis=0, tiled=True, ax...]
    psum x1 -> x0, blocking collectives: 33.9 us -> none  [shards(): gain_totals = lax.psum((gain_sum, node_gain), 'space')]
    scatter-add x4 -> x0, other arithmetic: 26.7 us -> none  [the longest x2 17.8 us: backward_step(): totals = totals.at[sender_ids].add(grad_in[:, :feat_width]).at[receiver_i...]
    dot_general x12 -> x0, matrix products: 23.6 us -> none  [the longest x4 8.68 us: transposed_times(): lax.dot_general(left, right, (((0,), (0,)), ((), ())), preferred_element_...]
    gather x5 -> x0, local copies, waits for them, and re-layouts: 20.1 us -> none  [the longest x2 7.41 us: backward_step(): grad_aggregate[receiver_ids].astype(jnp.float32)]
    pallas_call x0 -> x5, Pallas kernels: none -> 19.8 us  [call(): pl.pallas_call(body, grid=(steps,), in_specs=specs, out_specs=out_specs,...]
    all_to_all x1 -> x3, starting transfers between devices: 6.04 us -> 12.9 us  [the longest x2 7.12 us: spread(): lax.all_to_all(both, 'space', split_axis=0, concat_axis=0, tiled=True, ax...]
  transfers between devices with their start and end apart: 6 -> 6, of which waited for: 3 -> 4; matrix products, arithmetic and copies ran while one was open for 21% -> 4% of each run, Pallas kernels for 0% -> 10%
where the time goes in v1:
time: 116 us; the launch traced here: 115 us
  waiting for transfers between devices  50.3 us (43%)
  starting transfers between devices  20.8 us (18%)
  Pallas kernels  19.8 us (17%)
  local copies, waits for them, and re-layouts  18.5 us (16%)
  other arithmetic  3.78 us (3%)
  between operations  1.45 us (1%)
    all_to_all x2, waiting for transfers between devices, spread(): lax.all_to_all(both, 'space', split_axis=0, concat_axis=0, tiled=True, ax...  39.6 us
    pallas_call x5, Pallas kernels, call(): pl.pallas_call(body, grid=(steps,), in_specs=specs, out_specs=out_specs,...  19.8 us
    unnamed x49, local copies, waits for them, and re-layouts  15.9 us
    all_to_all x1, waiting for transfers between devices, shards(): lax.all_to_all(back, 'space', split_axis=0, concat_axis=0, tiled=True)  7.79 us
    all_to_all x1, starting transfers between devices, shards(): lax.all_to_all(outgoing, 'space', split_axis=0, concat_axis=0, tiled=True)  7.39 us
    all_to_all x2, starting transfers between devices, spread(): lax.all_to_all(both, 'space', split_axis=0, concat_axis=0, tiled=True, ax...  7.12 us
    all_to_all x1, starting transfers between devices, shards(): lax.all_to_all(back, 'space', split_axis=0, concat_axis=0, tiled=True)  5.75 us
    convert_element_type x2, other arithmetic, spread(): both = (keep.astype(F32) + received.astype(F32)).astype(BF16)  3.53 us
  transfers between devices with their start and end apart: 6, of which 4 were waited for; matrix products, arithmetic and copies ran while one was open for 4% of the time, Pallas kernels for 10%

profile of v1, /device:TPU:0, one launch (start us, length us, event | category | flops | bytes accessed | tf_op | source)
XLA Modules:
  0.0 114.7 jit_solution(10402258847889918704)
XLA Ops:
  0.6 0.8 copy.21.table_ref
  1.4 0.9 copy-done
  2.3 0.9 outgoing.1
  3.2 7.4 %all-to-all-start = ((bf16[16,8,512]{2,1,0:T(8,128)(2,1)}), bf16[16,8,512]{2,1,0:T(8,128)(2,1)S(1)}, u32[]{:S(2)}, u32[]{:S(2)}) async-start(bf16[16,8,512]{2,1,0:T(8,128)(2,1)} %bitcast.3), calls=%async_computation | async-start | bytes 262144 | tf_op jit(solution)/shard_map/all_to_all | solution.py:390
  11.3 0.9 copy-done.1
  12.2 1.4 %copy-done.3 = bf16[1536,512]{1,0:T(8,128)(2,1)S(1)} copy-done((bf16[1536,512]{1,0:T(8,128)(2,1)S(1)}, bf16[1536,512]{1,0:T(8,128)(2,1)}, u32[]{:S(2)}) %copy-start.3) | copy-done | bytes 1572888
  13.6 1.2 %copy-done.6 = bf16[1024,512]{1,0:T(8,128)(2,1)S(1)} copy-done((bf16[1024,512]{1,0:T(8,128)(2,1)S(1)}, bf16[1024,512]{1,0:T(8,128)(2,1)}, u32[]{:S(2)}) %copy-start.6) | copy-done | bytes 1048600
  14.9 1.2 %copy-done.9 = bf16[1024,512]{1,0:T(8,128)(2,1)S(1)} copy-done((bf16[1024,512]{1,0:T(8,128)(2,1)S(1)}, bf16[1024,512]{1,0:T(8,128)(2,1)}, u32[]{:S(2)}) %copy-start.9) | copy-done | bytes 1048600
  16.1 0.7 copy-done.15
  16.8 0.7 copy-done.17
  17.5 0.7 copy-done.19
  18.2 2.6 %prepare.1 = (f32[1024,512]{1,0:T(8,128)S(1)}, f32[256,512]{1,0:T(8,128)S(1)}) custom-call(bf16[256,512]{1,0:T(8,128)(2,1)S(1)} %copy-done.1, bf16[1024,512]{1,0:T(8,128)(2,1)S(1)} %copy-done.9, bf16[1536,512]{1,0:T(8,128)(2,1)S(1)} %copy-done.3, bf16[1024,512]{1,0:T(8,128)(2,1)S(1)} %copy-done.6, s32[8,128]{1,0:T(8,128)S(1)} %bitcast.7, ...), custom_call_target="tpu_custom_call" | custom-call | flops 1476395008 | bytes 6565888 | tf_op jit(solution)/shard_map/prepare/pallas_call | solution.py:341
  20.8 1.4 %copy-done.22 = f32[1024,512]{1,0:T(8,128)} copy-done((f32[1024,512]{1,0:T(8,128)}, f32[1024,512]{1,0:T(8,128)S(1)}, u32[]{:S(2)}) %copy-start.22) | copy-done | bytes 2097176
  22.2 1.4 %copy-done.4 = bf16[1536,512]{1,0:T(8,128)(2,1)S(1)} copy-done((bf16[1536,512]{1,0:T(8,128)(2,1)S(1)}, bf16[1536,512]{1,0:T(8,128)(2,1)}, u32[]{:S(2)}) %copy-start.4) | copy-done | bytes 1572888
  23.6 1.0 copy-done.13
  24.6 0.9 copy-done.14
  25.6 1.6 %copy-done.23 = f32[1024,512]{1,0:T(8,128)S(1)} copy-done((f32[1024,512]{1,0:T(8,128)S(1)}, f32[1024,512]{1,0:T(8,128)}, u32[]{:S(2)}) %copy-start.23) | copy-done | bytes 2097176
  27.2 7.2 %forward.1 = (bf16[1024,512]{1,0:T(8,128)(2,1)S(1)}, bf16[1024,512]{1,0:T(8,128)(2,1)S(1)}, bf16[1024,512]{1,0:T(8,128)(2,1)S(1)}, f32[1024,128]{1,0:T(8,128)S(1...) custom-call(f32[1024,512]{1,0:T(8,128)S(1)} %copy-done.23, ...), custom_call_target="tpu_custom_call" | custom-call | flops 2281701376 | bytes 12994564 | tf_op jit(solution)/shard_map/forward/pallas_call | solution.py:341
  34.9 8.2 %backward.1 = (bf16[1024,512]{1,0:T(8,128)(2,1)}, f32[256,512]{1,0:T(8,128)S(1)}, bf16[16,16,512]{2,1,0:T(8,128)(2,1)}, bf16[8,128,512]{2,1,0:T(8,128)(2,1)S(1)}, bf16[8,128,512]{2,1,0:T(8,128)(2,1)S(1)}) custom-call(bf16[1024,512]{1,0:T(8,128)(2,1)S(1)} %copy-done.8, bf16[1024,512]{1,0:T(8,128)(2,1)S(1)} %copy-done.10, ...), custom_call_target="tpu_custom_call" | custom-call | flops 3221225472 | bytes 12994564 | tf_op jit(solution)/shard_map/backward/pallas_call | solution.py:341
  43.0 1.0 copy-done.11
  44.0 5.7 %all-to-all-start.1 = ((bf16[16,16,512]{2,1,0:T(8,128)(2,1)}), bf16[16,16,512]{2,1,0:T(8,128)(2,1)S(1)}, u32[]{:S(2)}, u32[]{:S(2)}) async-start(bf16[16,16,512]{2,1,0:T(8,128)(2,1)} %get-tuple-element.35), calls=%async_computation.1 | async-start | bytes 524288 | tf_op jit(solution)/shard_map/all_to_all | solution.py:522
  49.8 2.2 %add_convert_fusion.1 = bf16[8,96,512]{2,1,0:T(8,128)(2,1)} fusion(bf16[8,96,512]{2,1,0:T(8,128)(2,1)} %collective-permute-done.1, bf16[8,96,512]{2,1,0:T(8,128)(2,1)S(1)} %get-tuple-element.40), kind=kLoop, calls=%fused_computation.3 | loop fusion | flops 1572864 | bytes 2359296 | tf_op jit(solution)/shard_map/convert_element_type | solution.py:466
  52.0 7.8 %all-to-all-done.1.returned_ref = bf16[16,16,512]{2,1,0:T(8,128)(2,1)S(1)} async-done(((bf16[16,16,512]{2,1,0:T(8,128)(2,1)}), bf16[16,16,512]{2,1,0:T(8,128)(2,1)S(1)}, u32[]{:S(2)}, u32[]{:S(2)}) %all-to-all-start.1) | async-done | bytes 262176 | tf_op jit(solution)/shard_map/all_to_all | solution.py:522
  59.8 3.5 %all-to-all-start.3 = ((bf16[8,96,512]{2,1,0:T(8,128)(2,1)}), bf16[8,96,512]{2,1,0:T(8,128)(2,1)S(1)}, u32[]{:S(2)}, u32[]{:S(2)}) async-start(bf16[8,96,512]{2,1,0:T(8,128)(2,1)} %add_convert_fusion.1), calls=%async_computation.3 | async-start | bytes 1572864 | tf_op jit(solution)/shard_map/all_to_all | solution.py:467
  63.4 2.9 %collective-permute-done = bf16[8,128,512]{2,1,0:T(8,128)(2,1)S(1)} collective-permute-done((bf16[8,128,512]{2,1,0:T(8,128)(2,1)}, bf16[8,128,512]{2,1,0:T(8,128)(2,1)S(1)}, u32[]{:S(2)}, u32[]{:S(2)}) %collective-permute-start) | collective-permute-done | bytes 1048608 | tf_op jit(solution)/shard_map/ppermute | solution.py:521
  66.3 1.3 %add_convert_fusion = bf16[8,128,512]{2,1,0:T(8,128)(2,1)} fusion(bf16[8,128,512]{2,1,0:T(8,128)(2,1)S(1)} %collective-permute-done, bf16[8,128,512]{2,1,0:T(8,128)(2,1)S(1)} %get-tuple-element.38), kind=kLoop, calls=%fused_computation.1 | loop fusion | flops 2097152 | bytes 3145728 | tf_op jit(solution)/shard_map/convert_element_type | solution.py:466
  67.6 16.1 %all-to-all-done.3 = bf16[8,96,512]{2,1,0:T(8,128)(2,1)S(1)} async-done(((bf16[8,96,512]{2,1,0:T(8,128)(2,1)}), bf16[8,96,512]{2,1,0:T(8,128)(2,1)S(1)}, u32[]{:S(2)}, u32[]{:S(2)}) %all-to-all-start.3) | async-done | bytes 786464 | tf_op jit(solution)/shard_map/all_to_all | solution.py:467
  83.7 3.6 %all-to-all-start.2 = ((bf16[8,128,512]{2,1,0:T(8,128)(2,1)}), bf16[8,128,512]{2,1,0:T(8,128)(2,1)S(1)}, u32[]{:S(2)}, u32[]{:S(2)}) async-start(bf16[8,128,512]{2,1,0:T(8,128)(2,1)} %add_convert_fusion), calls=%async_computation.2 | async-start | bytes 2097152 | tf_op jit(solution)/shard_map/all_to_all | solution.py:467
  87.3 1.0 nodes.1
  89.1 0.7 slice.18
  89.8 23.5 %all-to-all-done.2 = bf16[8,128,512]{2,1,0:T(8,128)(2,1)S(1)} async-done(((bf16[8,128,512]{2,1,0:T(8,128)(2,1)}), bf16[8,128,512]{2,1,0:T(8,128)(2,1)S(1)}, u32[]{:S(2)}, u32[]{:S(2)}) %all-to-all-start.2) | async-done | bytes 1048608 | tf_op jit(solution)/shard_map/all_to_all | solution.py:467
  114.0 0.7 slice.16
  (42 shorter events, 2.2 us)
Async XLA Ops:
  1.4 0.9 copy-start
  3.2 18.9 %all-to-all-start = ((bf16[16,8,512]{2,1,0:T(8,128)(2,1)}), bf16[16,8,512]{2,1,0:T(8,128)(2,1)S(1)}, u32[]{:S(2)}, u32[]{:S(2)}) async-start(bf16[16,8,512]{2,1,0:T(8,128)(2,1)} %bitcast.3), calls=%async_computation | async-start | bytes 262144 | tf_op jit(solution)/shard_map/all_to_all | solution.py:390
  11.3 1.0 copy-start.1
  12.2 1.4 %copy-start.3 = (bf16[1536,512]{1,0:T(8,128)(2,1)S(1)}, bf16[1536,512]{1,0:T(8,128)(2,1)}, u32[]{:S(2)}) copy-start(bf16[1536,512]{1,0:T(8,128)(2,1)} %first_ref.5) | copy-start | bytes 4718596
  13.6 1.2 %copy-start.6 = (bf16[1024,512]{1,0:T(8,128)(2,1)S(1)}, bf16[1024,512]{1,0:T(8,128)(2,1)}, u32[]{:S(2)}) copy-start(bf16[1024,512]{1,0:T(8,128)(2,1)} %node_first_ref.3) | copy-start | bytes 3145732
  14.9 1.2 %copy-start.9 = (bf16[1024,512]{1,0:T(8,128)(2,1)S(1)}, bf16[1024,512]{1,0:T(8,128)(2,1)}, u32[]{:S(2)}) copy-start(bf16[1024,512]{1,0:T(8,128)(2,1)} %edge_ref.3) | copy-start | bytes 3145732
  16.1 0.7 copy-start.15
  16.8 0.7 copy-start.17
  17.5 0.7 copy-start.19
  18.2 4.0 %copy-start.2 = (bf16[256,512]{1,0:T(8,128)(2,1)S(1)}, bf16[256,512]{1,0:T(8,128)(2,1)}, u32[]{:S(2)}) copy-start(bf16[256,512]{1,0:T(8,128)(2,1)} %node_ref.7) | copy-start | bytes 786436
  18.2 4.0 %copy-start.7 = (bf16[1024,512]{1,0:T(8,128)(2,1)S(1)}, bf16[1024,512]{1,0:T(8,128)(2,1)}, u32[]{:S(2)}) copy-start(bf16[1024,512]{1,0:T(8,128)(2,1)} %node_first_ref.3) | copy-start | bytes 3145732
  18.2 4.0 %copy-start.12 = (bf16[512,512]{1,0:T(8,128)(2,1)S(1)}, bf16[512,512]{1,0:T(8,128)(2,1)}, u32[]{:S(2)}) copy-start(bf16[512,512]{1,0:T(8,128)(2,1)} %node_second_ref.1) | copy-start | bytes 1572868
  18.2 4.0 %copy-start.16 = (s32[1024]{0:T(1024)S(1)}, s32[1024]{0:T(1024)}, u32[]{:S(2)}) copy-start(s32[1024]{0:T(1024)} %param.23) | copy-start | bytes 12292
  18.2 4.0 %copy-start.18 = (s32[1024]{0:T(1024)S(1)}, s32[1024]{0:T(1024)}, u32[]{:S(2)}) copy-start(s32[1024]{0:T(1024)} %param.24) | copy-start | bytes 12292
  18.2 4.0 %copy-start.20 = (s32[1024]{0:T(1024)S(1)}, s32[1024]{0:T(1024)}, u32[]{:S(2)}) copy-start(s32[1024]{0:T(1024)} %param.25) | copy-start | bytes 12292
  18.2 4.0 %copy-start.21 = (f32[2,512]{1,0:T(2,128)S(1)}, f32[2,512]{1,0:T(2,128)}, u32[]{:S(2)}) copy-start(f32[2,512]{1,0:T(2,128)} %gains_ref.3) | copy-start | bytes 12292
  20.8 1.4 %copy-start.22 = (f32[1024,512]{1,0:T(8,128)}, f32[1024,512]{1,0:T(8,128)S(1)}, u32[]{:S(2)}) copy-start(f32[1024,512]{1,0:T(8,128)S(1)} %get-tuple-element.25.part_ref) | copy-start | bytes 6291460
  22.2 1.4 %copy-start.4 = (bf16[1536,512]{1,0:T(8,128)(2,1)S(1)}, bf16[1536,512]{1,0:T(8,128)(2,1)}, u32[]{:S(2)}) copy-start(bf16[1536,512]{1,0:T(8,128)(2,1)} %first_ref.5) | copy-start | bytes 4718596
  23.6 1.0 copy-start.13
  24.6 0.9 copy-start.14
  25.6 1.6 %copy-start.23 = (f32[1024,512]{1,0:T(8,128)S(1)}, f32[1024,512]{1,0:T(8,128)}, u32[]{:S(2)}) copy-start(f32[1024,512]{1,0:T(8,128)} %copy-done.22) | copy-start | bytes 6291460
  27.2 7.7 %copy-start.5 = (bf16[1536,512]{1,0:T(8,128)(2,1)S(1)}, bf16[1536,512]{1,0:T(8,128)(2,1)}, u32[]{:S(2)}) copy-start(bf16[1536,512]{1,0:T(8,128)(2,1)} %first_ref.5) | copy-start | bytes 4718596
  27.2 7.7 %copy-start.8 = (bf16[1024,512]{1,0:T(8,128)(2,1)S(1)}, bf16[1024,512]{1,0:T(8,128)(2,1)}, u32[]{:S(2)}) copy-start(bf16[1024,512]{1,0:T(8,128)(2,1)} %grad_edges_ref.1) | copy-start | bytes 3145732
  27.2 7.7 %copy-start.10 = (bf16[1024,512]{1,0:T(8,128)(2,1)S(1)}, bf16[1024,512]{1,0:T(8,128)(2,1)}, u32[]{:S(2)}) copy-start(bf16[1024,512]{1,0:T(8,128)(2,1)} %edge_ref.3) | copy-start | bytes 3145732
  34.3 15.4 %collective-permute-start.1 = (bf16[8,96,512]{2,1,0:T(8,128)(2,1)}, bf16[8,96,512]{2,1,0:T(8,128)(2,1)}, u32[]{:S(2)}, u32[]{:S(2)}) collective-permute-start(bf16[8,96,512]{2,1,0:T(8,128)(2,1)} %get-tuple-element.41), channel_id=1, source_target_pairs={{0,1},{1,0},{2,3},{3,2},{4,5},{5,4},{6,7},{7,6},{8,9},{9,8},{10,11... | collective-permute-start | bytes 2359304 | tf_op jit(solution)/shard_map/ppermute | solution.py:471
  43.0 1.0 copy-start.11
  44.0 15.8 %all-to-all-start.1 = ((bf16[16,16,512]{2,1,0:T(8,128)(2,1)}), bf16[16,16,512]{2,1,0:T(8,128)(2,1)S(1)}, u32[]{:S(2)}, u32[]{:S(2)}) async-start(bf16[16,16,512]{2,1,0:T(8,128)(2,1)} %get-tuple-element.35), calls=%async_computation.1 | async-start | bytes 524288 | tf_op jit(solution)/shard_map/all_to_all | solution.py:522
  59.8 23.9 %all-to-all-start.3 = ((bf16[8,96,512]{2,1,0:T(8,128)(2,1)}), bf16[8,96,512]{2,1,0:T(8,128)(2,1)S(1)}, u32[]{:S(2)}, u32[]{:S(2)}) async-start(bf16[8,96,512]{2,1,0:T(8,128)(2,1)} %add_convert_fusion.1), calls=%async_computation.3 | async-start | bytes 1572864 | tf_op jit(solution)/shard_map/all_to_all | solution.py:467
  63.4 2.9 %collective-permute-start = (bf16[8,128,512]{2,1,0:T(8,128)(2,1)}, bf16[8,128,512]{2,1,0:T(8,128)(2,1)S(1)}, u32[]{:S(2)}, u32[]{:S(2)}) collective-permute-start(bf16[8,128,512]{2,1,0:T(8,128)(2,1)} %copy-done.11), channel_id=1, source_target_pairs={{0,1},{1,0},{2,3},{3,2},{4,5},{5,4},{6,7},{7,6},{8,9},{9,8},{10,11... | collective-permute-start | bytes 3145736 | tf_op jit(solution)/shard_map/ppermute | solution.py:521
  83.7 29.5 %all-to-all-start.2 = ((bf16[8,128,512]{2,1,0:T(8,128)(2,1)}), bf16[8,128,512]{2,1,0:T(8,128)(2,1)S(1)}, u32[]{:S(2)}, u32[]{:S(2)}) async-start(bf16[8,128,512]{2,1,0:T(8,128)(2,1)} %add_convert_fusion), calls=%async_computation.2 | async-start | bytes 2097152 | tf_op jit(solution)/shard_map/all_to_all | solution.py:467

commit v2 on v0

v2 whole, which is shorter than its diff:
```python
import functools

import jax
import jax.numpy as jnp
from jax import lax
from jax.experimental import pallas as pl
from jax.experimental.pallas import tpu as pltpu
from jax.sharding import PartitionSpec as P

EDGE_BLOCK = 128
CHUNK = 256
EPS = 1e-05
BF16 = jnp.bfloat16
F32 = jnp.float32
INT = jnp.int32
MIB = 1 << 20


def dot(left, right):
    return lax.dot_general(left, right, (((1,), (0,)), ((), ())), preferred_element_type=F32)


def times_transposed(left, right):
    return lax.dot_general(left, right, (((1,), (1,)), ((), ())), preferred_element_type=F32)


def transposed_times(left, right):
    return lax.dot_general(left, right, (((0,), (0,)), ((), ())), preferred_element_type=F32)


def ones_where(mask):
    return jnp.where(mask, 1.0, 0.0).astype(BF16)


def chosen(row, width):
    lane = lax.broadcasted_iota(INT, (EDGE_BLOCK, EDGE_BLOCK), 1)
    col = jnp.transpose(jnp.broadcast_to(row, (EDGE_BLOCK, EDGE_BLOCK)))
    return jnp.concatenate(
        [ones_where(col == lane + EDGE_BLOCK * j) for j in range(width // EDGE_BLOCK)], axis=1
    )


def chosen_transposed(row, width):
    return ones_where(lax.broadcasted_iota(INT, (width, EDGE_BLOCK), 0) == row)


def send_choice(table_ref, node_rows):
    capacity, devices = table_ref.shape[1:]
    lane = lax.broadcasted_iota(INT, (capacity, node_rows), 1)
    table = table_ref[0]
    out = [jnp.where(table[:, j : j + 1] == lane, 1.0, 0.0) for j in range(devices)]
    return jnp.concatenate(out, axis=0).astype(BF16)


def activation(pre):
    sigmoid = 0.5 * jnp.tanh(0.5 * pre) + 0.5
    hidden = pre * sigmoid
    return hidden.astype(BF16), sigmoid + hidden * (1.0 - sigmoid)


def normalize(post):
    centred = post - jnp.mean(post, axis=-1, keepdims=True)
    inv_std = lax.rsqrt(jnp.mean(centred * centred, axis=-1, keepdims=True) + EPS)
    return centred * inv_std, inv_std


def grad_normalize(grad_out, gain, normed, inv_std):
    grad_normed = grad_out * gain
    return (
        inv_std
        * (
            grad_normed
            - jnp.mean(grad_normed, axis=-1, keepdims=True)
            - normed * jnp.mean(grad_normed * normed, axis=-1, keepdims=True)
        )
    ).astype(BF16)


def pack(keep_ref, send_ref, stage, sems, sources, core):
    chips = stage.shape[0]
    copies = []
    for away in (True, False):
        for k in range(chips):
            place = 2 * k + 1 - core if away else 2 * k + core
            pieces = []
            for source in sources:
                share = source.shape[0] // (2 * chips)
                pieces.append(source[pl.ds(pl.multiple_of(place * share, 8), share), :])
            rows = jnp.concatenate(pieces, axis=0).astype(BF16)
            if away:
                stage[k] = rows
                copies.append(pltpu.make_async_copy(stage.at[k], send_ref.at[k], sems.at[k]))
                copies[-1].start()
            else:
                keep_ref[k] = rows
    return copies


def outgoing_kernel(node_hbm, table_hbm, out_ref, node, table, stage, sems):
    copies = [
        pltpu.make_async_copy(node_hbm, node, sems.at[0]),
        pltpu.make_async_copy(table_hbm, table, sems.at[1]),
    ]
    for copy in copies:
        copy.start()
    copies[1].wait()
    choice = send_choice(table, node.shape[0])
    copies[0].wait()
    stage[...] = dot(choice, node[...]).astype(BF16)
    copy = pltpu.make_async_copy(stage, out_ref, sems.at[0])
    copy.start()
    copy.wait()


def load(sources, targets, sems):
    copies = [
        pltpu.make_async_copy(source, target, sems.at[k])
        for k, (source, target) in enumerate(zip(sources, targets))
    ]
    for copy in copies:
        copy.start()
    return copies


def prepare_kernel(
    live_ref,
    peer_hbm,
    slot_hbm,
    recv_hbm,
    node_hbm,
    first_hbm,
    edge_hbm,
    node_first_hbm,
    second_hbm,
    part_ref,
    far_ref,
    top_ref,
    second_ref,
    node_part_ref,
    receive_ref,
    place_ref,
    peer_ref,
    slot_ref,
    recv_ref,
    node,
    first,
    edge,
    node_first,
    node_part,
    receive,
    places,
    table,
    sems,
    out_sems,
):
    nodes, width = node.shape
    copies = load(
        (
            peer_hbm,
            slot_hbm,
            recv_hbm,
            node_hbm,
            first_hbm,
            edge_hbm,
            node_first_hbm.at[pl.ds(0, width)],
            second_hbm,
            first_hbm.at[pl.ds(0, width)],
        ),
        (peer_ref, slot_ref, recv_ref, node, first, edge, node_first, second_ref, top_ref),
        sems,
    )
    own = lax.axis_index("space")
    blocks = peer_ref.shape[0]
    halo_rows = far_ref.shape[1]
    capacity = halo_rows // lax.axis_size("space")
    for k in range(3):
        copies[k].wait()
    near = []
    for b in range(blocks):
        rows = pl.ds(b * EDGE_BLOCK, EDGE_BLOCK)
        peer, slot, recv = (ref[b : b + 1, :] for ref in (peer_ref, slot_ref, recv_ref))
        mine = peer == own
        far = peer * capacity + slot
        near.append(chosen(jnp.where(mine, slot, -1), nodes))
        far_ref[rows, :] = chosen(jnp.where(mine, -1, far), halo_rows)
        received = jnp.where(b < live_ref[0], recv, -1)
        receive[rows, :] = chosen(received, nodes)
        places[0 : nodes + halo_rows, rows] = chosen_transposed(
            jnp.where(mine, slot, nodes + far), nodes + halo_rows
        )
        places[nodes + halo_rows :, rows] = chosen_transposed(received, nodes)
    out_copies = load((receive, places), (receive_ref, place_ref), out_sems)
    copies[3].wait()
    copies[4].wait()
    table[0:nodes] = dot(node[...], first[0:width]).astype(BF16)
    table[nodes:] = dot(node[...], first[width : 2 * width]).astype(BF16)
    copies[5].wait()
    count = CHUNK // EDGE_BLOCK
    for c in range(blocks // count):
        rows = pl.ds(c * CHUNK, CHUNK)
        choice = jnp.concatenate(
            [jnp.concatenate(near[c * count : (c + 1) * count], axis=0), receive[rows, :]], axis=1
        )
        part_ref[rows, :] = dot(edge[rows, :], first[2 * width :]) + dot(choice, table[...])
    copies[6].wait()
    node_part[...] = dot(node[...], node_first[...])
    out_copies.append(pltpu.make_async_copy(node_part, node_part_ref, out_sems.at[2]))
    out_copies[2].start()
    for copy in (*copies[7:], *out_copies):
        copy.wait()


def forward_kernel(
    part_ref,
    halo_ref,
    far_ref,
    top_ref,
    second_ref,
    gains_hbm,
    place_hbm,
    node_part_hbm,
    node_first_hbm,
    node_second_hbm,
    grad_nodes_hbm,
    node_hbm,
    slope_ref,
    hidden_ref,
    normed_ref,
    inv_ref,
    grad_agg_ref,
    node_gain_ref,
    keep_ref,
    node_base_ref,
    send_ref,
    gains,
    place,
    node_part,
    node_first,
    node_second,
    grad_nodes,
    node,
    messages,
    grad_first,
    grad_second,
    node_base,
    stage,
    sems,
    out_sems,
    base_sem,
):
    nodes, width = node.shape
    copies = load(
        (
            gains_hbm,
            place_hbm.at[pl.ds(place_hbm.shape[0] - nodes, nodes)],
            node_part_hbm,
            node_first_hbm,
            node_second_hbm,
            grad_nodes_hbm,
            node_hbm,
        ),
        (gains, place, node_part, node_first, node_second, grad_nodes, node),
        sems,
    )
    halo_part = dot(halo_ref[...], top_ref[...]).astype(BF16)
    copies[0].wait()
    for c in range(part_ref.shape[0] // CHUNK):
        rows = pl.ds(c * CHUNK, CHUNK)
        hidden, slope = activation(part_ref[rows, :] + dot(far_ref[rows, :], halo_part))
        hidden_ref[rows, :] = hidden
        slope_ref[rows, :] = slope.astype(BF16)
        normed, inv_std = normalize(dot(hidden, second_ref[...]))
        normed_ref[rows, :] = normed.astype(BF16)
        inv_ref[rows, :] = jnp.broadcast_to(inv_std, (CHUNK, inv_ref.shape[1]))
        messages[rows, :] = (normed * gains[0:1]).astype(BF16)
    for copy in copies[1:]:
        copy.wait()
    aggregate = dot(place[...], messages[...]).astype(BF16)
    node_hidden, node_slope = activation(node_part[...] + dot(aggregate, node_first[width:]))
    node_normed, node_inv = normalize(dot(node_hidden, node_second[...]))
    grad_out = grad_nodes[...].astype(F32)
    node_gain_ref[...] = jnp.sum(grad_out * node_normed, axis=0, keepdims=True)
    grad_post = grad_normalize(grad_out, gains[1:2], node_normed, node_inv)
    grad_second[...] = transposed_times(node_hidden, grad_post)
    grad_pre = (times_transposed(grad_post, node_second[...]) * node_slope).astype(BF16)
    grad_first[0:width] = transposed_times(node[...], grad_pre)
    grad_first[width:] = transposed_times(aggregate, grad_pre)
    core = lax.rem(lax.axis_index("space"), 2)
    copies = pack(keep_ref, send_ref, stage, out_sems, (grad_first, grad_second), core)
    node_base[...] = grad_out + times_transposed(grad_pre, node_first[0:width])
    copies.append(pltpu.make_async_copy(node_base, node_base_ref, base_sem.at[0]))
    copies[-1].start()
    grad_agg_ref[...] = times_transposed(grad_pre, node_first[width:]).astype(BF16)
    for copy in copies:
        copy.wait()


def backward_kernel(
    live_ref,
    grad_edges_ref,
    slope_ref,
    hidden_ref,
    normed_ref,
    inv_ref,
    grad_agg_ref,
    node_gain_ref,
    halo_ref,
    second_ref,
    receive_ref,
    first_ref,
    gains_ref,
    place_hbm,
    edge_hbm,
    node_hbm,
    node_base_hbm,
    keep_ref,
    node_total_ref,
    edge_out_ref,
    back_ref,
    send_ref,
    place_ref,
    edge_ref,
    node_ref,
    node_base,
    grad_post_all,
    grad_pre_all,
    edge_out,
    back_stage,
    grad_first,
    grad_second,
    stage,
    sems,
    edge_sems,
    back_sems,
    load_sems,
):
    nodes, width = node_ref.shape
    loads = load(
        (place_hbm, edge_hbm, node_hbm, node_base_hbm), (place_ref, edge_ref, node_ref, node_base), load_sems
    )
    halo_rows = halo_ref.shape[0]
    devices = back_ref.shape[0]
    capacity = halo_rows // devices
    count = CHUNK // EDGE_BLOCK
    edge_copies = []
    grad_gain = jnp.zeros((1, width), F32)
    for c in range(edge_ref.shape[0] // CHUNK):
        rows = pl.ds(c * CHUNK, CHUNK)
        incoming = grad_edges_ref[rows, :].astype(F32)
        live = jnp.concatenate(
            [
                jnp.where(jnp.full((EDGE_BLOCK, 1), c * count + k, INT) < live_ref[0], 1.0, 0.0)
                for k in range(count)
            ],
            axis=0,
        )
        grad_out = incoming * live + dot(receive_ref[rows, :], grad_agg_ref[...])
        normed = normed_ref[rows, :].astype(F32)
        grad_gain += jnp.sum(grad_out * normed, axis=0, keepdims=True)
        grad_post = grad_normalize(grad_out, gains_ref[0:1], normed, inv_ref[rows, 0:1])
        grad_post_all[rows, :] = grad_post
        grad_pre = (times_transposed(grad_post, second_ref[...]) * slope_ref[rows, :].astype(F32)).astype(BF16)
        grad_pre_all[rows, :] = grad_pre
        edge_out[rows, :] = (incoming + times_transposed(grad_pre, first_ref[2 * width :])).astype(BF16)
        copy = pltpu.make_async_copy(edge_out.at[rows], edge_out_ref.at[rows], edge_sems.at[c])
        copy.start()
        edge_copies.append(copy)
    for copy in loads:
        copy.wait()
    places = dot(place_ref[...], grad_pre_all[...])
    near = places[0:nodes].astype(BF16)
    far = places[nodes : nodes + halo_rows].astype(BF16)
    received = places[nodes + halo_rows :].astype(BF16)
    back = times_transposed(far, first_ref[0:width])
    gains = jnp.concatenate([grad_gain, node_gain_ref[...]], axis=0)
    coarse = gains.astype(BF16).astype(F32)
    tail = jnp.concatenate(
        [coarse, gains - coarse, jnp.zeros((back_ref.shape[1] - capacity - 4, width), F32)], axis=0
    )
    for k in range(devices):
        back_stage[k] = jnp.concatenate([back[k * capacity : (k + 1) * capacity], tail], axis=0).astype(BF16)
    back_copy = pltpu.make_async_copy(back_stage, back_ref, back_sems.at[0])
    back_copy.start()
    grad_second[...] = transposed_times(hidden_ref[...], grad_post_all[...])
    grad_first[2 * width :] = transposed_times(edge_ref[...], grad_pre_all[...])
    grad_first[0:width] = transposed_times(node_ref[...], near) + transposed_times(halo_ref[...], far)
    grad_first[width : 2 * width] = transposed_times(node_ref[...], received)
    core = lax.rem(lax.axis_index("space"), 2)
    copies = pack(keep_ref, send_ref, stage, sems, (grad_first, grad_second), core)
    node_base[...] += times_transposed(near, first_ref[0:width]) + times_transposed(
        received, first_ref[width : 2 * width]
    )
    total_copy = pltpu.make_async_copy(node_base, node_total_ref, back_sems.at[1])
    total_copy.start()
    for copy in (*edge_copies, back_copy, total_copy, *copies):
        copy.wait()


def nodes_kernel(total_hbm, returned_ref, table_hbm, out_ref, gains_ref, total, table, stage, gain_stage, sems):
    loads = load((total_hbm, table_hbm), (total, table), sems)
    capacity, devices = table.shape[1:]
    rows = [returned_ref[k].astype(F32) for k in range(devices)]
    returned = jnp.concatenate([row[0:capacity] for row in rows], axis=0).astype(BF16)
    tail = rows[0][capacity:]
    for row in rows[1:]:
        tail = tail + row[capacity:]
    gain_stage[...] = tail[0:2] + tail[2:4]
    for copy in loads:
        copy.wait()
    choice = send_choice(table, total.shape[0])
    stage[...] = (total[...] + transposed_times(choice, returned)).astype(BF16)
    for copy in load((stage, gain_stage), (out_ref, gains_ref), sems):
        copy.wait()


def exchange_orders(chips):
    bits = list(range(chips.bit_length() - 1))
    return bits, [*bits[1::-1], *bits[2:]]


def exchange(sent, bits, devices):
    return [
        lax.ppermute(piece, "space", [(i, i ^ (2 << bit)) for i in range(devices)])
        for piece, bit in zip(sent, bits)
    ]


def half_of(step, bit, position, away):
    value = (lax.axis_index("space") >> (bit + 1)) & 1
    value = 1 - value if away else value
    low = step & ((1 << position) - 1)
    return ((step >> position) << (position + 1)) | (value << position) | low


def fold(sums, sent, kept, stages, sems, bits, positions):
    copies = []
    for away in (True, False):
        for half, (bit, position) in enumerate(zip(bits, positions)):
            for k in range(kept[half].shape[0]):
                block = sums(half, half_of(k, bit, position, away)).astype(BF16)
                if away:
                    stages[half][k] = block
                    copies.append(
                        pltpu.make_async_copy(stages[half].at[k], sent[half].at[k], sems[half].at[k])
                    )
                    copies[-1].start()
                else:
                    kept[half][k] = block
    for copy in copies:
        copy.wait()


def first_fold_kernel(bits, node_keep, node_received, edge_keep, edge_received, *refs):
    def sums(half, place):
        columns = pl.ds(half * refs[0].shape[2], refs[0].shape[2])
        return jnp.concatenate(
            [
                kept[place, :, columns].astype(F32) + received[place, :, columns].astype(F32)
                for kept, received in ((node_keep, node_received), (edge_keep, edge_received))
            ],
            axis=0,
        )

    fold(sums, refs[0:2], refs[2:4], refs[4:6], refs[6:8], bits, bits)


def later_fold_kernel(bits, positions, *refs):
    def sums(half, place):
        return refs[half][place].astype(F32) + refs[2 + half][place].astype(F32)

    fold(sums, refs[4:6], refs[6:8], refs[8:10], refs[10:12], bits, positions)


def shares_kernel(left, right, left_in, right_in, *refs):
    outs, stages, sems = refs[:4], refs[4:8], refs[8]
    total = jnp.concatenate(
        [a[0].astype(F32) + b[0].astype(F32) for a, b in ((left, left_in), (right, right_in))], axis=1
    )
    start = 0
    copies = []
    for k, (out, stage) in enumerate(zip(outs, stages)):
        stage[...] = total[start : start + out.shape[0]]
        start += out.shape[0]
        copies.append(pltpu.make_async_copy(stage, out, sems.at[k]))
        copies[-1].start()
    for copy in copies:
        copy.wait()


VMEM, HBM, SMEM = pltpu.VMEM, pltpu.HBM, pltpu.SMEM


def call(body, name, operands, outs, scratch=(), flops=0):
    spaces = [space for _, space in operands]
    arrays = [
        array if space is SMEM else pltpu.with_memory_space_constraint(array, space) for array, space in operands
    ]
    moved = sum(a.size * a.dtype.itemsize for a, _ in operands)
    return pl.pallas_call(
        body,
        in_specs=[pl.BlockSpec(memory_space=space) for space in spaces],
        out_specs=[pl.BlockSpec(memory_space=space) for space, _, _ in outs],
        out_shape=[space(shape, dtype) for space, shape, dtype in outs],
        scratch_shapes=scratch,
        name=name,
        cost_estimate=pl.CostEstimate(flops=flops, bytes_accessed=moved, transcendentals=0),
        compiler_params=pltpu.CompilerParams(vmem_limit_bytes=24 * MIB),
    )(*arrays)


def semaphores(count):
    return pltpu.SemaphoreType.DMA((count,))


def fold_call(body, name, operands, shape):
    out = call(
        body,
        name,
        [(array, VMEM) for array in operands],
        [(HBM, shape, BF16), (HBM, shape, BF16), (VMEM, shape, BF16), (VMEM, shape, BF16)],
        [VMEM(shape, BF16), VMEM(shape, BF16), semaphores(shape[0]), semaphores(shape[0])],
    )
    return out[:2], out[2:]


def shards(
    node_feat,
    edge_feat,
    grad_nodes,
    grad_edges,
    edge_first,
    edge_second,
    node_first,
    node_second,
    gains,
    edge_peer,
    edge_slot,
    edge_recv,
    send_index,
    live_blocks,
):
    nodes, width = node_feat.shape
    edges = edge_feat.shape[0]
    devices, capacity = send_index.shape[1:]
    chips = devices // 2
    halo_rows = devices * capacity
    peer, slot, recv = (a.reshape(edges // EDGE_BLOCK, EDGE_BLOCK) for a in (edge_peer, edge_slot, edge_recv))
    other_core = [(i, i ^ 1) for i in range(devices)]
    block = width * width * 2

    send_table = jnp.swapaxes(send_index, 1, 2)
    (outgoing,) = call(
        outgoing_kernel,
        "outgoing",
        [(node_feat, HBM), (send_table, HBM)],
        [(HBM, (halo_rows, width), BF16)],
        [
            VMEM(node_feat.shape, BF16),
            VMEM(send_table.shape, INT),
            VMEM((halo_rows, width), BF16),
            semaphores(2),
        ],
    )
    halo = lax.all_to_all(
        outgoing.reshape(devices, capacity, width), "space", split_axis=0, concat_axis=0, tiled=True
    ).reshape(halo_rows, width)

    rows_bf16, nodes_f32 = (edges, width), (nodes, width)
    top_shape, place_shape = (width, width), (2 * nodes + halo_rows, edges)
    part, far, top, second, node_part, receive, place = call(
        prepare_kernel,
        "prepare",
        [
            (live_blocks, SMEM),
            *(
                (a, HBM)
                for a in (peer, slot, recv, node_feat, edge_first, edge_feat, node_first, edge_second)
            ),
        ],
        [
            (VMEM, rows_bf16, F32),
            (VMEM, (edges, halo_rows), BF16),
            (VMEM, top_shape, BF16),
            (VMEM, edge_second.shape, BF16),
            (HBM, nodes_f32, F32),
            (HBM, (edges, nodes), BF16),
            (HBM, place_shape, BF16),
        ],
        [
            VMEM(peer.shape, INT),
            VMEM(slot.shape, INT),
            VMEM(recv.shape, INT),
            VMEM(node_feat.shape, BF16),
            VMEM(edge_first.shape, BF16),
            VMEM(edge_feat.shape, BF16),
            VMEM(top_shape, BF16),
            VMEM(nodes_f32, F32),
            VMEM((edges, nodes), BF16),
            VMEM(place_shape, BF16),
            VMEM((2 * nodes, width), BF16),
            semaphores(9),
            semaphores(3),
        ],
        flops=block * (2 * edges + 3 * nodes),
    )

    share = node_first.shape[0] // devices + node_second.shape[0] // devices
    slope, hidden, normed, inv_std, grad_agg, node_gain, node_keep, node_base, node_send = call(
        forward_kernel,
        "forward",
        [
            *((a, VMEM) for a in (part, halo, far, top, second)),
            *((a, HBM) for a in (gains, place, node_part, node_first, node_second, grad_nodes, node_feat)),
        ],
        [
            (VMEM, rows_bf16, BF16),
            (VMEM, rows_bf16, BF16),
            (VMEM, rows_bf16, BF16),
            (VMEM, (edges, 128), F32),
            (VMEM, nodes_f32, BF16),
            (VMEM, (1, width), F32),
            (VMEM, (chips, share, width), BF16),
            (HBM, nodes_f32, F32),
            (HBM, (chips, share, width), BF16),
        ],
        [
            VMEM(gains.shape, F32),
            VMEM((nodes, edges), BF16),
            VMEM(nodes_f32, F32),
            VMEM(node_first.shape, BF16),
            VMEM(node_second.shape, BF16),
            VMEM(nodes_f32, BF16),
            VMEM(nodes_f32, BF16),
            VMEM(rows_bf16, BF16),
            VMEM(node_first.shape, F32),
            VMEM(node_second.shape, F32),
            VMEM(nodes_f32, F32),
            VMEM((chips, share, width), BF16),
            semaphores(7),
            semaphores(chips),
            semaphores(1),
        ],
        flops=block * (2 * edges + 9 * nodes),
    )
    node_received = lax.ppermute(node_send, "space", other_core)

    share = edge_first.shape[0] // devices + edge_second.shape[0] // devices
    back_shape = (devices, capacity + 8, width)
    edge_keep, node_total, grad_edge_feat, back, edge_send = call(
        backward_kernel,
        "backward",
        [
            (live_blocks, SMEM),
            *(
                (a, VMEM)
                for a in (
                    grad_edges,
                    slope,
                    hidden,
                    normed,
                    inv_std,
                    grad_agg,
                    node_gain,
                    halo,
                    second,
                    receive,
                    edge_first,
                    gains,
                )
            ),
            *((a, HBM) for a in (place, edge_feat, node_feat, node_base)),
        ],
        [
            (VMEM, (chips, share, width), BF16),
            (HBM, nodes_f32, F32),
            (HBM, rows_bf16, BF16),
            (HBM, back_shape, BF16),
            (HBM, (chips, share, width), BF16),
        ],
        [
            VMEM(place_shape, BF16),
            VMEM(rows_bf16, BF16),
            VMEM(nodes_f32, BF16),
            VMEM(nodes_f32, F32),
            VMEM(rows_bf16, BF16),
            VMEM(rows_bf16, BF16),
            VMEM(rows_bf16, BF16),
            VMEM(back_shape, BF16),
            VMEM(edge_first.shape, F32),
            VMEM(edge_second.shape, F32),
            VMEM((chips, share, width), BF16),
            semaphores(chips),
            semaphores(edges // CHUNK),
            semaphores(2),
            semaphores(4),
        ],
        flops=block * (6 * edges),
    )

    edge_received = lax.ppermute(edge_send, "space", other_core)
    halves = (node_keep, node_received, edge_keep, edge_received)
    orders = exchange_orders(chips)
    bits = [order[0] for order in orders]
    shape = (chips // 2, node_keep.shape[1] + edge_keep.shape[1], width // 2)
    sent, kept = fold_call(functools.partial(first_fold_kernel, bits), "first_fold", halves, shape)
    received = exchange(sent, bits, devices)
    returned = lax.all_to_all(back, "space", split_axis=0, concat_axis=0, tiled=True)
    for done in range(1, len(orders[0])):
        bits = [order[done] for order in orders]
        positions = [
            bit - sum(earlier < bit for earlier in order[:done]) for bit, order in zip(bits, orders)
        ]
        shape = (shape[0] // 2, *shape[1:])
        sent, kept = fold_call(
            functools.partial(later_fold_kernel, bits, positions), "later_fold", (*kept, *received), shape
        )
        received = exchange(sent, bits, devices)

    grad_node_feat, gain_totals = call(
        nodes_kernel,
        "nodes",
        [(node_total, HBM), (returned, VMEM), (send_table, HBM)],
        [(HBM, (nodes, width), BF16), (HBM, (2, width), F32)],
        [VMEM((nodes, width), F32), VMEM(send_table.shape, INT), VMEM((nodes, width), BF16), VMEM((2, width), F32), semaphores(2)],
    )
    shapes = [(w.shape[0] // devices, width) for w in (node_first, node_second, edge_first, edge_second)]
    grad_node_first, grad_node_second, grad_edge_first, grad_edge_second = call(
        shares_kernel,
        "shares",
        [(a, VMEM) for a in (*kept, *received)],
        [(HBM, shape, F32) for shape in shapes],
        [*(VMEM(shape, F32) for shape in shapes), semaphores(4)],
    )
    return (
        grad_node_feat,
        grad_edge_feat,
        grad_edge_first,
        grad_edge_second,
        grad_node_first,
        grad_node_second,
        gain_totals,
    )


def solution(mesh):
    placed = (
        P(("group", "space"), None),
        P(("group", "space"), None),
        P(("group", "space"), None),
        P(("group", "space"), None),
        P(),
        P(),
        P(),
        P(),
        P(),
        P(("group", "space")),
        P(("group", "space")),
        P(("group", "space")),
        P(("group", "space"), None, None),
        P(("group", "space")),
    )
    return jax.shard_map(
        shards,
        mesh=mesh,
        in_specs=placed,
        out_specs=(
            P(("group", "space"), None),
            P(("group", "space"), None),
            P(("group", "space"), None),
            P(("group", "space"), None),
            P(("group", "space"), None),
            P(("group", "space"), None),
            P("group", None),
        ),
        check_vma=False,
    )
```

time: 319 us -> 74 us (0.23)
  waiting for transfers between devices: 148 us -> 26.9 us
  local copies, waits for them, and re-layouts: 44.5 us -> 0.02 us
  other arithmetic: 39.4 us -> 0 us
  blocking collectives: 33.9 us -> 0 us
  Pallas kernels: 0 us -> 27.3 us
  matrix products: 23.6 us -> 0 us
  between operations: 14.8 us -> 1.44 us
  starting transfers between devices: 13.8 us -> 17.9 us
    reduce_scatter x4 -> x0, waiting for transfers between devices: 148 us -> none  [the longest x1 69.9 us: shards(): lax.psum_scatter(first_sum, 'space', scatter_dimension=0, tiled=True)]
    psum x1 -> x0, blocking collectives: 33.9 us -> none  [shards(): gain_totals = lax.psum((gain_sum, node_gain), 'space')]
    pallas_call x0 -> x9, Pallas kernels: none -> 27.3 us  [call(): pl.pallas_call(body, in_specs=[pl.BlockSpec(memory_space=space) for space...]
    scatter-add x4 -> x0, other arithmetic: 26.7 us -> none  [the longest x2 17.8 us: backward_step(): totals = totals.at[sender_ids].add(grad_in[:, :feat_width]).at[receiver_i...]
    ppermute x0 -> x8, waiting for transfers between devices: none -> 24.3 us  [the longest x6 21.1 us: exchange(): lax.ppermute(piece, 'space', [(i, i ^ 2 << bit) for i in range(devices)])]
    dot_general x12 -> x0, matrix products: 23.6 us -> none  [the longest x4 8.68 us: transposed_times(): lax.dot_general(left, right, (((0,), (0,)), ((), ())), preferred_element_...]
    gather x5 -> x0, local copies, waits for them, and re-layouts: 20.1 us -> none  [the longest x2 7.41 us: backward_step(): grad_aggregate[receiver_ids].astype(jnp.float32)]
    unnamed x56 -> x10, local copies, waits for them, and re-layouts: 17.3 us -> 0.02 us
  transfers between devices with their start and end apart: 6 -> 10, of which waited for: 3 -> 8; matrix products, arithmetic and copies ran while one was open for 21% -> 0% of each run, Pallas kernels for 0% -> 11%
where the time goes in v2:
time: 74 us; the launch traced here: 73.6 us
  Pallas kernels  27.3 us (37%)
  waiting for transfers between devices  26.9 us (36%)
  starting transfers between devices  17.9 us (24%)
  between operations  1.44 us (2%)
    pallas_call x9, Pallas kernels, call(): pl.pallas_call(body, in_specs=[pl.BlockSpec(memory_space=space) for space...  27.3 us
    ppermute x6, waiting for transfers between devices, exchange(): lax.ppermute(piece, 'space', [(i, i ^ 2 << bit) for i in range(devices)])  21.1 us
    all_to_all x1, starting transfers between devices, shards(): lax.all_to_all(outgoing.reshape(devices, capacity, width), 'space', split...  7.39 us
    ppermute x6, starting transfers between devices, exchange(): lax.ppermute(piece, 'space', [(i, i ^ 2 << bit) for i in range(devices)])  5.9 us
    all_to_all x1, starting transfers between devices, shards(): lax.all_to_all(back, 'space', split_axis=0, concat_axis=0, tiled=True)  4 us
    ppermute x1, waiting for transfers between devices, shards(): node_received = lax.ppermute(node_send, 'space', other_core)  3.27 us
    all_to_all x1, waiting for transfers between devices, shards(): lax.all_to_all(outgoing.reshape(devices, capacity, width), 'space', split...  2.57 us
  transfers between devices with their start and end apart: 10, of which 8 were waited for; matrix products, arithmetic and copies ran while one was open for 0% of the time, Pallas kernels for 11%

profile of v2, /device:TPU:0, one launch (start us, length us, event | category | flops | bytes accessed | tf_op | source)
XLA Modules:
  0.0 73.6 jit_solution(11084264888578714997)
XLA Ops:
  0.6 1.8 %outgoing.1 = bf16[128,512]{1,0:T(8,128)(2,1)} custom-call(bf16[256,512]{1,0:T(8,128)(2,1)} %node_hbm.7, s32[1,8,16]{2,1,0:T(8,128)} %bitcast.9), custom_call_target="tpu_custom_call" | custom-call | bytes 262656 | tf_op jit(solution)/shard_map/outgoing/pallas_call | solution.py:499
  2.5 7.4 %all-to-all-start = ((bf16[16,8,512]{2,1,0:T(8,128)(2,1)}), bf16[16,8,512]{2,1,0:T(8,128)(2,1)S(1)}, u32[]{:S(2)}, u32[]{:S(2)}) async-start(bf16[16,8,512]{2,1,0:T(8,128)(2,1)} %bitcast.8), calls=%async_computation | async-start | bytes 262144 | tf_op jit(solution)/shard_map/all_to_all | solution.py:564
  10.5 4.7 %prepare.1 = (f32[1024,512]{1,0:T(8,128)S(1)}, bf16[1024,128]{1,0:T(8,128)(2,1)S(1)}, bf16[512,512]{1,0:T(8,128)(2,1)S(1)}, bf16[512,512]{1,0:T(8,128)(2,1)S(1)}...) custom-call(s32[1]{0:T(128)S(6)} %copy.21.live_ref, s32[8,128]{1,0:T(8,128)} %bitcast.11, ...), custom_call_target="tpu_custom_call" | custom-call | flops 1476395008 | bytes 4468740 | tf_op jit(solution)/shard_map/prepare/pallas_call | solution.py:499
  15.2 2.6 %all-to-all-done = bf16[16,8,512]{2,1,0:T(8,128)(2,1)S(1)} async-done(((bf16[16,8,512]{2,1,0:T(8,128)(2,1)}), bf16[16,8,512]{2,1,0:T(8,128)(2,1)S(1)}, u32[]{:S(2)}, u32[]{:S(2)}) %all-to-all-start) | async-done | bytes 131104 | tf_op jit(solution)/shard_map/all_to_all | solution.py:564
  17.8 6.5 %forward.1 = (bf16[1024,512]{1,0:T(8,128)(2,1)S(1)}, bf16[1024,512]{1,0:T(8,128)(2,1)S(1)}, bf16[1024,512]{1,0:T(8,128)(2,1)S(1)}, f32[1024,128]{1,0:T(8,128)S(1...) custom-call(f32[1024,512]{1,0:T(8,128)S(1)} %get-tuple-element.46.pa, ...), custom_call_target="tpu_custom_call" | custom-call | flops 2281701376 | bytes 7475200 | tf_op jit(solution)/shard_map/forward/pallas_call | solution.py:499
  24.3 0.0 copy-done
  24.3 0.0 copy-done.1
  24.3 8.8 %backward.1 = (bf16[8,128,512]{2,1,0:T(8,128)(2,1)S(1)}, f32[256,512]{1,0:T(8,128)}, bf16[1024,512]{1,0:T(8,128)(2,1)}, bf16[16,16,512]{2,1,0:T(8,128)(2,1)}, bf16[8,128,512]{2,1,0:T(8,128)(2,1)}) custom-call(s32[1]{0:T(128)S(6)} %copy.21.live_ref, bf16[1024,512]{1,0:T(8,128)(2,1)S(1)} %copy-done.1, bf16[1024,512]{1,0:T(8,128)(2,1)S(1)} %get-tuple-element.52.slope_ref, ...), custom_call_target="tpu_custom_call" | custom-call | flops 3221225472 | bytes 10885124 | tf_op jit(solution)/shard_map/backward/pallas_call | solution.py:499
  33.2 0.1 collective-permute-start.1
  33.2 0.0 copy-done.4
  33.3 0.5 collective-permute-start
  33.7 3.3 %collective-permute-done.node_received = bf16[8,96,512]{2,1,0:T(8,128)(2,1)S(1)} collective-permute-done((bf16[8,96,512]{2,1,0:T(8,128)(2,1)S(1)}, bf16[8,96,512]{2,1,0:T(8,128)(2,1)S(1)}, u32[]{:S(2)}, u32[]{:S(2)}) %collective-permute-start) | collective-permute-done | bytes 786464 | tf_op jit(solution)/shard_map/ppermute | solution.py:645
  37.0 0.0 collective-permute-done.1.edge_received
  37.0 1.0 %first_fold.1 = (bf16[4,224,256]{2,1,0:T(8,128)(2,1)}, bf16[4,224,256]{2,1,0:T(8,128)(2,1)}, bf16[4,224,256]{2,1,0:T(8,128)(2,1)S(1)}, bf16[4,224,256]{2,1,0:T(8,128)(2,1)S(1)}) custom-call(bf16[8,96,512]{2,1,0:T(8,128)(2,1)S(1)} %get-tuple-element.64.node_keep, bf16[8,96,512]{2,1,0:T(8,128)(2,1)S(1)} %collective-permute-done.node_received, ...), custom_call_target="tpu_custom_call" | custom-call | bytes 3670016 | tf_op jit(solution)/shard_map/first_fold/pallas_call | solution.py:499
  38.1 0.1 collective-permute-start.2
  38.2 0.9 %collective-permute-start.3 = (bf16[4,224,256]{2,1,0:T(8,128)(2,1)}, bf16[4,224,256]{2,1,0:T(8,128)(2,1)S(1)}, u32[]{:S(2)}, u32[]{:S(2)}) collective-permute-start(bf16[4,224,256]{2,1,0:T(8,128)(2,1)} %get-tuple-element.71), channel_id=1, source_target_pairs={{0,4},{1,5},{2,6},{3,7},{4,0},{5,1},{6,2},{7,3},{8,12},{9,13},{10,... | collective-permute-start | bytes 1376264 | tf_op jit(solution)/shard_map/ppermute | solution.py:423
  39.0 4.0 %all-to-all-start.1 = ((bf16[16,16,512]{2,1,0:T(8,128)(2,1)}), bf16[16,16,512]{2,1,0:T(8,128)(2,1)S(1)}, u32[]{:S(2)}, u32[]{:S(2)}) async-start(bf16[16,16,512]{2,1,0:T(8,128)(2,1)} %get-tuple-element.61), calls=%async_computation.1 | async-start | bytes 524288 | tf_op jit(solution)/shard_map/all_to_all | solution.py:707
  43.0 8.9 %collective-permute-done.2.refs_2_ = bf16[4,224,256]{2,1,0:T(8,128)(2,1)S(1)} collective-permute-done((bf16[4,224,256]{2,1,0:T(8,128)(2,1)}, bf16[4,224,256]{2,1,0:T(8,128)(2,1)S(1)}, u32[]{:S(2)}, u32[]{:S(2)}) %collective-permute-start.2) | collective-permute-done | bytes 458784 | tf_op jit(solution)/shard_map/ppermute | solution.py:423
  52.0 2.2 %collective-permute-done.3.refs_3_ = bf16[4,224,256]{2,1,0:T(8,128)(2,1)S(1)} collective-permute-done((bf16[4,224,256]{2,1,0:T(8,128)(2,1)}, bf16[4,224,256]{2,1,0:T(8,128)(2,1)S(1)}, u32[]{:S(2)}, u32[]{:S(2)}) %collective-permute-start.3) | collective-permute-done | bytes 458784 | tf_op jit(solution)/shard_map/ppermute | solution.py:423
  54.1 0.8 %later_fold.2 = (bf16[2,224,256]{2,1,0:T(8,128)(2,1)}, bf16[2,224,256]{2,1,0:T(8,128)(2,1)}, bf16[2,224,256]{2,1,0:T(8,128)(2,1)S(1)}, bf16[2,224,256]{2,1,0:T(8,128)(2,1)S(1)}) custom-call(bf16[4,224,256]{2,1,0:T(8,128)(2,1)S(1)} %get-tuple-element.68.refs_0_, bf16[4,224,256]{2,1,0:T(8,128)(2,1)S(1)} %get-tuple-element.69.refs_1_, ...), custom_call_target="tpu_custom_call" | custom-call | bytes 1835008 | tf_op jit(solution)/shard_map/later_fold/pallas_call | solution.py:499
  55.0 0.1 collective-permute-start.4
  55.1 1.9 %collective-permute-start.5 = (bf16[2,224,256]{2,1,0:T(8,128)(2,1)}, bf16[2,224,256]{2,1,0:T(8,128)(2,1)S(1)}, u32[]{:S(2)}, u32[]{:S(2)}) collective-permute-start(bf16[2,224,256]{2,1,0:T(8,128)(2,1)} %get-tuple-element.75), channel_id=1, source_target_pairs={{0,2},{1,3},{2,0},{3,1},{4,6},{5,7},{6,4},{7,5},{8,10},{9,11},{10,... | collective-permute-start | bytes 688136 | tf_op jit(solution)/shard_map/ppermute | solution.py:423
  57.0 4.3 %collective-permute-done.4.refs_2_ = bf16[2,224,256]{2,1,0:T(8,128)(2,1)S(1)} collective-permute-done((bf16[2,224,256]{2,1,0:T(8,128)(2,1)}, bf16[2,224,256]{2,1,0:T(8,128)(2,1)S(1)}, u32[]{:S(2)}, u32[]{:S(2)}) %collective-permute-start.4) | collective-permute-done | bytes 229408 | tf_op jit(solution)/shard_map/ppermute | solution.py:423
  61.3 0.1 collective-permute-done.5.refs_3_
  61.4 0.7 later_fold.3
  62.1 2.3 %collective-permute-start.6 = (bf16[1,224,256]{2,1,0:T(8,128)(2,1)}, bf16[1,224,256]{2,1,0:T(8,128)(2,1)S(1)}, u32[]{:S(2)}, u32[]{:S(2)}) collective-permute-start(bf16[1,224,256]{2,1,0:T(8,128)(2,1)} %get-tuple-element.78), channel_id=1, source_target_pairs={{0,8},{1,9},{2,10},{3,11},{4,12},{5,13},{6,14},{7,15},{8,0},{9,1},... | collective-permute-start | bytes 344072 | tf_op jit(solution)/shard_map/ppermute | solution.py:423
  64.4 0.7 collective-permute-start.7
  65.1 0.0 all-to-all-done.1.returned_ref
  65.1 2.1 %nodes.1 = (bf16[256,512]{1,0:T(8,128)(2,1)}, f32[2,512]{1,0:T(2,128)}) custom-call(f32[256,512]{1,0:T(8,128)} %get-tuple-element.60.total_hbm, bf16[16,16,512]{2,1,0:T(8,128)(2,1)S(1)} %all-to-all-done.1.returned_ref, s32[1,8,16]{2,1,0:T(8,128)} %bitcast.10), custom_call_target="tpu_custom_call" | custom-call | bytes 786944 | tf_op jit(solution)/shard_map/nodes/pallas_call | solution.py:499
  67.2 4.3 %collective-permute-done.6.left_in = bf16[1,224,256]{2,1,0:T(8,128)(2,1)S(1)} collective-permute-done((bf16[1,224,256]{2,1,0:T(8,128)(2,1)}, bf16[1,224,256]{2,1,0:T(8,128)(2,1)S(1)}, u32[]{:S(2)}, u32[]{:S(2)}) %collective-permute-start.6) | collective-permute-done | bytes 114720 | tf_op jit(solution)/shard_map/ppermute | solution.py:423
  71.5 1.2 %collective-permute-done.7.right_in = bf16[1,224,256]{2,1,0:T(8,128)(2,1)S(1)} collective-permute-done((bf16[1,224,256]{2,1,0:T(8,128)(2,1)}, bf16[1,224,256]{2,1,0:T(8,128)(2,1)S(1)}, u32[]{:S(2)}, u32[]{:S(2)}) %collective-permute-start.7) | collective-permute-done | bytes 114720 | tf_op jit(solution)/shard_map/ppermute | solution.py:423
  72.7 0.8 %shares.1 = (f32[64,512]{1,0:T(8,128)}, f32[32,512]{1,0:T(8,128)}, f32[96,512]{1,0:T(8,128)}, f32[32,512]{1,0:T(8,128)}) custom-call(bf16[1,224,256]{2,1,0:T(8,128)(2,1)S(1)} %get-tuple-element.76.left, bf16[1,224,256]{2,1,0:T(8,128)(2,1)S(1)} %get-tuple-element.77.right, bf16[1,224,256]{2,1,0:T(8,128)(2,1)S(1)} %collective-permute-done.6.left_in, ...), custom_call_target="tpu_custom_call" | custom-call | bytes 458752 | tf_op jit(solution)/shard_map/shares/pallas_call | solution.py:499
  (7 shorter events, 0.0 us)
Async XLA Ops:
  2.5 15.3 %all-to-all-start = ((bf16[16,8,512]{2,1,0:T(8,128)(2,1)}), bf16[16,8,512]{2,1,0:T(8,128)(2,1)S(1)}, u32[]{:S(2)}, u32[]{:S(2)}) async-start(bf16[16,8,512]{2,1,0:T(8,128)(2,1)} %bitcast.8), calls=%async_computation | async-start | bytes 262144 | tf_op jit(solution)/shard_map/all_to_all | solution.py:564
  17.8 6.5 %copy-start = (bf16[1536,512]{1,0:T(8,128)(2,1)S(1)}, bf16[1536,512]{1,0:T(8,128)(2,1)}, u32[]{:S(2)}) copy-start(bf16[1536,512]{1,0:T(8,128)(2,1)} %first_ref.1) | copy-start | bytes 4718596
  17.8 6.5 %copy-start.1 = (bf16[1024,512]{1,0:T(8,128)(2,1)S(1)}, bf16[1024,512]{1,0:T(8,128)(2,1)}, u32[]{:S(2)}) copy-start(bf16[1024,512]{1,0:T(8,128)(2,1)} %grad_edges_ref.1) | copy-start | bytes 3145732
  17.8 6.5 %copy-start.2 = (f32[2,512]{1,0:T(2,128)S(1)}, f32[2,512]{1,0:T(2,128)}, u32[]{:S(2)}) copy-start(f32[2,512]{1,0:T(2,128)} %gains_ref.1) | copy-start | bytes 12292
  17.8 6.5 %copy-start.3 = (bf16[1024,256]{1,0:T(8,128)(2,1)S(1)}, bf16[1024,256]{1,0:T(8,128)(2,1)}, u32[]{:S(2)}) copy-start(bf16[1024,256]{1,0:T(8,128)(2,1)} %get-tuple-element.58.receive_ref) | copy-start | bytes 1572868
  24.3 8.9 %copy-start.4 = (bf16[8,96,512]{2,1,0:T(8,128)(2,1)S(1)}, bf16[8,96,512]{2,1,0:T(8,128)(2,1)}, u32[]{:S(2)}) copy-start(bf16[8,96,512]{2,1,0:T(8,128)(2,1)} %get-tuple-element.65) | copy-start | bytes 2359300
  33.2 3.9 %collective-permute-start.1 = (bf16[8,128,512]{2,1,0:T(8,128)(2,1)}, bf16[8,128,512]{2,1,0:T(8,128)(2,1)S(1)}, u32[]{:S(2)}, u32[]{:S(2)}) collective-permute-start(bf16[8,128,512]{2,1,0:T(8,128)(2,1)} %get-tuple-element.67), channel_id=1, source_target_pairs={{0,1},{1,0},{2,3},{3,2},{4,5},{5,4},{6,7},{7,6},{8,9},{9,8},{10,11... | collective-permute-start | bytes 3145736 | tf_op jit(solution)/shard_map/ppermute | solution.py:700
  33.3 3.8 %collective-permute-start = (bf16[8,96,512]{2,1,0:T(8,128)(2,1)S(1)}, bf16[8,96,512]{2,1,0:T(8,128)(2,1)S(1)}, u32[]{:S(2)}, u32[]{:S(2)}) collective-permute-start(bf16[8,96,512]{2,1,0:T(8,128)(2,1)S(1)} %copy-done.4), channel_id=1, source_target_pairs={{0,1},{1,0},{2,3},{3,2},{4,5},{5,4},{6,7},{7,6},{8,9},{9,8},{10,11... | collective-permute-start | bytes 2359304 | tf_op jit(solution)/shard_map/ppermute | solution.py:645
  38.1 13.9 %collective-permute-start.2 = (bf16[4,224,256]{2,1,0:T(8,128)(2,1)}, bf16[4,224,256]{2,1,0:T(8,128)(2,1)S(1)}, u32[]{:S(2)}, u32[]{:S(2)}) collective-permute-start(bf16[4,224,256]{2,1,0:T(8,128)(2,1)} %get-tuple-element.70), channel_id=1, source_target_pairs={{0,2},{1,3},{2,0},{3,1},{4,6},{5,7},{6,4},{7,5},{8,10},{9,11},{10,... | collective-permute-start | bytes 1376264 | tf_op jit(solution)/shard_map/ppermute | solution.py:423
  38.2 16.0 %collective-permute-start.3 = (bf16[4,224,256]{2,1,0:T(8,128)(2,1)}, bf16[4,224,256]{2,1,0:T(8,128)(2,1)S(1)}, u32[]{:S(2)}, u32[]{:S(2)}) collective-permute-start(bf16[4,224,256]{2,1,0:T(8,128)(2,1)} %get-tuple-element.71), channel_id=1, source_target_pairs={{0,4},{1,5},{2,6},{3,7},{4,0},{5,1},{6,2},{7,3},{8,12},{9,13},{10,... | collective-permute-start | bytes 1376264 | tf_op jit(solution)/shard_map/ppermute | solution.py:423
  39.0 26.1 %all-to-all-start.1 = ((bf16[16,16,512]{2,1,0:T(8,128)(2,1)}), bf16[16,16,512]{2,1,0:T(8,128)(2,1)S(1)}, u32[]{:S(2)}, u32[]{:S(2)}) async-start(bf16[16,16,512]{2,1,0:T(8,128)(2,1)} %get-tuple-element.61), calls=%async_computation.1 | async-start | bytes 524288 | tf_op jit(solution)/shard_map/all_to_all | solution.py:707
  55.0 6.3 %collective-permute-start.4 = (bf16[2,224,256]{2,1,0:T(8,128)(2,1)}, bf16[2,224,256]{2,1,0:T(8,128)(2,1)S(1)}, u32[]{:S(2)}, u32[]{:S(2)}) collective-permute-start(bf16[2,224,256]{2,1,0:T(8,128)(2,1)} %get-tuple-element.74), channel_id=1, source_target_pairs={{0,4},{1,5},{2,6},{3,7},{4,0},{5,1},{6,2},{7,3},{8,12},{9,13},{10,... | collective-permute-start | bytes 688136 | tf_op jit(solution)/shard_map/ppermute | solution.py:423
  55.1 6.3 %collective-permute-start.5 = (bf16[2,224,256]{2,1,0:T(8,128)(2,1)}, bf16[2,224,256]{2,1,0:T(8,128)(2,1)S(1)}, u32[]{:S(2)}, u32[]{:S(2)}) collective-permute-start(bf16[2,224,256]{2,1,0:T(8,128)(2,1)} %get-tuple-element.75), channel_id=1, source_target_pairs={{0,2},{1,3},{2,0},{3,1},{4,6},{5,7},{6,4},{7,5},{8,10},{9,11},{10,... | collective-permute-start | bytes 688136 | tf_op jit(solution)/shard_map/ppermute | solution.py:423
  62.1 9.4 %collective-permute-start.6 = (bf16[1,224,256]{2,1,0:T(8,128)(2,1)}, bf16[1,224,256]{2,1,0:T(8,128)(2,1)S(1)}, u32[]{:S(2)}, u32[]{:S(2)}) collective-permute-start(bf16[1,224,256]{2,1,0:T(8,128)(2,1)} %get-tuple-element.78), channel_id=1, source_target_pairs={{0,8},{1,9},{2,10},{3,11},{4,12},{5,13},{6,14},{7,15},{8,0},{9,1},... | collective-permute-start | bytes 344072 | tf_op jit(solution)/shard_map/ppermute | solution.py:423
  64.4 8.4 %collective-permute-start.7 = (bf16[1,224,256]{2,1,0:T(8,128)(2,1)}, bf16[1,224,256]{2,1,0:T(8,128)(2,1)S(1)}, u32[]{:S(2)}, u32[]{:S(2)}) collective-permute-start(bf16[1,224,256]{2,1,0:T(8,128)(2,1)} %get-tuple-element.79), channel_id=1, source_target_pairs={{0,8},{1,9},{2,10},{3,11},{4,12},{5,13},{6,14},{7,15},{8,0},{9,1},... | collective-permute-start | bytes 344072 | tf_op jit(solution)/shard_map/ppermute | solution.py:423

commit v3 on v2

v3 whole, which is shorter than its diff:
```python
import functools

import jax
import jax.numpy as jnp
from jax import lax
from jax.experimental import pallas as pl
from jax.experimental.pallas import tpu as pltpu
from jax.sharding import PartitionSpec as P

EDGE_BLOCK = 128
CHUNK = 512
GAIN_ROWS = 16
EPS = 1e-05
BF16 = jnp.bfloat16
F32 = jnp.float32
INT = jnp.int32
MIB = 1 << 20


def dot(left, right):
    return lax.dot_general(left, right, (((1,), (0,)), ((), ())), preferred_element_type=F32)


def times_transposed(left, right):
    return lax.dot_general(left, right, (((1,), (1,)), ((), ())), preferred_element_type=F32)


def transposed_times(left, right):
    return lax.dot_general(left, right, (((0,), (0,)), ((), ())), preferred_element_type=F32)


def ones_where(mask):
    return jnp.where(mask, 1.0, 0.0).astype(BF16)


def chosen(row, width):
    lane = lax.broadcasted_iota(INT, (EDGE_BLOCK, EDGE_BLOCK), 1)
    col = jnp.transpose(jnp.broadcast_to(row, (EDGE_BLOCK, EDGE_BLOCK)))
    return jnp.concatenate(
        [ones_where(col == lane + EDGE_BLOCK * j) for j in range(width // EDGE_BLOCK)], axis=1
    )


def chosen_transposed(row, width):
    return ones_where(lax.broadcasted_iota(INT, (width, EDGE_BLOCK), 0) == row)


def send_choice(table_ref, node_rows):
    capacity, devices = table_ref.shape[1:]
    lane = lax.broadcasted_iota(INT, (capacity, node_rows), 1)
    table = table_ref[0]
    out = [jnp.where(table[:, j : j + 1] == lane, 1.0, 0.0) for j in range(devices)]
    return jnp.concatenate(out, axis=0).astype(BF16)


def activation(pre):
    sigmoid = 0.5 * jnp.tanh(0.5 * pre) + 0.5
    hidden = pre * sigmoid
    return hidden.astype(BF16), sigmoid + hidden * (1.0 - sigmoid)


def normalize(post):
    centred = post - jnp.mean(post, axis=-1, keepdims=True)
    inv_std = lax.rsqrt(jnp.mean(centred * centred, axis=-1, keepdims=True) + EPS)
    return centred * inv_std, inv_std


def grad_normalize(grad_out, gain, normed, inv_std):
    grad_normed = grad_out * gain
    return (
        inv_std
        * (
            grad_normed
            - jnp.mean(grad_normed, axis=-1, keepdims=True)
            - normed * jnp.mean(grad_normed * normed, axis=-1, keepdims=True)
        )
    ).astype(BF16)


def pack(keep_ref, send_ref, stage, sems, sources, tail):
    chips = stage.shape[0]
    core = lax.rem(lax.axis_index("space"), 2)
    copies = []
    for away in (True, False):
        for k in range(chips):
            place = 2 * k + 1 - core if away else 2 * k + core
            pieces = []
            for source in sources:
                share = source.shape[0] // (2 * chips)
                pieces.append(source[pl.ds(pl.multiple_of(place * share, 8), share), :])
            rows = jnp.concatenate([*pieces, *tail], axis=0).astype(BF16)
            if away:
                stage[k] = rows
                copies.append(pltpu.make_async_copy(stage.at[k], send_ref.at[k], sems.at[k]))
                copies[-1].start()
            else:
                keep_ref[k] = rows
    return copies


def weight_grads(columns, acts, grads, outs, sums, tail=()):
    place, edge, node, halo, hidden, aggregate, node_hidden = acts
    grad_pre, grad_post, node_grad_pre, node_grad_post = grads
    placed_ref, keep_ref, send_ref, stage, sems = outs
    node_first, node_second, edge_first, edge_second = sums
    nodes, width = node.shape
    far_end = place.shape[0] - nodes
    pre = grad_pre[:, columns]
    placed = dot(place[...], pre).astype(BF16)
    placed_ref[...] = placed
    edge_second[...] = transposed_times(hidden[...], grad_post[:, columns])
    edge_first[2 * width :] = transposed_times(edge[...], pre)
    node_first[0:width] = transposed_times(node[...], node_grad_pre[:, columns])
    node_first[width:] = transposed_times(aggregate[...], node_grad_pre[:, columns])
    node_second[...] = transposed_times(node_hidden[...], node_grad_post[:, columns])
    edge_first[0:width] = transposed_times(node[...], placed[0:nodes]) + transposed_times(
        halo[...], placed[nodes:far_end]
    )
    edge_first[width : 2 * width] = transposed_times(node[...], placed[far_end:])
    return pack(keep_ref, send_ref, stage, sems, sums, tail)


def outgoing_kernel(node_hbm, table_hbm, out_ref, node, table, stage, sems):
    copies = [
        pltpu.make_async_copy(node_hbm, node, sems.at[0]),
        pltpu.make_async_copy(table_hbm, table, sems.at[1]),
    ]
    for copy in copies:
        copy.start()
    copies[1].wait()
    choice = send_choice(table, node.shape[0])
    copies[0].wait()
    stage[...] = dot(choice, node[...]).astype(BF16)
    copy = pltpu.make_async_copy(stage, out_ref, sems.at[0])
    copy.start()
    copy.wait()


def load(sources, targets, sems):
    copies = [
        pltpu.make_async_copy(source, target, sems.at[k])
        for k, (source, target) in enumerate(zip(sources, targets))
    ]
    for copy in copies:
        copy.start()
    return copies


def prepare_kernel(
    live_ref,
    peer_hbm,
    slot_hbm,
    recv_hbm,
    node_hbm,
    first_hbm,
    edge_hbm,
    node_first_hbm,
    second_hbm,
    part_ref,
    far_ref,
    top_ref,
    second_ref,
    node_part_ref,
    receive_ref,
    place_ref,
    peer_ref,
    slot_ref,
    recv_ref,
    node,
    first,
    edge,
    node_first,
    node_part,
    receive,
    places,
    table,
    sems,
    out_sems,
):
    nodes, width = node.shape
    copies = load(
        (
            peer_hbm,
            slot_hbm,
            recv_hbm,
            node_hbm,
            first_hbm,
            edge_hbm,
            node_first_hbm.at[pl.ds(0, width)],
            second_hbm,
            first_hbm.at[pl.ds(0, width)],
        ),
        (peer_ref, slot_ref, recv_ref, node, first, edge, node_first, second_ref, top_ref),
        sems,
    )
    own = lax.axis_index("space")
    blocks = peer_ref.shape[0]
    halo_rows = far_ref.shape[1]
    capacity = halo_rows // lax.axis_size("space")
    for k in range(3):
        copies[k].wait()
    near = []
    for b in range(blocks):
        rows = pl.ds(b * EDGE_BLOCK, EDGE_BLOCK)
        peer, slot, recv = (ref[b : b + 1, :] for ref in (peer_ref, slot_ref, recv_ref))
        mine = peer == own
        far = peer * capacity + slot
        near.append(chosen(jnp.where(mine, slot, -1), nodes))
        far_ref[rows, :] = chosen(jnp.where(mine, -1, far), halo_rows)
        received = jnp.where(b < live_ref[0], recv, -1)
        receive[rows, :] = chosen(received, nodes)
        places[0 : nodes + halo_rows, rows] = chosen_transposed(
            jnp.where(mine, slot, nodes + far), nodes + halo_rows
        )
        places[nodes + halo_rows :, rows] = chosen_transposed(received, nodes)
    out_copies = load((receive, places), (receive_ref, place_ref), out_sems)
    copies[3].wait()
    copies[4].wait()
    table[0:nodes] = dot(node[...], first[0:width]).astype(BF16)
    table[nodes:] = dot(node[...], first[width : 2 * width]).astype(BF16)
    copies[5].wait()
    count = CHUNK // EDGE_BLOCK
    for c in range(blocks // count):
        rows = pl.ds(c * CHUNK, CHUNK)
        choice = jnp.concatenate(
            [jnp.concatenate(near[c * count : (c + 1) * count], axis=0), receive[rows, :]], axis=1
        )
        part_ref[rows, :] = dot(edge[rows, :], first[2 * width :]) + dot(choice, table[...])
    copies[6].wait()
    node_part[...] = dot(node[...], node_first[...])
    out_copies.append(pltpu.make_async_copy(node_part, node_part_ref, out_sems.at[2]))
    out_copies[2].start()
    for copy in (*copies[7:], *out_copies):
        copy.wait()


def forward_kernel(
    part_ref,
    halo_ref,
    far_ref,
    top_ref,
    second_ref,
    gains_hbm,
    place_hbm,
    node_part_hbm,
    node_first_hbm,
    node_second_hbm,
    grad_nodes_hbm,
    slope_ref,
    hidden_ref,
    normed_ref,
    inv_ref,
    grad_agg_ref,
    node_gain_ref,
    aggregate_ref,
    node_hidden_ref,
    node_grad_pre_ref,
    node_grad_post_ref,
    gains,
    place,
    node_part,
    node_first,
    node_second,
    grad_nodes,
    messages,
    sems,
):
    nodes, width = node_part.shape
    copies = load(
        (
            gains_hbm,
            place_hbm.at[pl.ds(place_hbm.shape[0] - nodes, nodes)],
            node_part_hbm,
            node_first_hbm.at[pl.ds(width, width)],
            node_second_hbm,
            grad_nodes_hbm,
        ),
        (gains, place, node_part, node_first, node_second, grad_nodes),
        sems,
    )
    halo_part = dot(halo_ref[...], top_ref[...]).astype(BF16)
    for c in range(part_ref.shape[0] // CHUNK):
        rows = pl.ds(c * CHUNK, CHUNK)
        hidden, slope = activation(part_ref[rows, :] + dot(far_ref[rows, :], halo_part))
        hidden_ref[rows, :] = hidden
        slope_ref[rows, :] = slope.astype(BF16)
        normed, inv_std = normalize(dot(hidden, second_ref[...]))
        normed_ref[rows, :] = normed.astype(BF16)
        inv_ref[rows, :] = jnp.broadcast_to(inv_std, (CHUNK, inv_ref.shape[1]))
        if c == 0:
            copies[0].wait()
        messages[rows, :] = (normed * gains[0:1]).astype(BF16)
    for copy in copies[1:]:
        copy.wait()
    aggregate = dot(place[...], messages[...]).astype(BF16)
    node_hidden, node_slope = activation(node_part[...] + dot(aggregate, node_first[...]))
    node_normed, node_inv = normalize(dot(node_hidden, node_second[...]))
    grad_out = grad_nodes[...].astype(F32)
    node_gain_ref[...] = jnp.sum(grad_out * node_normed, axis=0, keepdims=True)
    grad_post = grad_normalize(grad_out, gains[1:2], node_normed, node_inv)
    grad_pre = (times_transposed(grad_post, node_second[...]) * node_slope).astype(BF16)
    grad_agg_ref[...] = times_transposed(grad_pre, node_first[...]).astype(BF16)
    aggregate_ref[...] = aggregate
    node_hidden_ref[...] = node_hidden
    node_grad_pre_ref[...] = grad_pre
    node_grad_post_ref[...] = grad_post


def backward_kernel(
    live_ref,
    grad_edges_ref,
    slope_ref,
    hidden_ref,
    normed_ref,
    inv_ref,
    grad_agg_ref,
    node_gain_ref,
    aggregate_ref,
    node_hidden_ref,
    node_grad_pre_ref,
    node_grad_post_ref,
    halo_ref,
    second_ref,
    receive_ref,
    gains_ref,
    place_hbm,
    edge_hbm,
    node_hbm,
    grad_post_ref,
    grad_pre_ref,
    placed_ref,
    keep_ref,
    send_ref,
    place,
    edge,
    node,
    node_first,
    node_second,
    edge_first,
    edge_second,
    stage,
    sems,
    load_sems,
):
    width = node.shape[1]
    half = placed_ref.shape[1]
    loads = load((place_hbm, edge_hbm, node_hbm), (place, edge, node), load_sems)
    count = CHUNK // EDGE_BLOCK
    grad_gain = jnp.zeros((1, width), F32)
    for c in range(edge.shape[0] // CHUNK):
        rows = pl.ds(c * CHUNK, CHUNK)
        live = jnp.concatenate(
            [
                jnp.where(jnp.full((EDGE_BLOCK, 1), c * count + k, INT) < live_ref[0], 1.0, 0.0)
                for k in range(count)
            ],
            axis=0,
        )
        grad_out = grad_edges_ref[rows, :].astype(F32) * live + dot(receive_ref[rows, :], grad_agg_ref[...])
        normed = normed_ref[rows, :].astype(F32)
        grad_gain += jnp.sum(grad_out * normed, axis=0, keepdims=True)
        grad_post = grad_normalize(grad_out, gains_ref[0:1], normed, inv_ref[rows, 0:1])
        grad_post_ref[rows, :] = grad_post
        grad_hidden = times_transposed(grad_post, second_ref[...])
        grad_pre_ref[rows, :] = (grad_hidden * slope_ref[rows, :].astype(F32)).astype(BF16)
    for copy in loads:
        copy.wait()
    node_gain = node_gain_ref[...]
    tail = [row[:, half * k : half * (k + 1)] for row in (grad_gain, node_gain) for k in range(2)]
    copies = weight_grads(
        slice(0, half),
        (place, edge, node, halo_ref, hidden_ref, aggregate_ref, node_hidden_ref),
        (grad_pre_ref, grad_post_ref, node_grad_pre_ref, node_grad_post_ref),
        (placed_ref, keep_ref, send_ref, stage, sems),
        (node_first, node_second, edge_first, edge_second),
        [*tail, jnp.zeros((GAIN_ROWS - 4, half), F32)],
    )
    for copy in copies:
        copy.wait()


def right_kernel(
    grad_post_ref,
    grad_pre_ref,
    hidden_ref,
    aggregate_ref,
    node_hidden_ref,
    node_grad_pre_ref,
    node_grad_post_ref,
    halo_ref,
    place_ref,
    edge_ref,
    node_ref,
    placed_ref,
    keep_ref,
    send_ref,
    node_first,
    node_second,
    edge_first,
    edge_second,
    stage,
    sems,
):
    half = placed_ref.shape[1]
    copies = weight_grads(
        slice(half, 2 * half),
        (place_ref, edge_ref, node_ref, halo_ref, hidden_ref, aggregate_ref, node_hidden_ref),
        (grad_pre_ref, grad_post_ref, node_grad_pre_ref, node_grad_post_ref),
        (placed_ref, keep_ref, send_ref, stage, sems),
        (node_first, node_second, edge_first, edge_second),
    )
    for copy in copies:
        copy.wait()


def finish_kernel(
    left_ref,
    right_ref,
    grad_pre_ref,
    node_grad_pre_ref,
    first_hbm,
    node_first_hbm,
    grad_nodes_hbm,
    grad_edges_hbm,
    back_ref,
    edge_out_ref,
    node_total_ref,
    first,
    node_first,
    grad_nodes,
    grad_edges,
    back_stage,
    edge_out,
    node_total,
    sems,
    out_sems,
    edge_sems,
):
    nodes, width = grad_nodes.shape
    loads = load(
        (first_hbm, node_first_hbm.at[pl.ds(0, width)], grad_nodes_hbm, grad_edges_hbm),
        (first, node_first, grad_nodes, grad_edges),
        sems,
    )
    devices, capacity = back_ref.shape[:2]
    far_end = left_ref.shape[0] - nodes
    placed = jnp.concatenate([left_ref[...], right_ref[...]], axis=1)
    loads[0].wait()
    back = times_transposed(placed[nodes:far_end], first[0:width])
    for k in range(devices):
        back_stage[k] = back[k * capacity : (k + 1) * capacity].astype(BF16)
    copies = load((back_stage,), (back_ref,), out_sems)
    loads[1].wait()
    loads[2].wait()
    node_total[...] = (
        grad_nodes[...].astype(F32)
        + times_transposed(node_grad_pre_ref[...], node_first[...])
        + times_transposed(placed[0:nodes], first[0:width])
        + times_transposed(placed[far_end:], first[width : 2 * width])
    )
    copies.append(pltpu.make_async_copy(node_total, node_total_ref, out_sems.at[1]))
    copies[-1].start()
    loads[3].wait()
    for c in range(grad_edges.shape[0] // CHUNK):
        rows = pl.ds(c * CHUNK, CHUNK)
        grad_edge = grad_edges[rows, :].astype(F32) + times_transposed(grad_pre_ref[rows, :], first[2 * width :])
        edge_out[rows, :] = grad_edge.astype(BF16)
        copies.append(pltpu.make_async_copy(edge_out.at[rows], edge_out_ref.at[rows], edge_sems.at[c]))
        copies[-1].start()
    for copy in copies:
        copy.wait()


def nodes_kernel(total_hbm, returned_ref, table_hbm, out_ref, total, table, stage, sems):
    loads = load((total_hbm, table_hbm), (total, table), sems)
    capacity, devices = table.shape[1:]
    returned = jnp.concatenate([returned_ref[k].astype(F32) for k in range(devices)], axis=0).astype(BF16)
    for copy in loads:
        copy.wait()
    choice = send_choice(table, total.shape[0])
    stage[...] = (total[...] + transposed_times(choice, returned)).astype(BF16)
    copy = pltpu.make_async_copy(stage, out_ref, sems.at[0])
    copy.start()
    copy.wait()


def exchange_orders(chips):
    bits = list(range(chips.bit_length() - 1))
    return bits, [*bits[1::-1], *bits[2:]]


def exchange(piece, bit, devices):
    return lax.ppermute(piece, "space", [(i, i ^ (2 << bit)) for i in range(devices)])


def half_of(step, bit, position, away):
    value = (lax.axis_index("space") >> (bit + 1)) & 1
    value = 1 - value if away else value
    low = step & ((1 << position) - 1)
    return ((step >> position) << (position + 1)) | (value << position) | low


def fold_kernel(bit, position, kept_ref, received_ref, *refs):
    sent, kept, stage, sems = refs[-4:]
    copies = []
    for away in (True, False):
        for k in range(kept.shape[0]):
            place = half_of(k, bit, position, away)
            block = (kept_ref[place].astype(F32) + received_ref[place].astype(F32)).astype(BF16)
            if away:
                stage[k] = block
                copies.append(pltpu.make_async_copy(stage.at[k], sent.at[k], sems.at[k]))
                copies[-1].start()
            else:
                kept[k] = block
    for copy in copies:
        copy.wait()


def shares_kernel(left, left_in, right, right_in, *refs):
    outs, stages, sems = refs[:5], refs[5:10], refs[10]
    sides = [a[0].astype(F32) + b[0].astype(F32) for a, b in ((left, left_in), (right, right_in))]
    rows = sides[1].shape[0]
    total = jnp.concatenate([sides[0][0:rows], sides[1]], axis=1)
    start = 0
    for out, stage in zip(outs[:4], stages):
        stage[...] = total[start : start + out.shape[0]]
        start += out.shape[0]
    gains = [sides[0][rows + k : rows + k + 1] for k in range(4)]
    stages[4][...] = jnp.concatenate(
        [jnp.concatenate(gains[0:2], axis=1), jnp.concatenate(gains[2:4], axis=1)], axis=0
    )
    for copy in load(stages, outs, sems):
        copy.wait()


VMEM, HBM, SMEM = pltpu.VMEM, pltpu.HBM, pltpu.SMEM


def call(body, name, operands, outs, scratch=(), flops=0):
    spaces = [space for _, space in operands]
    arrays = [
        array if space is SMEM else pltpu.with_memory_space_constraint(array, space) for array, space in operands
    ]
    moved = sum(a.size * a.dtype.itemsize for a, _ in operands)
    return pl.pallas_call(
        body,
        in_specs=[pl.BlockSpec(memory_space=space) for space in spaces],
        out_specs=[pl.BlockSpec(memory_space=space) for space, _, _ in outs],
        out_shape=[space(shape, dtype) for space, shape, dtype in outs],
        scratch_shapes=scratch,
        name=name,
        cost_estimate=pl.CostEstimate(flops=flops, bytes_accessed=moved, transcendentals=0),
        compiler_params=pltpu.CompilerParams(vmem_limit_bytes=24 * MIB),
    )(*arrays)


def semaphores(count):
    return pltpu.SemaphoreType.DMA((count,))


def fold_call(name, bit, position, kept, received, *before):
    shape = (kept.shape[0] // 2, *kept.shape[1:])
    return call(
        functools.partial(fold_kernel, bit, position),
        name,
        [(kept, VMEM), (received, VMEM), *((a, HBM) for a in before)],
        [(HBM, shape, BF16), (VMEM, shape, BF16)],
        [VMEM(shape, BF16), semaphores(shape[0])],
    )


def shards(
    node_feat,
    edge_feat,
    grad_nodes,
    grad_edges,
    edge_first,
    edge_second,
    node_first,
    node_second,
    gains,
    edge_peer,
    edge_slot,
    edge_recv,
    send_index,
    live_blocks,
):
    nodes, width = node_feat.shape
    edges = edge_feat.shape[0]
    devices, capacity = send_index.shape[1:]
    chips = devices // 2
    halo_rows = devices * capacity
    peer, slot, recv = (a.reshape(edges // EDGE_BLOCK, EDGE_BLOCK) for a in (edge_peer, edge_slot, edge_recv))
    other_core = [(i, i ^ 1) for i in range(devices)]
    block = width * width * 2

    send_table = jnp.swapaxes(send_index, 1, 2)
    (outgoing,) = call(
        outgoing_kernel,
        "outgoing",
        [(node_feat, HBM), (send_table, HBM)],
        [(HBM, (halo_rows, width), BF16)],
        [
            VMEM(node_feat.shape, BF16),
            VMEM(send_table.shape, INT),
            VMEM((halo_rows, width), BF16),
            semaphores(2),
        ],
    )
    halo = lax.all_to_all(
        outgoing.reshape(devices, capacity, width), "space", split_axis=0, concat_axis=0, tiled=True
    ).reshape(halo_rows, width)

    rows_bf16, nodes_f32 = (edges, width), (nodes, width)
    top_shape, place_shape = (width, width), (2 * nodes + halo_rows, edges)
    part, far, top, second, node_part, receive, place = call(
        prepare_kernel,
        "prepare",
        [
            (live_blocks, SMEM),
            *(
                (a, HBM)
                for a in (peer, slot, recv, node_feat, edge_first, edge_feat, node_first, edge_second)
            ),
        ],
        [
            (VMEM, rows_bf16, F32),
            (VMEM, (edges, halo_rows), BF16),
            (VMEM, top_shape, BF16),
            (VMEM, edge_second.shape, BF16),
            (HBM, nodes_f32, F32),
            (HBM, (edges, nodes), BF16),
            (HBM, place_shape, BF16),
        ],
        [
            VMEM(peer.shape, INT),
            VMEM(slot.shape, INT),
            VMEM(recv.shape, INT),
            VMEM(node_feat.shape, BF16),
            VMEM(edge_first.shape, BF16),
            VMEM(edge_feat.shape, BF16),
            VMEM(top_shape, BF16),
            VMEM(nodes_f32, F32),
            VMEM((edges, nodes), BF16),
            VMEM(place_shape, BF16),
            VMEM((2 * nodes, width), BF16),
            semaphores(9),
            semaphores(3),
        ],
        flops=block * (2 * edges + 3 * nodes),
    )

    nodes_bf16 = (VMEM, nodes_f32, BF16)
    kept_rows = (VMEM, rows_bf16, BF16)
    (
        slope,
        hidden,
        normed,
        inv_std,
        grad_agg,
        node_gain,
        aggregate,
        node_hidden,
        node_grad_pre,
        node_grad_post,
    ) = call(
        forward_kernel,
        "forward",
        [
            *((a, VMEM) for a in (part, halo, far, top, second)),
            *((a, HBM) for a in (gains, place, node_part, node_first, node_second, grad_nodes)),
        ],
        [
            kept_rows,
            kept_rows,
            kept_rows,
            (VMEM, (edges, 128), F32),
            nodes_bf16,
            (VMEM, (1, width), F32),
            nodes_bf16,
            nodes_bf16,
            nodes_bf16,
            nodes_bf16,
        ],
        [
            VMEM(gains.shape, F32),
            VMEM((nodes, edges), BF16),
            VMEM(nodes_f32, F32),
            VMEM(top_shape, BF16),
            VMEM(node_second.shape, BF16),
            VMEM(nodes_f32, BF16),
            VMEM(rows_bf16, BF16),
            semaphores(6),
        ],
        flops=block * (2 * edges + 6 * nodes),
    )

    half = width // 2
    weights = (node_first, node_second, edge_first, edge_second)
    share = sum(w.shape[0] // devices for w in weights)
    left_shape, right_shape = (chips, share + GAIN_ROWS, half), (chips, share, half)
    placed = (VMEM, (2 * nodes + halo_rows, half), BF16)
    halves = [VMEM((w.shape[0], half), F32) for w in weights]
    grad_post, grad_pre, left_placed, left_keep, left_send = call(
        backward_kernel,
        "backward",
        [
            (live_blocks, SMEM),
            *(
                (a, VMEM)
                for a in (
                    grad_edges,
                    slope,
                    hidden,
                    normed,
                    inv_std,
                    grad_agg,
                    node_gain,
                    aggregate,
                    node_hidden,
                    node_grad_pre,
                    node_grad_post,
                    halo,
                    second,
                    receive,
                    gains,
                )
            ),
            *((a, HBM) for a in (place, edge_feat, node_feat)),
        ],
        [kept_rows, kept_rows, placed, (VMEM, left_shape, BF16), (HBM, left_shape, BF16)],
        [
            VMEM(place_shape, BF16),
            VMEM(rows_bf16, BF16),
            VMEM(nodes_f32, BF16),
            *halves,
            VMEM(left_shape, BF16),
            semaphores(chips),
            semaphores(3),
        ],
        flops=block * (4 * edges),
    )
    left_received = lax.ppermute(left_send, "space", other_core)
    right_placed, right_keep, right_send = call(
        right_kernel,
        "right",
        [
            (a, VMEM)
            for a in (
                grad_post,
                grad_pre,
                hidden,
                aggregate,
                node_hidden,
                node_grad_pre,
                node_grad_post,
                halo,
                place,
                edge_feat,
                node_feat,
            )
        ],
        [placed, (VMEM, right_shape, BF16), (HBM, right_shape, BF16)],
        [*halves, VMEM(right_shape, BF16), semaphores(chips)],
        flops=block * (2 * edges),
    )
    right_received = lax.ppermute(right_send, "space", other_core)
    back, grad_edge_feat, node_total = call(
        finish_kernel,
        "finish",
        [
            *((a, VMEM) for a in (left_placed, right_placed, grad_pre, node_grad_pre)),
            *((a, HBM) for a in (edge_first, node_first, grad_nodes, grad_edges)),
        ],
        [
            (HBM, (devices, capacity, width), BF16),
            (HBM, rows_bf16, BF16),
            (HBM, nodes_f32, F32),
        ],
        [
            VMEM(edge_first.shape, BF16),
            VMEM(top_shape, BF16),
            VMEM(nodes_f32, BF16),
            VMEM(rows_bf16, BF16),
            VMEM((devices, capacity, width), BF16),
            VMEM(rows_bf16, BF16),
            VMEM(nodes_f32, F32),
            semaphores(4),
            semaphores(2),
            semaphores(edges // CHUNK),
        ],
        flops=block * (edges + 4 * nodes),
    )
    returned = lax.all_to_all(back, "space", split_axis=0, concat_axis=0, tiled=True)

    pieces = [("left", left_keep, left_received), ("right", right_keep, right_received)]
    for stage in range(chips.bit_length() - 1):
        for side, order in enumerate(exchange_orders(chips)):
            name, kept, received = pieces[side]
            bit = order[stage]
            position = bit - sum(earlier < bit for earlier in order[:stage])
            before = (back,) if stage == 1 and side == 0 else ()
            sent, kept = fold_call(f"{name}_fold", bit, position, kept, received, *before)
            pieces[side] = (name, kept, exchange(sent, bit, devices))

    (grad_node_feat,) = call(
        nodes_kernel,
        "nodes",
        [(node_total, HBM), (returned, VMEM), (send_table, HBM)],
        [(HBM, nodes_f32, BF16)],
        [VMEM(nodes_f32, F32), VMEM(send_table.shape, INT), VMEM(nodes_f32, BF16), semaphores(2)],
    )
    shapes = [*((w.shape[0] // devices, width) for w in weights), (2, width)]
    grad_node_first, grad_node_second, grad_edge_first, grad_edge_second, gain_totals = call(
        shares_kernel,
        "shares",
        [(a, VMEM) for _, *pair in pieces for a in pair],
        [(HBM, shape, F32) for shape in shapes],
        [*(VMEM(shape, F32) for shape in shapes), semaphores(5)],
    )
    return (
        grad_node_feat,
        grad_edge_feat,
        grad_edge_first,
        grad_edge_second,
        grad_node_first,
        grad_node_second,
        gain_totals,
    )


def solution(mesh):
    placed = (
        P(("group", "space"), None),
        P(("group", "space"), None),
        P(("group", "space"), None),
        P(("group", "space"), None),
        P(),
        P(),
        P(),
        P(),
        P(),
        P(("group", "space")),
        P(("group", "space")),
        P(("group", "space")),
        P(("group", "space"), None, None),
        P(("group", "space")),
    )
    return jax.shard_map(
        shards,
        mesh=mesh,
        in_specs=placed,
        out_specs=(
            P(("group", "space"), None),
            P(("group", "space"), None),
            P(("group", "space"), None),
            P(("group", "space"), None),
            P(("group", "space"), None),
            P(("group", "space"), None),
            P("group", None),
        ),
        check_vma=False,
    )
```

time: 74 us -> 71.4 us (0.965)
  waiting for transfers between devices: 26.9 us -> 22.6 us
  Pallas kernels: 27.3 us -> 31.4 us
  starting transfers between devices: 17.9 us -> 15.5 us
    ppermute x6, waiting for transfers between devices: 21.1 us -> 16 us  [exchange(): lax.ppermute(piece, 'space', [(i, i ^ 2 << bit) for i in range(devices)])]
    pallas_call x9 -> x14, Pallas kernels: 27.3 us -> 31.4 us  [call(): pl.pallas_call(body, in_specs=[pl.BlockSpec(memory_space=space) for space...]
    all_to_all x1, waiting for transfers between devices: 0.01 us -> 2.7 us  [shards(): lax.all_to_all(back, 'space', split_axis=0, concat_axis=0, tiled=True)]
    ppermute x6, starting transfers between devices: 5.9 us -> 3.37 us  [exchange(): lax.ppermute(piece, 'space', [(i, i ^ 2 << bit) for i in range(devices)])]
    ppermute x2, waiting for transfers between devices: 3.27 us -> 1.36 us  [the longest x1 1.36 us: shards(): right_received = lax.ppermute(right_send, 'space', other_core)]
  transfers between devices with their start and end apart: 10 -> 10, of which waited for: 8 -> 7; matrix products, arithmetic and copies ran while one was open for 0% -> 0% of each run, Pallas kernels for 11% -> 26%
where the time goes in v3:
time: 71.4 us; the launch traced here: 71.1 us
  Pallas kernels  31.4 us (44%)
  waiting for transfers between devices  22.6 us (32%)
  starting transfers between devices  15.5 us (22%)
  between operations  1.51 us (2%)
    pallas_call x14, Pallas kernels, call(): pl.pallas_call(body, in_specs=[pl.BlockSpec(memory_space=space) for space...  31.4 us
    ppermute x6, waiting for transfers between devices, exchange(): lax.ppermute(piece, 'space', [(i, i ^ 2 << bit) for i in range(devices)])  16 us
    all_to_all x1, starting transfers between devices, shards(): lax.all_to_all(outgoing.reshape(devices, capacity, width), 'space', split...  7.39 us
    all_to_all x1, starting transfers between devices, shards(): lax.all_to_all(back, 'space', split_axis=0, concat_axis=0, tiled=True)  4.01 us
    ppermute x6, starting transfers between devices, exchange(): lax.ppermute(piece, 'space', [(i, i ^ 2 << bit) for i in range(devices)])  3.37 us
    all_to_all x1, waiting for transfers between devices, shards(): lax.all_to_all(back, 'space', split_axis=0, concat_axis=0, tiled=True)  2.7 us
    all_to_all x1, waiting for transfers between devices, shards(): lax.all_to_all(outgoing.reshape(devices, capacity, width), 'space', split...  2.57 us
  transfers between devices with their start and end apart: 10, of which 7 were waited for; matrix products, arithmetic and copies ran while one was open for 0% of the time, Pallas kernels for 26%

profile of v3, /device:TPU:0, one launch (start us, length us, event | category | flops | bytes accessed | tf_op | source)
XLA Modules:
  0.0 71.1 jit_solution(16384005857909398771)
XLA Ops:
  0.6 1.8 %outgoing.1 = bf16[128,512]{1,0:T(8,128)(2,1)} custom-call(bf16[256,512]{1,0:T(8,128)(2,1)} %node_ref.1, s32[1,8,16]{2,1,0:T(8,128)} %bitcast.10), custom_call_target="tpu_custom_call" | custom-call | bytes 262656 | tf_op jit(solution)/shard_map/outgoing/pallas_call | solution.py:546
  2.5 7.4 %all-to-all-start = ((bf16[16,8,512]{2,1,0:T(8,128)(2,1)}), bf16[16,8,512]{2,1,0:T(8,128)(2,1)S(1)}, u32[]{:S(2)}, u32[]{:S(2)}) async-start(bf16[16,8,512]{2,1,0:T(8,128)(2,1)} %bitcast.9), calls=%async_computation | async-start | bytes 262144 | tf_op jit(solution)/shard_map/all_to_all | solution.py:611
  10.5 4.7 %prepare.1 = (f32[1024,512]{1,0:T(8,128)S(1)}, bf16[1024,128]{1,0:T(8,128)(2,1)S(1)}, bf16[512,512]{1,0:T(8,128)(2,1)S(1)}, bf16[512,512]{1,0:T(8,128)(2,1)S(1)}...) custom-call(s32[1]{0:T(128)S(6)} %copy.21.live_ref, s32[8,128]{1,0:T(8,128)} %bitcast.12, ...), custom_call_target="tpu_custom_call" | custom-call | flops 1476395008 | bytes 4468740 | tf_op jit(solution)/shard_map/prepare/pallas_call | solution.py:546
  15.2 2.6 %all-to-all-done = bf16[16,8,512]{2,1,0:T(8,128)(2,1)S(1)} async-done(((bf16[16,8,512]{2,1,0:T(8,128)(2,1)}), bf16[16,8,512]{2,1,0:T(8,128)(2,1)S(1)}, u32[]{:S(2)}, u32[]{:S(2)}) %all-to-all-start) | async-done | bytes 131104 | tf_op jit(solution)/shard_map/all_to_all | solution.py:611
  17.8 4.1 %forward.1 = (bf16[1024,512]{1,0:T(8,128)(2,1)S(1)}, bf16[1024,512]{1,0:T(8,128)(2,1)S(1)}, bf16[1024,512]{1,0:T(8,128)(2,1)S(1)}, f32[1024,128]{1,0:T(8,128)S(1...) custom-call(f32[1024,512]{1,0:T(8,128)S(1)} %get-tuple-element.52.pa, ...), custom_call_target="tpu_custom_call" | custom-call | flops 1879048192 | bytes 7213056 | tf_op jit(solution)/shard_map/forward/pallas_call | solution.py:546
  21.9 0.0 copy-start.3
  21.9 6.4 %backward.1 = (bf16[1024,512]{1,0:T(8,128)(2,1)S(1)}, bf16[1024,512]{1,0:T(8,128)(2,1)S(1)}, bf16[640,256]{1,0:T(8,128)(2,1)S(1)}, bf16[8,240,256]{2,1,0:T(8,128)(2,1)S(1)}, bf16[8,240,256]{2,1,0:T(8,128)(2,1)}) custom-call(s32[1]{0:T(128)S(6)} %copy.21.live_ref, bf16[1024,512]{1,0:T(8,128)(2,1)S(1)} %copy-done.2, ...), custom_call_target="tpu_custom_call" | custom-call | flops 2147483648 | bytes 9836548 | tf_op jit(solution)/shard_map/backward/pallas_call | solution.py:546
  28.4 0.1 collective-permute-start
  28.5 3.0 %right.1 = (bf16[640,256]{1,0:T(8,128)(2,1)S(1)}, bf16[8,224,256]{2,1,0:T(8,128)(2,1)S(1)}, bf16[8,224,256]{2,1,0:T(8,128)(2,1)}) custom-call(bf16[1024,512]{1,0:T(8,128)(2,1)S(1)} %get-tuple-element.70.grad_post_ref, bf16[1024,512]{1,0:T(8,128)(2,1)S(1)} %get-tuple-element.71.grad_pre_ref, bf16[1024,512]{1,0:T(8,128)(2,1)S(1)} %get-tuple-element.59.hidden_ref, ...), custom_call_target="tpu_custom_call" | custom-call | flops 1073741824 | bytes 6946816 | tf_op jit(solution)/shard_map/right/pallas_call | solution.py:546
  31.5 0.6 collective-permute-start.4
  32.1 0.9 %left_fold.3 = (bf16[4,240,256]{2,1,0:T(8,128)(2,1)}, bf16[4,240,256]{2,1,0:T(8,128)(2,1)S(1)}) custom-call(bf16[8,240,256]{2,1,0:T(8,128)(2,1)S(1)} %get-tuple-element.76.kept_ref, bf16[8,240,256]{2,1,0:T(8,128)(2,1)S(1)} %collective-permute-done.received_ref), custom_call_target="tpu_custom_call" | custom-call | bytes 1966080 | tf_op jit(solution)/shard_map/left_fold/pallas_call | solution.py:546
  33.0 0.1 collective-permute-start.1
  33.0 1.4 %collective-permute-done.4.received_ref = bf16[8,224,256]{2,1,0:T(8,128)(2,1)S(1)} collective-permute-done((bf16[8,224,256]{2,1,0:T(8,128)(2,1)}, bf16[8,224,256]{2,1,0:T(8,128)(2,1)S(1)}, u32[]{:S(2)}, u32[]{:S(2)}) %collective-permute-start.4) | collective-permute-done | bytes 917536 | tf_op jit(solution)/shard_map/ppermute | solution.py:768
  34.4 0.9 %right_fold.3 = (bf16[4,224,256]{2,1,0:T(8,128)(2,1)}, bf16[4,224,256]{2,1,0:T(8,128)(2,1)S(1)}) custom-call(bf16[8,224,256]{2,1,0:T(8,128)(2,1)S(1)} %get-tuple-element.84.kept_ref, bf16[8,224,256]{2,1,0:T(8,128)(2,1)S(1)} %collective-permute-done.4.received_ref), custom_call_target="tpu_custom_call" | custom-call | bytes 1835008 | tf_op jit(solution)/shard_map/right_fold/pallas_call | solution.py:546
  35.3 0.1 collective-permute-start.5
  35.3 3.9 %finish.1 = (bf16[16,8,512]{2,1,0:T(8,128)(2,1)}, bf16[1024,512]{1,0:T(8,128)(2,1)}, f32[256,512]{1,0:T(8,128)}) custom-call(bf16[640,256]{1,0:T(8,128)(2,1)S(1)} %get-tuple-element.69.left_ref, bf16[640,256]{1,0:T(8,128)(2,1)S(1)} %get-tuple-element.72.right_ref, bf16[1024,512]{1,0:T(8,128)(2,1)S(1)} %get-tuple-element.71.grad_pre_ref, ...), custom_call_target="tpu_custom_call" | custom-call | flops 1073741824 | bytes 5898240 | tf_op jit(solution)/shard_map/finish/pallas_call | solution.py:546
  39.3 7.1 %collective-permute-done.1.received_ref = bf16[4,240,256]{2,1,0:T(8,128)(2,1)S(1)} collective-permute-done((bf16[4,240,256]{2,1,0:T(8,128)(2,1)}, bf16[4,240,256]{2,1,0:T(8,128)(2,1)S(1)}, u32[]{:S(2)}, u32[]{:S(2)}) %collective-permute-start.1) | collective-permute-done | bytes 491552 | tf_op jit(solution)/shard_map/ppermute | solution.py:493
  46.4 0.7 %left_fold.4 = (bf16[2,240,256]{2,1,0:T(8,128)(2,1)}, bf16[2,240,256]{2,1,0:T(8,128)(2,1)S(1)}) custom-call(bf16[4,240,256]{2,1,0:T(8,128)(2,1)S(1)} %get-tuple-element.78.kept_ref, bf16[4,240,256]{2,1,0:T(8,128)(2,1)S(1)} %collective-permute-done.1.received_ref, bf16[16,8,512]{2,1,0:T(8,128)(2,1)} %get-tuple-element.74.refs_0_), custom_call_target="tpu_custom_call" | custom-call | bytes 1114112 | tf_op jit(solution)/shard_map/left_fold/pallas_call | solution.py:546
  47.1 0.1 collective-permute-start.2
  47.2 1.1 %collective-permute-done.5.received_ref = bf16[4,224,256]{2,1,0:T(8,128)(2,1)S(1)} collective-permute-done((bf16[4,224,256]{2,1,0:T(8,128)(2,1)}, bf16[4,224,256]{2,1,0:T(8,128)(2,1)S(1)}, u32[]{:S(2)}, u32[]{:S(2)}) %collective-permute-start.5) | collective-permute-done | bytes 458784 | tf_op jit(solution)/shard_map/ppermute | solution.py:493
  48.3 0.7 %right_fold.4 = (bf16[2,224,256]{2,1,0:T(8,128)(2,1)}, bf16[2,224,256]{2,1,0:T(8,128)(2,1)S(1)}) custom-call(bf16[4,224,256]{2,1,0:T(8,128)(2,1)S(1)} %get-tuple-element.86.kept_ref, bf16[4,224,256]{2,1,0:T(8,128)(2,1)S(1)} %collective-permute-done.5.received_ref), custom_call_target="tpu_custom_call" | custom-call | bytes 917504 | tf_op jit(solution)/shard_map/right_fold/pallas_call | solution.py:546
  49.1 0.1 collective-permute-start.6
  49.2 4.0 %all-to-all-start.1 = ((bf16[16,8,512]{2,1,0:T(8,128)(2,1)}), bf16[16,8,512]{2,1,0:T(8,128)(2,1)S(1)}, u32[]{:S(2)}, u32[]{:S(2)}) async-start(bf16[16,8,512]{2,1,0:T(8,128)(2,1)} %get-tuple-element.74.refs_0_), calls=%async_computation.1 | async-start | bytes 262144 | tf_op jit(solution)/shard_map/all_to_all | solution.py:795
  53.2 1.3 %collective-permute-done.2.received_ref = bf16[2,240,256]{2,1,0:T(8,128)(2,1)S(1)} collective-permute-done((bf16[2,240,256]{2,1,0:T(8,128)(2,1)}, bf16[2,240,256]{2,1,0:T(8,128)(2,1)S(1)}, u32[]{:S(2)}, u32[]{:S(2)}) %collective-permute-start.2) | collective-permute-done | bytes 245792 | tf_op jit(solution)/shard_map/ppermute | solution.py:493
  54.5 0.7 left_fold.5
  55.2 1.7 %collective-permute-start.3 = (bf16[1,240,256]{2,1,0:T(8,128)(2,1)}, bf16[1,240,256]{2,1,0:T(8,128)(2,1)S(1)}, u32[]{:S(2)}, u32[]{:S(2)}) collective-permute-start(bf16[1,240,256]{2,1,0:T(8,128)(2,1)} %get-tuple-element.83), channel_id=1, source_target_pairs={{0,8},{1,9},{2,10},{3,11},{4,12},{5,13},{6,14},{7,15},{8,0},{9,1},... | collective-permute-start | bytes 368648 | tf_op jit(solution)/shard_map/ppermute | solution.py:493
  56.8 0.7 right_fold.5
  57.5 1.4 %collective-permute-start.7 = (bf16[1,224,256]{2,1,0:T(8,128)(2,1)}, bf16[1,224,256]{2,1,0:T(8,128)(2,1)S(1)}, u32[]{:S(2)}, u32[]{:S(2)}) collective-permute-start(bf16[1,224,256]{2,1,0:T(8,128)(2,1)} %get-tuple-element.91), channel_id=1, source_target_pairs={{0,8},{1,9},{2,10},{3,11},{4,12},{5,13},{6,14},{7,15},{8,0},{9,1},... | collective-permute-start | bytes 344072 | tf_op jit(solution)/shard_map/ppermute | solution.py:493
  58.9 2.7 %all-to-all-done.1.returned_ref = bf16[16,8,512]{2,1,0:T(8,128)(2,1)S(1)} async-done(((bf16[16,8,512]{2,1,0:T(8,128)(2,1)}), bf16[16,8,512]{2,1,0:T(8,128)(2,1)S(1)}, u32[]{:S(2)}, u32[]{:S(2)}) %all-to-all-start.1) | async-done | bytes 131104 | tf_op jit(solution)/shard_map/all_to_all | solution.py:795
  61.6 2.1 %nodes.1 = bf16[256,512]{1,0:T(8,128)(2,1)} custom-call(f32[256,512]{1,0:T(8,128)} %get-tuple-element.73.total_hbm, bf16[16,8,512]{2,1,0:T(8,128)(2,1)S(1)} %all-to-all-done.1.returned_ref, s32[1,8,16]{2,1,0:T(8,128)} %bitcast.11), custom_call_target="tpu_custom_call" | custom-call | bytes 655872 | tf_op jit(solution)/shard_map/nodes/pallas_call | solution.py:546
  63.7 6.5 %collective-permute-done.7.right_in = bf16[1,224,256]{2,1,0:T(8,128)(2,1)S(1)} collective-permute-done((bf16[1,224,256]{2,1,0:T(8,128)(2,1)}, bf16[1,224,256]{2,1,0:T(8,128)(2,1)S(1)}, u32[]{:S(2)}, u32[]{:S(2)}) %collective-permute-start.7) | collective-permute-done | bytes 114720 | tf_op jit(solution)/shard_map/ppermute | solution.py:493
  70.2 0.8 %shares.1 = (f32[64,512]{1,0:T(8,128)}, f32[32,512]{1,0:T(8,128)}, f32[96,512]{1,0:T(8,128)}, f32[32,512]{1,0:T(8,128)}, f32[2,512]{1,0:T(2,128)}) custom-call(bf16[1,240,256]{2,1,0:T(8,128)(2,1)S(1)} %get-tuple-element.82.left, bf16[1,240,256]{2,1,0:T(8,128)(2,1)S(1)} %collective-permute-done.3.left_in, bf16[1,224,256]{2,1,0:T(8,128)(2,1)S(1)} %get-tuple-element.90.right, ...), custom_call_target="tpu_custom_call" | custom-call | bytes 475136 | tf_op jit(solution)/shard_map/shares/pallas_call | solution.py:546
  (14 shorter events, 0.0 us)
Async XLA Ops:
  2.5 15.3 %all-to-all-start = ((bf16[16,8,512]{2,1,0:T(8,128)(2,1)}), bf16[16,8,512]{2,1,0:T(8,128)(2,1)S(1)}, u32[]{:S(2)}, u32[]{:S(2)}) async-start(bf16[16,8,512]{2,1,0:T(8,128)(2,1)} %bitcast.9), calls=%async_computation | async-start | bytes 262144 | tf_op jit(solution)/shard_map/all_to_all | solution.py:611
  17.8 4.1 %copy-start.2 = (bf16[1024,512]{1,0:T(8,128)(2,1)S(1)}, bf16[1024,512]{1,0:T(8,128)(2,1)}, u32[]{:S(2)}) copy-start(bf16[1024,512]{1,0:T(8,128)(2,1)} %grad_edges_hbm.1) | copy-start | bytes 3145732
  17.8 4.1 %copy-start.4 = (bf16[1024,256]{1,0:T(8,128)(2,1)S(1)}, bf16[1024,256]{1,0:T(8,128)(2,1)}, u32[]{:S(2)}) copy-start(bf16[1024,256]{1,0:T(8,128)(2,1)} %get-tuple-element.68.receive_ref) | copy-start | bytes 1572868
  17.8 4.1 %copy-start.5 = (f32[2,512]{1,0:T(2,128)S(1)}, f32[2,512]{1,0:T(2,128)}, u32[]{:S(2)}) copy-start(f32[2,512]{1,0:T(2,128)} %gains_ref.1) | copy-start | bytes 12292
  21.9 6.6 %copy-start = (bf16[640,1024]{1,0:T(8,128)(2,1)S(1)}, bf16[640,1024]{1,0:T(8,128)(2,1)}, u32[]{:S(2)}) copy-start(bf16[640,1024]{1,0:T(8,128)(2,1)} %get-tuple-element.56.place_hbm.place_ref) | copy-start | bytes 3932164
  21.9 6.6 %copy-start.1 = (bf16[1024,512]{1,0:T(8,128)(2,1)S(1)}, bf16[1024,512]{1,0:T(8,128)(2,1)}, u32[]{:S(2)}) copy-start(bf16[1024,512]{1,0:T(8,128)(2,1)} %edge_ref.1) | copy-start | bytes 3145732
  21.9 6.5 %copy-start.3 = (bf16[256,512]{1,0:T(8,128)(2,1)S(1)}, bf16[256,512]{1,0:T(8,128)(2,1)}, u32[]{:S(2)}) copy-start(bf16[256,512]{1,0:T(8,128)(2,1)} %node_ref.1) | copy-start | bytes 786436
  28.4 3.7 %collective-permute-start = (bf16[8,240,256]{2,1,0:T(8,128)(2,1)}, bf16[8,240,256]{2,1,0:T(8,128)(2,1)S(1)}, u32[]{:S(2)}, u32[]{:S(2)}) collective-permute-start(bf16[8,240,256]{2,1,0:T(8,128)(2,1)} %get-tuple-element.77), channel_id=1, source_target_pairs={{0,1},{1,0},{2,3},{3,2},{4,5},{5,4},{6,7},{7,6},{8,9},{9,8},{10,11... | collective-permute-start | bytes 2949128 | tf_op jit(solution)/shard_map/ppermute | solution.py:744
  31.5 2.9 %collective-permute-start.4 = (bf16[8,224,256]{2,1,0:T(8,128)(2,1)}, bf16[8,224,256]{2,1,0:T(8,128)(2,1)S(1)}, u32[]{:S(2)}, u32[]{:S(2)}) collective-permute-start(bf16[8,224,256]{2,1,0:T(8,128)(2,1)} %get-tuple-element.85), channel_id=1, source_target_pairs={{0,1},{1,0},{2,3},{3,2},{4,5},{5,4},{6,7},{7,6},{8,9},{9,8},{10,11... | collective-permute-start | bytes 2752520 | tf_op jit(solution)/shard_map/ppermute | solution.py:768
  33.0 13.4 %collective-permute-start.1 = (bf16[4,240,256]{2,1,0:T(8,128)(2,1)}, bf16[4,240,256]{2,1,0:T(8,128)(2,1)S(1)}, u32[]{:S(2)}, u32[]{:S(2)}) collective-permute-start(bf16[4,240,256]{2,1,0:T(8,128)(2,1)} %get-tuple-element.79), channel_id=1, source_target_pairs={{0,2},{1,3},{2,0},{3,1},{4,6},{5,7},{6,4},{7,5},{8,10},{9,11},{10,... | collective-permute-start | bytes 1474568 | tf_op jit(solution)/shard_map/ppermute | solution.py:493
  35.3 13.1 %collective-permute-start.5 = (bf16[4,224,256]{2,1,0:T(8,128)(2,1)}, bf16[4,224,256]{2,1,0:T(8,128)(2,1)S(1)}, u32[]{:S(2)}, u32[]{:S(2)}) collective-permute-start(bf16[4,224,256]{2,1,0:T(8,128)(2,1)} %get-tuple-element.87), channel_id=1, source_target_pairs={{0,4},{1,5},{2,6},{3,7},{4,0},{5,1},{6,2},{7,3},{8,12},{9,13},{10,... | collective-permute-start | bytes 1376264 | tf_op jit(solution)/shard_map/ppermute | solution.py:493
  47.1 7.3 %collective-permute-start.2 = (bf16[2,240,256]{2,1,0:T(8,128)(2,1)}, bf16[2,240,256]{2,1,0:T(8,128)(2,1)S(1)}, u32[]{:S(2)}, u32[]{:S(2)}) collective-permute-start(bf16[2,240,256]{2,1,0:T(8,128)(2,1)} %get-tuple-element.81), channel_id=1, source_target_pairs={{0,4},{1,5},{2,6},{3,7},{4,0},{5,1},{6,2},{7,3},{8,12},{9,13},{10,... | collective-permute-start | bytes 737288 | tf_op jit(solution)/shard_map/ppermute | solution.py:493
  49.1 7.7 %collective-permute-start.6 = (bf16[2,224,256]{2,1,0:T(8,128)(2,1)}, bf16[2,224,256]{2,1,0:T(8,128)(2,1)S(1)}, u32[]{:S(2)}, u32[]{:S(2)}) collective-permute-start(bf16[2,224,256]{2,1,0:T(8,128)(2,1)} %get-tuple-element.89), channel_id=1, source_target_pairs={{0,2},{1,3},{2,0},{3,1},{4,6},{5,7},{6,4},{7,5},{8,10},{9,11},{10,... | collective-permute-start | bytes 688136 | tf_op jit(solution)/shard_map/ppermute | solution.py:493
  49.2 12.4 %all-to-all-start.1 = ((bf16[16,8,512]{2,1,0:T(8,128)(2,1)}), bf16[16,8,512]{2,1,0:T(8,128)(2,1)S(1)}, u32[]{:S(2)}, u32[]{:S(2)}) async-start(bf16[16,8,512]{2,1,0:T(8,128)(2,1)} %get-tuple-element.74.refs_0_), calls=%async_computation.1 | async-start | bytes 262144 | tf_op jit(solution)/shard_map/all_to_all | solution.py:795
  55.2 15.1 %collective-permute-start.3 = (bf16[1,240,256]{2,1,0:T(8,128)(2,1)}, bf16[1,240,256]{2,1,0:T(8,128)(2,1)S(1)}, u32[]{:S(2)}, u32[]{:S(2)}) collective-permute-start(bf16[1,240,256]{2,1,0:T(8,128)(2,1)} %get-tuple-element.83), channel_id=1, source_target_pairs={{0,8},{1,9},{2,10},{3,11},{4,12},{5,13},{6,14},{7,15},{8,0},{9,1},... | collective-permute-start | bytes 368648 | tf_op jit(solution)/shard_map/ppermute | solution.py:493
  57.5 12.7 %collective-permute-start.7 = (bf16[1,224,256]{2,1,0:T(8,128)(2,1)}, bf16[1,224,256]{2,1,0:T(8,128)(2,1)S(1)}, u32[]{:S(2)}, u32[]{:S(2)}) collective-permute-start(bf16[1,224,256]{2,1,0:T(8,128)(2,1)} %get-tuple-element.91), channel_id=1, source_target_pairs={{0,8},{1,9},{2,10},{3,11},{4,12},{5,13},{6,14},{7,15},{8,0},{9,1},... | collective-permute-start | bytes 344072 | tf_op jit(solution)/shard_map/ppermute | solution.py:493

commit v4 on v3

--- a/solution.py
+++ b/solution.py
@@ -486,26 +486,36 @@
 
 def exchange_orders(chips):
     bits = list(range(chips.bit_length() - 1))
-    return bits, [*bits[1::-1], *bits[2:]]
-
-
-def exchange(piece, bit, devices):
-    return lax.ppermute(piece, "space", [(i, i ^ (2 << bit)) for i in range(devices)])
-
-
-def half_of(step, bit, position, away):
-    value = (lax.axis_index("space") >> (bit + 1)) & 1
+    if len(bits) < 3:
+        return (bits, bits[::-1]), (bits, bits[::-1])
+    first, second, third, *rest = bits
+    return (
+        ([first, second, third, *rest], [second, first, third, *rest]),
+        ([first, third, second, *rest], [third, first, second, *rest]),
+    )
+
+
+def exchange(piece, bits, devices):
+    return lax.ppermute(piece, "space", [(i, i ^ (2 << bits[i % 2])) for i in range(devices)])
+
+
+def half_of(step, bits, positions, away):
+    own = lax.axis_index("space")
+    core = lax.rem(own, 2)
+    bit, position = (pair[0] + core * (pair[1] - pair[0]) for pair in (bits, positions))
+    value = lax.shift_right_logical(own, bit + 1) & 1
     value = 1 - value if away else value
-    low = step & ((1 << position) - 1)
-    return ((step >> position) << (position + 1)) | (value << position) | low
-
-
-def fold_kernel(bit, position, kept_ref, received_ref, *refs):
+    above = lax.shift_right_logical(jnp.int32(step), position)
+    low = step - lax.shift_left(above, position)
+    return lax.shift_left(above, position + 1) + lax.shift_left(value, position) + low
+
+
+def fold_kernel(bits, positions, kept_ref, received_ref, *refs):
     sent, kept, stage, sems = refs[-4:]
     copies = []
     for away in (True, False):
         for k in range(kept.shape[0]):
-            place = half_of(k, bit, position, away)
+            place = half_of(k, bits, positions, away)
             block = (kept_ref[place].astype(F32) + received_ref[place].astype(F32)).astype(BF16)
             if away:
                 stage[k] = block
@@ -559,10 +569,10 @@
     return pltpu.SemaphoreType.DMA((count,))
 
 
-def fold_call(name, bit, position, kept, received, *before):
+def fold_call(name, bits, positions, kept, received, *before):
     shape = (kept.shape[0] // 2, *kept.shape[1:])
     return call(
-        functools.partial(fold_kernel, bit, position),
+        functools.partial(fold_kernel, bits, positions),
         name,
         [(kept, VMEM), (received, VMEM), *((a, HBM) for a in before)],
         [(HBM, shape, BF16), (VMEM, shape, BF16)],
@@ -796,13 +806,15 @@
 
     pieces = [("left", left_keep, left_received), ("right", right_keep, right_received)]
     for stage in range(chips.bit_length() - 1):
-        for side, order in enumerate(exchange_orders(chips)):
+        for side, orders in enumerate(exchange_orders(chips)):
             name, kept, received = pieces[side]
-            bit = order[stage]
-            position = bit - sum(earlier < bit for earlier in order[:stage])
+            bits = [order[stage] for order in orders]
+            positions = [
+                order[stage] - sum(earlier < order[stage] for earlier in order[:stage]) for order in orders
+            ]
             before = (back,) if stage == 1 and side == 0 else ()
-            sent, kept = fold_call(f"{name}_fold", bit, position, kept, received, *before)
-            pieces[side] = (name, kept, exchange(sent, bit, devices))
+            sent, kept = fold_call(f"{name}_fold", bits, positions, kept, received, *before)
+            pieces[side] = (name, kept, exchange(sent, bits, devices))
 
     (grad_node_feat,) = call(
         nodes_kernel,

time: 71.4 us -> 66.7 us (0.934)
  waiting for transfers between devices: 22.6 us -> 14.7 us
  starting transfers between devices: 15.5 us -> 18.7 us
    ppermute x6, waiting for transfers between devices: 16 us -> 8.2 us  [exchange(): lax.ppermute(piece, 'space', [(i, i ^ 2 << bits[i % 2]) for i in range(de...]
    ppermute x6, starting transfers between devices: 3.37 us -> 5.68 us  [exchange(): lax.ppermute(piece, 'space', [(i, i ^ 2 << bits[i % 2]) for i in range(de...]
    all_to_all x1, starting transfers between devices: 4.01 us -> 4.89 us  [shards(): lax.all_to_all(back, 'space', split_axis=0, concat_axis=0, tiled=True)]
  transfers between devices with their start and end apart: 10 -> 10, of which waited for: 7 -> 6; matrix products, arithmetic and copies ran while one was open for 0% -> 0% of each run, Pallas kernels for 26% -> 28%
where the time goes in v4:
time: 66.7 us; the launch traced here: 66.3 us
  Pallas kernels  31.4 us (47%)
  starting transfers between devices  18.7 us (28%)
  waiting for transfers between devices  14.7 us (22%)
  between operations  1.52 us (2%)
    pallas_call x14, Pallas kernels, call(): pl.pallas_call(body, in_specs=[pl.BlockSpec(memory_space=space) for space...  31.4 us
    ppermute x6, waiting for transfers between devices, exchange(): lax.ppermute(piece, 'space', [(i, i ^ 2 << bits[i % 2]) for i in range(de...  8.2 us
    all_to_all x1, starting transfers between devices, shards(): lax.all_to_all(outgoing.reshape(devices, capacity, width), 'space', split...  7.39 us
    ppermute x6, starting transfers between devices, exchange(): lax.ppermute(piece, 'space', [(i, i ^ 2 << bits[i % 2]) for i in range(de...  5.68 us
    all_to_all x1, starting transfers between devices, shards(): lax.all_to_all(back, 'space', split_axis=0, concat_axis=0, tiled=True)  4.89 us
    all_to_all x1, waiting for transfers between devices, shards(): lax.all_to_all(back, 'space', split_axis=0, concat_axis=0, tiled=True)  2.57 us
    all_to_all x1, waiting for transfers between devices, shards(): lax.all_to_all(outgoing.reshape(devices, capacity, width), 'space', split...  2.57 us
    ppermute x1, waiting for transfers between devices, shards(): right_received = lax.ppermute(right_send, 'space', other_core)  1.36 us
  transfers between devices with their start and end apart: 10, of which 6 were waited for; matrix products, arithmetic and copies ran while one was open for 0% of the time, Pallas kernels for 28%

profile of v4, /device:TPU:0, one launch (start us, length us, event | category | flops | bytes accessed | tf_op | source)
XLA Modules:
  0.0 66.3 jit_solution(5006194880007545889)
XLA Ops:
  0.6 1.8 %outgoing.1 = bf16[128,512]{1,0:T(8,128)(2,1)} custom-call(bf16[256,512]{1,0:T(8,128)(2,1)} %node_ref.1, s32[1,8,16]{2,1,0:T(8,128)} %bitcast.10), custom_call_target="tpu_custom_call" | custom-call | bytes 262656 | tf_op jit(solution)/shard_map/outgoing/pallas_call | solution.py:556
  2.5 7.4 %all-to-all-start = ((bf16[16,8,512]{2,1,0:T(8,128)(2,1)}), bf16[16,8,512]{2,1,0:T(8,128)(2,1)S(1)}, u32[]{:S(2)}, u32[]{:S(2)}) async-start(bf16[16,8,512]{2,1,0:T(8,128)(2,1)} %bitcast.9), calls=%async_computation | async-start | bytes 262144 | tf_op jit(solution)/shard_map/all_to_all | solution.py:621
  10.5 4.7 %prepare.1 = (f32[1024,512]{1,0:T(8,128)S(1)}, bf16[1024,128]{1,0:T(8,128)(2,1)S(1)}, bf16[512,512]{1,0:T(8,128)(2,1)S(1)}, bf16[512,512]{1,0:T(8,128)(2,1)S(1)}...) custom-call(s32[1]{0:T(128)S(6)} %copy.21.live_ref, s32[8,128]{1,0:T(8,128)} %bitcast.12, ...), custom_call_target="tpu_custom_call" | custom-call | flops 1476395008 | bytes 4468740 | tf_op jit(solution)/shard_map/prepare/pallas_call | solution.py:556
  15.2 2.6 %all-to-all-done = bf16[16,8,512]{2,1,0:T(8,128)(2,1)S(1)} async-done(((bf16[16,8,512]{2,1,0:T(8,128)(2,1)}), bf16[16,8,512]{2,1,0:T(8,128)(2,1)S(1)}, u32[]{:S(2)}, u32[]{:S(2)}) %all-to-all-start) | async-done | bytes 131104 | tf_op jit(solution)/shard_map/all_to_all | solution.py:621
  17.8 4.1 %forward.1 = (bf16[1024,512]{1,0:T(8,128)(2,1)S(1)}, bf16[1024,512]{1,0:T(8,128)(2,1)S(1)}, bf16[1024,512]{1,0:T(8,128)(2,1)S(1)}, f32[1024,128]{1,0:T(8,128)S(1...) custom-call(f32[1024,512]{1,0:T(8,128)S(1)} %get-tuple-element.52.pa, ...), custom_call_target="tpu_custom_call" | custom-call | flops 1879048192 | bytes 7213056 | tf_op jit(solution)/shard_map/forward/pallas_call | solution.py:556
  21.9 0.0 copy-start.1
  21.9 0.0 copy-start.3
  21.9 6.4 %backward.1 = (bf16[1024,512]{1,0:T(8,128)(2,1)S(1)}, bf16[1024,512]{1,0:T(8,128)(2,1)S(1)}, bf16[640,256]{1,0:T(8,128)(2,1)S(1)}, bf16[8,240,256]{2,1,0:T(8,128)(2,1)S(1)}, bf16[8,240,256]{2,1,0:T(8,128)(2,1)}) custom-call(s32[1]{0:T(128)S(6)} %copy.21.live_ref, bf16[1024,512]{1,0:T(8,128)(2,1)S(1)} %copy-done.2, ...), custom_call_target="tpu_custom_call" | custom-call | flops 2147483648 | bytes 9836548 | tf_op jit(solution)/shard_map/backward/pallas_call | solution.py:556
  28.4 0.1 collective-permute-start
  28.5 3.0 %right.1 = (bf16[640,256]{1,0:T(8,128)(2,1)S(1)}, bf16[8,224,256]{2,1,0:T(8,128)(2,1)S(1)}, bf16[8,224,256]{2,1,0:T(8,128)(2,1)}) custom-call(bf16[1024,512]{1,0:T(8,128)(2,1)S(1)} %get-tuple-element.70.grad_post_ref, bf16[1024,512]{1,0:T(8,128)(2,1)S(1)} %get-tuple-element.71.grad_pre_ref, bf16[1024,512]{1,0:T(8,128)(2,1)S(1)} %get-tuple-element.59.hidden_ref, ...), custom_call_target="tpu_custom_call" | custom-call | flops 1073741824 | bytes 6946816 | tf_op jit(solution)/shard_map/right/pallas_call | solution.py:556
  31.5 0.6 collective-permute-start.4
  32.1 0.9 %left_fold.3 = (bf16[4,240,256]{2,1,0:T(8,128)(2,1)}, bf16[4,240,256]{2,1,0:T(8,128)(2,1)S(1)}) custom-call(bf16[8,240,256]{2,1,0:T(8,128)(2,1)S(1)} %get-tuple-element.76.kept_ref, bf16[8,240,256]{2,1,0:T(8,128)(2,1)S(1)} %collective-permute-done.received_ref), custom_call_target="tpu_custom_call" | custom-call | bytes 1966080 | tf_op jit(solution)/shard_map/left_fold/pallas_call | solution.py:556
  33.0 0.1 collective-permute-start.1
  33.0 1.4 %collective-permute-done.4.received_ref = bf16[8,224,256]{2,1,0:T(8,128)(2,1)S(1)} collective-permute-done((bf16[8,224,256]{2,1,0:T(8,128)(2,1)}, bf16[8,224,256]{2,1,0:T(8,128)(2,1)S(1)}, u32[]{:S(2)}, u32[]{:S(2)}) %collective-permute-start.4) | collective-permute-done | bytes 917536 | tf_op jit(solution)/shard_map/ppermute | solution.py:778
  34.4 0.9 %right_fold.3 = (bf16[4,224,256]{2,1,0:T(8,128)(2,1)}, bf16[4,224,256]{2,1,0:T(8,128)(2,1)S(1)}) custom-call(bf16[8,224,256]{2,1,0:T(8,128)(2,1)S(1)} %get-tuple-element.84.kept_ref, bf16[8,224,256]{2,1,0:T(8,128)(2,1)S(1)} %collective-permute-done.4.received_ref), custom_call_target="tpu_custom_call" | custom-call | bytes 1835008 | tf_op jit(solution)/shard_map/right_fold/pallas_call | solution.py:556
  35.3 0.7 %collective-permute-start.5 = (bf16[4,224,256]{2,1,0:T(8,128)(2,1)}, bf16[4,224,256]{2,1,0:T(8,128)(2,1)S(1)}, u32[]{:S(2)}, u32[]{:S(2)}) collective-permute-start(bf16[4,224,256]{2,1,0:T(8,128)(2,1)} %get-tuple-element.87), channel_id=1, source_target_pairs={{0,2},{1,9},{2,0},{3,11},{4,6},{5,13},{6,4},{7,15},{8,10},{9,1},{1... | collective-permute-start | bytes 1376264 | tf_op jit(solution)/shard_map/ppermute | solution.py:499
  36.0 3.9 %finish.1 = (bf16[16,8,512]{2,1,0:T(8,128)(2,1)}, bf16[1024,512]{1,0:T(8,128)(2,1)}, f32[256,512]{1,0:T(8,128)}) custom-call(bf16[640,256]{1,0:T(8,128)(2,1)S(1)} %get-tuple-element.69.left_ref, bf16[640,256]{1,0:T(8,128)(2,1)S(1)} %get-tuple-element.72.right_ref, bf16[1024,512]{1,0:T(8,128)(2,1)S(1)} %get-tuple-element.71.grad_pre_ref, ...), custom_call_target="tpu_custom_call" | custom-call | flops 1073741824 | bytes 5898240 | tf_op jit(solution)/shard_map/finish/pallas_call | solution.py:556
  39.9 2.1 %collective-permute-done.1.received_ref = bf16[4,240,256]{2,1,0:T(8,128)(2,1)S(1)} collective-permute-done((bf16[4,240,256]{2,1,0:T(8,128)(2,1)}, bf16[4,240,256]{2,1,0:T(8,128)(2,1)S(1)}, u32[]{:S(2)}, u32[]{:S(2)}) %collective-permute-start.1) | collective-permute-done | bytes 491552 | tf_op jit(solution)/shard_map/ppermute | solution.py:499
  42.1 0.7 %left_fold.4 = (bf16[2,240,256]{2,1,0:T(8,128)(2,1)}, bf16[2,240,256]{2,1,0:T(8,128)(2,1)S(1)}) custom-call(bf16[4,240,256]{2,1,0:T(8,128)(2,1)S(1)} %get-tuple-element.78.kept_ref, bf16[4,240,256]{2,1,0:T(8,128)(2,1)S(1)} %collective-permute-done.1.received_ref, bf16[16,8,512]{2,1,0:T(8,128)(2,1)} %get-tuple-element.74.refs_0_), custom_call_target="tpu_custom_call" | custom-call | bytes 1114112 | tf_op jit(solution)/shard_map/left_fold/pallas_call | solution.py:556
  42.8 0.1 collective-permute-start.2
  42.9 4.5 %collective-permute-done.5.received_ref = bf16[4,224,256]{2,1,0:T(8,128)(2,1)S(1)} collective-permute-done((bf16[4,224,256]{2,1,0:T(8,128)(2,1)}, bf16[4,224,256]{2,1,0:T(8,128)(2,1)S(1)}, u32[]{:S(2)}, u32[]{:S(2)}) %collective-permute-start.5) | collective-permute-done | bytes 458784 | tf_op jit(solution)/shard_map/ppermute | solution.py:499
  47.4 0.7 %right_fold.4 = (bf16[2,224,256]{2,1,0:T(8,128)(2,1)}, bf16[2,224,256]{2,1,0:T(8,128)(2,1)S(1)}) custom-call(bf16[4,224,256]{2,1,0:T(8,128)(2,1)S(1)} %get-tuple-element.86.kept_ref, bf16[4,224,256]{2,1,0:T(8,128)(2,1)S(1)} %collective-permute-done.5.received_ref), custom_call_target="tpu_custom_call" | custom-call | bytes 917504 | tf_op jit(solution)/shard_map/right_fold/pallas_call | solution.py:556
  48.1 0.4 collective-permute-start.6
  48.5 4.9 %all-to-all-start.1 = ((bf16[16,8,512]{2,1,0:T(8,128)(2,1)}), bf16[16,8,512]{2,1,0:T(8,128)(2,1)S(1)}, u32[]{:S(2)}, u32[]{:S(2)}) async-start(bf16[16,8,512]{2,1,0:T(8,128)(2,1)} %get-tuple-element.74.refs_0_), calls=%async_computation.1 | async-start | bytes 262144 | tf_op jit(solution)/shard_map/all_to_all | solution.py:805
  53.4 0.7 %left_fold.5 = (bf16[1,240,256]{2,1,0:T(8,128)(2,1)}, bf16[1,240,256]{2,1,0:T(8,128)(2,1)S(1)}) custom-call(bf16[2,240,256]{2,1,0:T(8,128)(2,1)S(1)} %get-tuple-element.80.kept_ref, bf16[2,240,256]{2,1,0:T(8,128)(2,1)S(1)} %collective-permute-done.2.received_ref), custom_call_target="tpu_custom_call" | custom-call | bytes 491520 | tf_op jit(solution)/shard_map/left_fold/pallas_call | solution.py:556
  54.1 2.9 %collective-permute-start.3 = (bf16[1,240,256]{2,1,0:T(8,128)(2,1)}, bf16[1,240,256]{2,1,0:T(8,128)(2,1)S(1)}, u32[]{:S(2)}, u32[]{:S(2)}) collective-permute-start(bf16[1,240,256]{2,1,0:T(8,128)(2,1)} %get-tuple-element.83), channel_id=1, source_target_pairs={{0,8},{1,9},{2,10},{3,11},{4,12},{5,13},{6,14},{7,15},{8,0},{9,1},... | collective-permute-start | bytes 368648 | tf_op jit(solution)/shard_map/ppermute | solution.py:499
  57.0 0.7 %right_fold.5 = (bf16[1,224,256]{2,1,0:T(8,128)(2,1)}, bf16[1,224,256]{2,1,0:T(8,128)(2,1)S(1)}) custom-call(bf16[2,224,256]{2,1,0:T(8,128)(2,1)S(1)} %get-tuple-element.88.kept_ref, bf16[2,224,256]{2,1,0:T(8,128)(2,1)S(1)} %collective-permute-done.6.received_ref), custom_call_target="tpu_custom_call" | custom-call | bytes 458752 | tf_op jit(solution)/shard_map/right_fold/pallas_call | solution.py:556
  57.7 1.5 %collective-permute-start.7 = (bf16[1,224,256]{2,1,0:T(8,128)(2,1)}, bf16[1,224,256]{2,1,0:T(8,128)(2,1)S(1)}, u32[]{:S(2)}, u32[]{:S(2)}) collective-permute-start(bf16[1,224,256]{2,1,0:T(8,128)(2,1)} %get-tuple-element.91), channel_id=1, source_target_pairs={{0,4},{1,5},{2,6},{3,7},{4,0},{5,1},{6,2},{7,3},{8,12},{9,13},{10,... | collective-permute-start | bytes 344072 | tf_op jit(solution)/shard_map/ppermute | solution.py:499
  59.3 2.6 %all-to-all-done.1.returned_ref = bf16[16,8,512]{2,1,0:T(8,128)(2,1)S(1)} async-done(((bf16[16,8,512]{2,1,0:T(8,128)(2,1)}), bf16[16,8,512]{2,1,0:T(8,128)(2,1)S(1)}, u32[]{:S(2)}, u32[]{:S(2)}) %all-to-all-start.1) | async-done | bytes 131104 | tf_op jit(solution)/shard_map/all_to_all | solution.py:805
  61.8 2.1 %nodes.1 = bf16[256,512]{1,0:T(8,128)(2,1)} custom-call(f32[256,512]{1,0:T(8,128)} %get-tuple-element.73.total_hbm, bf16[16,8,512]{2,1,0:T(8,128)(2,1)S(1)} %all-to-all-done.1.returned_ref, s32[1,8,16]{2,1,0:T(8,128)} %bitcast.11), custom_call_target="tpu_custom_call" | custom-call | bytes 655872 | tf_op jit(solution)/shard_map/nodes/pallas_call | solution.py:556
  63.9 1.6 %collective-permute-done.3.left_in = bf16[1,240,256]{2,1,0:T(8,128)(2,1)S(1)} collective-permute-done((bf16[1,240,256]{2,1,0:T(8,128)(2,1)}, bf16[1,240,256]{2,1,0:T(8,128)(2,1)S(1)}, u32[]{:S(2)}, u32[]{:S(2)}) %collective-permute-start.3) | collective-permute-done | bytes 122912 | tf_op jit(solution)/shard_map/ppermute | solution.py:499
  65.5 0.8 %shares.1 = (f32[64,512]{1,0:T(8,128)}, f32[32,512]{1,0:T(8,128)}, f32[96,512]{1,0:T(8,128)}, f32[32,512]{1,0:T(8,128)}, f32[2,512]{1,0:T(2,128)}) custom-call(bf16[1,240,256]{2,1,0:T(8,128)(2,1)S(1)} %get-tuple-element.82.left, bf16[1,240,256]{2,1,0:T(8,128)(2,1)S(1)} %collective-permute-done.3.left_in, bf16[1,224,256]{2,1,0:T(8,128)(2,1)S(1)} %get-tuple-element.90.right, ...), custom_call_target="tpu_custom_call" | custom-call | bytes 475136 | tf_op jit(solution)/shard_map/shares/pallas_call | solution.py:556
  (14 shorter events, 0.0 us)
Async XLA Ops:
  2.5 15.3 %all-to-all-start = ((bf16[16,8,512]{2,1,0:T(8,128)(2,1)}), bf16[16,8,512]{2,1,0:T(8,128)(2,1)S(1)}, u32[]{:S(2)}, u32[]{:S(2)}) async-start(bf16[16,8,512]{2,1,0:T(8,128)(2,1)} %bitcast.9), calls=%async_computation | async-start | bytes 262144 | tf_op jit(solution)/shard_map/all_to_all | solution.py:621
  17.8 4.1 %copy-start.2 = (bf16[1024,512]{1,0:T(8,128)(2,1)S(1)}, bf16[1024,512]{1,0:T(8,128)(2,1)}, u32[]{:S(2)}) copy-start(bf16[1024,512]{1,0:T(8,128)(2,1)} %grad_edges_hbm.1) | copy-start | bytes 3145732
  17.8 4.1 %copy-start.4 = (bf16[1024,256]{1,0:T(8,128)(2,1)S(1)}, bf16[1024,256]{1,0:T(8,128)(2,1)}, u32[]{:S(2)}) copy-start(bf16[1024,256]{1,0:T(8,128)(2,1)} %get-tuple-element.68.receive_ref) | copy-start | bytes 1572868
  17.8 4.1 %copy-start.5 = (f32[2,512]{1,0:T(2,128)S(1)}, f32[2,512]{1,0:T(2,128)}, u32[]{:S(2)}) copy-start(f32[2,512]{1,0:T(2,128)} %gains_ref.1) | copy-start | bytes 12292
  21.9 6.6 %copy-start = (bf16[640,1024]{1,0:T(8,128)(2,1)S(1)}, bf16[640,1024]{1,0:T(8,128)(2,1)}, u32[]{:S(2)}) copy-start(bf16[640,1024]{1,0:T(8,128)(2,1)} %get-tuple-element.56.place_hbm.place_ref) | copy-start | bytes 3932164
  21.9 6.6 %copy-start.1 = (bf16[1024,512]{1,0:T(8,128)(2,1)S(1)}, bf16[1024,512]{1,0:T(8,128)(2,1)}, u32[]{:S(2)}) copy-start(bf16[1024,512]{1,0:T(8,128)(2,1)} %edge_ref.1) | copy-start | bytes 3145732
  21.9 6.5 %copy-start.3 = (bf16[256,512]{1,0:T(8,128)(2,1)S(1)}, bf16[256,512]{1,0:T(8,128)(2,1)}, u32[]{:S(2)}) copy-start(bf16[256,512]{1,0:T(8,128)(2,1)} %node_ref.1) | copy-start | bytes 786436
  28.4 3.7 %collective-permute-start = (bf16[8,240,256]{2,1,0:T(8,128)(2,1)}, bf16[8,240,256]{2,1,0:T(8,128)(2,1)S(1)}, u32[]{:S(2)}, u32[]{:S(2)}) collective-permute-start(bf16[8,240,256]{2,1,0:T(8,128)(2,1)} %get-tuple-element.77), channel_id=1, source_target_pairs={{0,1},{1,0},{2,3},{3,2},{4,5},{5,4},{6,7},{7,6},{8,9},{9,8},{10,11... | collective-permute-start | bytes 2949128 | tf_op jit(solution)/shard_map/ppermute | solution.py:754
  31.5 2.9 %collective-permute-start.4 = (bf16[8,224,256]{2,1,0:T(8,128)(2,1)}, bf16[8,224,256]{2,1,0:T(8,128)(2,1)S(1)}, u32[]{:S(2)}, u32[]{:S(2)}) collective-permute-start(bf16[8,224,256]{2,1,0:T(8,128)(2,1)} %get-tuple-element.85), channel_id=1, source_target_pairs={{0,1},{1,0},{2,3},{3,2},{4,5},{5,4},{6,7},{7,6},{8,9},{9,8},{10,11... | collective-permute-start | bytes 2752520 | tf_op jit(solution)/shard_map/ppermute | solution.py:778
  33.0 9.1 %collective-permute-start.1 = (bf16[4,240,256]{2,1,0:T(8,128)(2,1)}, bf16[4,240,256]{2,1,0:T(8,128)(2,1)S(1)}, u32[]{:S(2)}, u32[]{:S(2)}) collective-permute-start(bf16[4,240,256]{2,1,0:T(8,128)(2,1)} %get-tuple-element.79), channel_id=1, source_target_pairs={{0,2},{1,5},{2,0},{3,7},{4,6},{5,1},{6,4},{7,3},{8,10},{9,13},{10,... | collective-permute-start | bytes 1474568 | tf_op jit(solution)/shard_map/ppermute | solution.py:499
  35.3 12.1 %collective-permute-start.5 = (bf16[4,224,256]{2,1,0:T(8,128)(2,1)}, bf16[4,224,256]{2,1,0:T(8,128)(2,1)S(1)}, u32[]{:S(2)}, u32[]{:S(2)}) collective-permute-start(bf16[4,224,256]{2,1,0:T(8,128)(2,1)} %get-tuple-element.87), channel_id=1, source_target_pairs={{0,2},{1,9},{2,0},{3,11},{4,6},{5,13},{6,4},{7,15},{8,10},{9,1},{1... | collective-permute-start | bytes 1376264 | tf_op jit(solution)/shard_map/ppermute | solution.py:499
  42.8 10.6 %collective-permute-start.2 = (bf16[2,240,256]{2,1,0:T(8,128)(2,1)}, bf16[2,240,256]{2,1,0:T(8,128)(2,1)S(1)}, u32[]{:S(2)}, u32[]{:S(2)}) collective-permute-start(bf16[2,240,256]{2,1,0:T(8,128)(2,1)} %get-tuple-element.81), channel_id=1, source_target_pairs={{0,4},{1,3},{2,6},{3,1},{4,0},{5,7},{6,2},{7,5},{8,12},{9,11},{10,... | collective-permute-start | bytes 737288 | tf_op jit(solution)/shard_map/ppermute | solution.py:499
  48.1 8.9 %collective-permute-start.6 = (bf16[2,224,256]{2,1,0:T(8,128)(2,1)}, bf16[2,224,256]{2,1,0:T(8,128)(2,1)S(1)}, u32[]{:S(2)}, u32[]{:S(2)}) collective-permute-start(bf16[2,224,256]{2,1,0:T(8,128)(2,1)} %get-tuple-element.89), channel_id=1, source_target_pairs={{0,8},{1,3},{2,10},{3,1},{4,12},{5,7},{6,14},{7,5},{8,0},{9,11},{1... | collective-permute-start | bytes 688136 | tf_op jit(solution)/shard_map/ppermute | solution.py:499
  48.5 13.3 %all-to-all-start.1 = ((bf16[16,8,512]{2,1,0:T(8,128)(2,1)}), bf16[16,8,512]{2,1,0:T(8,128)(2,1)S(1)}, u32[]{:S(2)}, u32[]{:S(2)}) async-start(bf16[16,8,512]{2,1,0:T(8,128)(2,1)} %get-tuple-element.74.refs_0_), calls=%async_computation.1 | async-start | bytes 262144 | tf_op jit(solution)/shard_map/all_to_all | solution.py:805
  54.1 11.4 %collective-permute-start.3 = (bf16[1,240,256]{2,1,0:T(8,128)(2,1)}, bf16[1,240,256]{2,1,0:T(8,128)(2,1)S(1)}, u32[]{:S(2)}, u32[]{:S(2)}) collective-permute-start(bf16[1,240,256]{2,1,0:T(8,128)(2,1)} %get-tuple-element.83), channel_id=1, source_target_pairs={{0,8},{1,9},{2,10},{3,11},{4,12},{5,13},{6,14},{7,15},{8,0},{9,1},... | collective-permute-start | bytes 368648 | tf_op jit(solution)/shard_map/ppermute | solution.py:499
  57.7 6.2 %collective-permute-start.7 = (bf16[1,224,256]{2,1,0:T(8,128)(2,1)}, bf16[1,224,256]{2,1,0:T(8,128)(2,1)S(1)}, u32[]{:S(2)}, u32[]{:S(2)}) collective-permute-start(bf16[1,224,256]{2,1,0:T(8,128)(2,1)} %get-tuple-element.91), channel_id=1, source_target_pairs={{0,4},{1,5},{2,6},{3,7},{4,0},{5,1},{6,2},{7,3},{8,12},{9,13},{10,... | collective-permute-start | bytes 344072 | tf_op jit(solution)/shard_map/ppermute | solution.py:499

commit v5 on v4

--- a/solution.py
+++ b/solution.py
@@ -9,7 +9,7 @@
 
 EDGE_BLOCK = 128
 CHUNK = 512
-GAIN_ROWS = 16
+GAIN_ROWS = 8
 EPS = 1e-05
 BF16 = jnp.bfloat16
 F32 = jnp.float32
@@ -96,28 +96,6 @@
             else:
                 keep_ref[k] = rows
     return copies
-
-
-def weight_grads(columns, acts, grads, outs, sums, tail=()):
-    place, edge, node, halo, hidden, aggregate, node_hidden = acts
-    grad_pre, grad_post, node_grad_pre, node_grad_post = grads
-    placed_ref, keep_ref, send_ref, stage, sems = outs
-    node_first, node_second, edge_first, edge_second = sums
-    nodes, width = node.shape
-    far_end = place.shape[0] - nodes
-    pre = grad_pre[:, columns]
-    placed = dot(place[...], pre).astype(BF16)
-    placed_ref[...] = placed
-    edge_second[...] = transposed_times(hidden[...], grad_post[:, columns])
-    edge_first[2 * width :] = transposed_times(edge[...], pre)
-    node_first[0:width] = transposed_times(node[...], node_grad_pre[:, columns])
-    node_first[width:] = transposed_times(aggregate[...], node_grad_pre[:, columns])
-    node_second[...] = transposed_times(node_hidden[...], node_grad_post[:, columns])
-    edge_first[0:width] = transposed_times(node[...], placed[0:nodes]) + transposed_times(
-        halo[...], placed[nodes:far_end]
-    )
-    edge_first[width : 2 * width] = transposed_times(node[...], placed[far_end:])
-    return pack(keep_ref, send_ref, stage, sems, sums, tail)
 
 
 def outgoing_kernel(node_hbm, table_hbm, out_ref, node, table, stage, sems):
@@ -309,7 +287,6 @@
 def backward_kernel(
     live_ref,
     grad_edges_ref,
-    slope_ref,
     hidden_ref,
     normed_ref,
     inv_ref,
@@ -319,35 +296,25 @@
     node_hidden_ref,
     node_grad_pre_ref,
     node_grad_post_ref,
-    halo_ref,
-    second_ref,
     receive_ref,
     gains_ref,
-    place_hbm,
-    edge_hbm,
     node_hbm,
     grad_post_ref,
-    grad_pre_ref,
-    placed_ref,
     keep_ref,
     send_ref,
-    place,
-    edge,
     node,
     node_first,
     node_second,
-    edge_first,
     edge_second,
     stage,
     sems,
-    load_sems,
+    load_sem,
 ):
     width = node.shape[1]
-    half = placed_ref.shape[1]
-    loads = load((place_hbm, edge_hbm, node_hbm), (place, edge, node), load_sems)
+    loads = load((node_hbm,), (node,), load_sem)
     count = CHUNK // EDGE_BLOCK
     grad_gain = jnp.zeros((1, width), F32)
-    for c in range(edge.shape[0] // CHUNK):
+    for c in range(grad_edges_ref.shape[0] // CHUNK):
         rows = pl.ds(c * CHUNK, CHUNK)
         live = jnp.concatenate(
             [
@@ -359,63 +326,54 @@
         grad_out = grad_edges_ref[rows, :].astype(F32) * live + dot(receive_ref[rows, :], grad_agg_ref[...])
         normed = normed_ref[rows, :].astype(F32)
         grad_gain += jnp.sum(grad_out * normed, axis=0, keepdims=True)
-        grad_post = grad_normalize(grad_out, gains_ref[0:1], normed, inv_ref[rows, 0:1])
-        grad_post_ref[rows, :] = grad_post
-        grad_hidden = times_transposed(grad_post, second_ref[...])
-        grad_pre_ref[rows, :] = (grad_hidden * slope_ref[rows, :].astype(F32)).astype(BF16)
+        grad_post_ref[rows, :] = grad_normalize(grad_out, gains_ref[0:1], normed, inv_ref[rows, 0:1])
+    grad_pre = node_grad_pre_ref[...]
+    node_second[...] = transposed_times(node_hidden_ref[...], node_grad_post_ref[...])
+    node_first[width:] = transposed_times(aggregate_ref[...], grad_pre)
     for copy in loads:
         copy.wait()
-    node_gain = node_gain_ref[...]
-    tail = [row[:, half * k : half * (k + 1)] for row in (grad_gain, node_gain) for k in range(2)]
-    copies = weight_grads(
-        slice(0, half),
-        (place, edge, node, halo_ref, hidden_ref, aggregate_ref, node_hidden_ref),
-        (grad_pre_ref, grad_post_ref, node_grad_pre_ref, node_grad_post_ref),
-        (placed_ref, keep_ref, send_ref, stage, sems),
-        (node_first, node_second, edge_first, edge_second),
-        [*tail, jnp.zeros((GAIN_ROWS - 4, half), F32)],
-    )
-    for copy in copies:
+    node_first[0:width] = transposed_times(node[...], grad_pre)
+    edge_second[...] = transposed_times(hidden_ref[...], grad_post_ref[...])
+    tail = (grad_gain, node_gain_ref[...], jnp.zeros((GAIN_ROWS - 2, width), F32))
+    for copy in pack(keep_ref, send_ref, stage, sems, (node_first, node_second, edge_second), tail):
         copy.wait()
 
 
 def right_kernel(
     grad_post_ref,
-    grad_pre_ref,
-    hidden_ref,
-    aggregate_ref,
-    node_hidden_ref,
-    node_grad_pre_ref,
-    node_grad_post_ref,
+    slope_ref,
+    second_ref,
     halo_ref,
     place_ref,
     edge_ref,
     node_ref,
+    grad_pre_ref,
     placed_ref,
     keep_ref,
     send_ref,
-    node_first,
-    node_second,
-    edge_first,
-    edge_second,
+    first,
     stage,
     sems,
 ):
-    half = placed_ref.shape[1]
-    copies = weight_grads(
-        slice(half, 2 * half),
-        (place_ref, edge_ref, node_ref, halo_ref, hidden_ref, aggregate_ref, node_hidden_ref),
-        (grad_pre_ref, grad_post_ref, node_grad_pre_ref, node_grad_post_ref),
-        (placed_ref, keep_ref, send_ref, stage, sems),
-        (node_first, node_second, edge_first, edge_second),
-    )
-    for copy in copies:
+    nodes, width = node_ref.shape
+    far_end = place_ref.shape[0] - nodes
+    for c in range(edge_ref.shape[0] // CHUNK):
+        rows = pl.ds(c * CHUNK, CHUNK)
+        grad_hidden = times_transposed(grad_post_ref[rows, :], second_ref[...])
+        grad_pre_ref[rows, :] = (grad_hidden * slope_ref[rows, :].astype(F32)).astype(BF16)
+    placed = dot(place_ref[...], grad_pre_ref[...]).astype(BF16)
+    placed_ref[...] = placed
+    first[2 * width :] = transposed_times(edge_ref[...], grad_pre_ref[...])
+    first[0:width] = transposed_times(node_ref[...], placed[0:nodes]) + transposed_times(
+        halo_ref[...], placed[nodes:far_end]
+    )
+    first[width : 2 * width] = transposed_times(node_ref[...], placed[far_end:])
+    for copy in pack(keep_ref, send_ref, stage, sems, (first,), ()):
         copy.wait()
 
 
 def finish_kernel(
-    left_ref,
-    right_ref,
+    placed_ref,
     grad_pre_ref,
     node_grad_pre_ref,
     first_hbm,
@@ -443,8 +401,8 @@
         sems,
     )
     devices, capacity = back_ref.shape[:2]
-    far_end = left_ref.shape[0] - nodes
-    placed = jnp.concatenate([left_ref[...], right_ref[...]], axis=1)
+    far_end = placed_ref.shape[0] - nodes
+    placed = placed_ref[...]
     loads[0].wait()
     back = times_transposed(placed[nodes:far_end], first[0:width])
     for k in range(devices):
@@ -490,8 +448,8 @@
         return (bits, bits[::-1]), (bits, bits[::-1])
     first, second, third, *rest = bits
     return (
-        ([first, second, third, *rest], [second, first, third, *rest]),
-        ([first, third, second, *rest], [third, first, second, *rest]),
+        ([first, second, third, *rest], [second, third, first, *rest]),
+        ([first, second, third, *rest], [third, first, second, *rest]),
     )
 
 
@@ -527,19 +485,13 @@
         copy.wait()
 
 
-def shares_kernel(left, left_in, right, right_in, *refs):
-    outs, stages, sems = refs[:5], refs[5:10], refs[10]
-    sides = [a[0].astype(F32) + b[0].astype(F32) for a, b in ((left, left_in), (right, right_in))]
-    rows = sides[1].shape[0]
-    total = jnp.concatenate([sides[0][0:rows], sides[1]], axis=1)
+def shares_kernel(count, kept, received, *refs):
+    outs, stages, sems = refs[-2 * count - 1 : -count - 1], refs[-count - 1 : -1], refs[-1]
+    total = kept[0].astype(F32) + received[0].astype(F32)
     start = 0
-    for out, stage in zip(outs[:4], stages):
-        stage[...] = total[start : start + out.shape[0]]
-        start += out.shape[0]
-    gains = [sides[0][rows + k : rows + k + 1] for k in range(4)]
-    stages[4][...] = jnp.concatenate(
-        [jnp.concatenate(gains[0:2], axis=1), jnp.concatenate(gains[2:4], axis=1)], axis=0
-    )
+    for stage in stages:
+        stage[...] = total[start : start + stage.shape[0]]
+        start += stage.shape[0]
     for copy in load(stages, outs, sems):
         copy.wait()
 
@@ -577,6 +529,16 @@
         [(kept, VMEM), (received, VMEM), *((a, HBM) for a in before)],
         [(HBM, shape, BF16), (VMEM, shape, BF16)],
         [VMEM(shape, BF16), semaphores(shape[0])],
+    )
+
+
+def share_call(name, kept, received, shapes, *before):
+    return call(
+        functools.partial(shares_kernel, len(shapes)),
+        f"{name}_shares",
+        [(kept, VMEM), (received, VMEM), *((a, HBM) for a in before)],
+        [(HBM, shape, F32) for shape in shapes],
+        [*(VMEM(shape, F32) for shape in shapes), semaphores(len(shapes))],
     )
 
 
@@ -706,13 +668,13 @@
         flops=block * (2 * edges + 6 * nodes),
     )
 
-    half = width // 2
-    weights = (node_first, node_second, edge_first, edge_second)
-    share = sum(w.shape[0] // devices for w in weights)
-    left_shape, right_shape = (chips, share + GAIN_ROWS, half), (chips, share, half)
-    placed = (VMEM, (2 * nodes + halo_rows, half), BF16)
-    halves = [VMEM((w.shape[0], half), F32) for w in weights]
-    grad_post, grad_pre, left_placed, left_keep, left_send = call(
+    node_shares = [(w.shape[0] // devices, width) for w in (node_first, node_second)]
+    edge_shares = [(w.shape[0] // devices, width) for w in (edge_first, edge_second)]
+    left_shares = [*node_shares, edge_shares[1], (2, width)]
+    left_shape = (chips, sum(rows for rows, _ in left_shares[:3]) + GAIN_ROWS, width)
+    right_shape = (chips, edge_shares[0][0], width)
+    placed_shape = (2 * nodes + halo_rows, width)
+    grad_post, left_keep, left_send = call(
         backward_kernel,
         "backward",
         [
@@ -721,7 +683,6 @@
                 (a, VMEM)
                 for a in (
                     grad_edges,
-                    slope,
                     hidden,
                     normed,
                     inv_std,
@@ -731,56 +692,39 @@
                     node_hidden,
                     node_grad_pre,
                     node_grad_post,
-                    halo,
-                    second,
                     receive,
                     gains,
                 )
             ),
-            *((a, HBM) for a in (place, edge_feat, node_feat)),
-        ],
-        [kept_rows, kept_rows, placed, (VMEM, left_shape, BF16), (HBM, left_shape, BF16)],
-        [
-            VMEM(place_shape, BF16),
-            VMEM(rows_bf16, BF16),
+            (node_feat, HBM),
+        ],
+        [kept_rows, (VMEM, left_shape, BF16), (HBM, left_shape, BF16)],
+        [
             VMEM(nodes_f32, BF16),
-            *halves,
+            VMEM(node_first.shape, F32),
+            VMEM(node_second.shape, F32),
+            VMEM(edge_second.shape, F32),
             VMEM(left_shape, BF16),
             semaphores(chips),
-            semaphores(3),
-        ],
-        flops=block * (4 * edges),
+            semaphores(1),
+        ],
+        flops=block * (2 * edges + 3 * nodes),
     )
     left_received = lax.ppermute(left_send, "space", other_core)
-    right_placed, right_keep, right_send = call(
+    grad_pre, placed, right_keep, right_send = call(
         right_kernel,
         "right",
-        [
-            (a, VMEM)
-            for a in (
-                grad_post,
-                grad_pre,
-                hidden,
-                aggregate,
-                node_hidden,
-                node_grad_pre,
-                node_grad_post,
-                halo,
-                place,
-                edge_feat,
-                node_feat,
-            )
-        ],
-        [placed, (VMEM, right_shape, BF16), (HBM, right_shape, BF16)],
-        [*halves, VMEM(right_shape, BF16), semaphores(chips)],
-        flops=block * (2 * edges),
+        [(a, VMEM) for a in (grad_post, slope, second, halo, place, edge_feat, node_feat)],
+        [kept_rows, (VMEM, placed_shape, BF16), (VMEM, right_shape, BF16), (HBM, right_shape, BF16)],
+        [VMEM(edge_first.shape, F32), VMEM(right_shape, BF16), semaphores(chips)],
+        flops=block * (4 * edges),
     )
     right_received = lax.ppermute(right_send, "space", other_core)
     back, grad_edge_feat, node_total = call(
         finish_kernel,
         "finish",
         [
-            *((a, VMEM) for a in (left_placed, right_placed, grad_pre, node_grad_pre)),
+            *((a, VMEM) for a in (placed, grad_pre, node_grad_pre)),
             *((a, HBM) for a in (edge_first, node_first, grad_nodes, grad_edges)),
         ],
         [
@@ -823,14 +767,8 @@
         [(HBM, nodes_f32, BF16)],
         [VMEM(nodes_f32, F32), VMEM(send_table.shape, INT), VMEM(nodes_f32, BF16), semaphores(2)],
     )
-    shapes = [*((w.shape[0] // devices, width) for w in weights), (2, width)]
-    grad_node_first, grad_node_second, grad_edge_first, grad_edge_second, gain_totals = call(
-        shares_kernel,
-        "shares",
-        [(a, VMEM) for _, *pair in pieces for a in pair],
-        [(HBM, shape, F32) for shape in shapes],
-        [*(VMEM(shape, F32) for shape in shapes), semaphores(5)],
-    )
+    grad_node_first, grad_node_second, grad_edge_second, gain_totals = share_call(*pieces[0], left_shares)
+    (grad_edge_first,) = share_call(*pieces[1], edge_shares[:1], gain_totals)
     return (
         grad_node_feat,
         grad_edge_feat,

time: 66.7 us -> 62.9 us (0.943)
  starting transfers between devices: 18.7 us -> 16 us
  Pallas kernels: 31.4 us -> 30 us
    ppermute x6, starting transfers between devices: 5.68 us -> 3.89 us  [exchange(): lax.ppermute(piece, 'space', [(i, i ^ 2 << bits[i % 2]) for i in range(de...]
    pallas_call x14 -> x15, Pallas kernels: 31.4 us -> 30 us  [call(): pl.pallas_call(body, in_specs=[pl.BlockSpec(memory_space=space) for space...]
    all_to_all x1, starting transfers between devices: 4.89 us -> 4.02 us  [shards(): lax.all_to_all(back, 'space', split_axis=0, concat_axis=0, tiled=True)]
  transfers between devices with their start and end apart: 10 -> 10, of which waited for: 6 -> 8; matrix products, arithmetic and copies ran while one was open for 0% -> 0% of each run, Pallas kernels for 28% -> 31%
where the time goes in v5:
time: 62.9 us; the launch traced here: 62.5 us
  Pallas kernels  30 us (48%)
  starting transfers between devices  16 us (25%)
  waiting for transfers between devices  14.9 us (24%)
  between operations  1.53 us (2%)
    pallas_call x15, Pallas kernels, call(): pl.pallas_call(body, in_specs=[pl.BlockSpec(memory_space=space) for space...  30 us
    ppermute x6, waiting for transfers between devices, exchange(): lax.ppermute(piece, 'space', [(i, i ^ 2 << bits[i % 2]) for i in range(de...  8.44 us
    all_to_all x1, starting transfers between devices, shards(): lax.all_to_all(outgoing.reshape(devices, capacity, width), 'space', split...  7.39 us
    all_to_all x1, starting transfers between devices, shards(): lax.all_to_all(back, 'space', split_axis=0, concat_axis=0, tiled=True)  4.02 us
    ppermute x6, starting transfers between devices, exchange(): lax.ppermute(piece, 'space', [(i, i ^ 2 << bits[i % 2]) for i in range(de...  3.89 us
    all_to_all x1, waiting for transfers between devices, shards(): lax.all_to_all(back, 'space', split_axis=0, concat_axis=0, tiled=True)  2.8 us
    all_to_all x1, waiting for transfers between devices, shards(): lax.all_to_all(outgoing.reshape(devices, capacity, width), 'space', split...  2.57 us
  transfers between devices with their start and end apart: 10, of which 8 were waited for; matrix products, arithmetic and copies ran while one was open for 0% of the time, Pallas kernels for 31%

profile of v5, /device:TPU:0, one launch (start us, length us, event | category | flops | bytes accessed | tf_op | source)
XLA Modules:
  0.0 62.5 jit_solution(16483616760887701123)
XLA Ops:
  0.6 1.8 %outgoing.1 = bf16[128,512]{1,0:T(8,128)(2,1)} custom-call(bf16[256,512]{1,0:T(8,128)(2,1)} %node_ref.1, s32[1,8,16]{2,1,0:T(8,128)} %bitcast.9), custom_call_target="tpu_custom_call" | custom-call | bytes 262656 | tf_op jit(solution)/shard_map/outgoing/pallas_call | solution.py:508
  2.5 7.4 %all-to-all-start = ((bf16[16,8,512]{2,1,0:T(8,128)(2,1)}), bf16[16,8,512]{2,1,0:T(8,128)(2,1)S(1)}, u32[]{:S(2)}, u32[]{:S(2)}) async-start(bf16[16,8,512]{2,1,0:T(8,128)(2,1)} %bitcast.8), calls=%async_computation | async-start | bytes 262144 | tf_op jit(solution)/shard_map/all_to_all | solution.py:583
  10.5 4.7 %prepare.1 = (f32[1024,512]{1,0:T(8,128)S(1)}, bf16[1024,128]{1,0:T(8,128)(2,1)S(1)}, bf16[512,512]{1,0:T(8,128)(2,1)S(1)}, bf16[512,512]{1,0:T(8,128)(2,1)S(1)}...) custom-call(s32[1]{0:T(128)S(6)} %copy.21.live_ref, s32[8,128]{1,0:T(8,128)} %bitcast.11, ...), custom_call_target="tpu_custom_call" | custom-call | flops 1476395008 | bytes 4468740 | tf_op jit(solution)/shard_map/prepare/pallas_call | solution.py:508
  15.2 2.6 %all-to-all-done = bf16[16,8,512]{2,1,0:T(8,128)(2,1)S(1)} async-done(((bf16[16,8,512]{2,1,0:T(8,128)(2,1)}), bf16[16,8,512]{2,1,0:T(8,128)(2,1)S(1)}, u32[]{:S(2)}, u32[]{:S(2)}) %all-to-all-start) | async-done | bytes 131104 | tf_op jit(solution)/shard_map/all_to_all | solution.py:583
  17.8 4.1 %forward.1 = (bf16[1024,512]{1,0:T(8,128)(2,1)S(1)}, bf16[1024,512]{1,0:T(8,128)(2,1)S(1)}, bf16[1024,512]{1,0:T(8,128)(2,1)S(1)}, f32[1024,128]{1,0:T(8,128)S(1...) custom-call(f32[1024,512]{1,0:T(8,128)S(1)} %get-tuple-element.50.pa, ...), custom_call_target="tpu_custom_call" | custom-call | flops 1879048192 | bytes 7213056 | tf_op jit(solution)/shard_map/forward/pallas_call | solution.py:508
  21.9 3.9 %backward.1 = (bf16[1024,512]{1,0:T(8,128)(2,1)S(1)}, bf16[8,136,512]{2,1,0:T(8,128)(2,1)S(1)}, bf16[8,136,512]{2,1,0:T(8,128)(2,1)}) custom-call(s32[1]{0:T(128)S(6)} %copy.21.live_ref, bf16[1024,512]{1,0:T(8,128)(2,1)S(1)} %copy-done, bf16[1024,512]{1,0:T(8,128)(2,1)S(1)} %get-tuple-element.56.hidden_ref, ...), custom_call_target="tpu_custom_call" | custom-call | flops 1476395008 | bytes 5773316 | tf_op jit(solution)/shard_map/backward/pallas_call | solution.py:508
  25.9 0.1 collective-permute-start.4
  26.0 3.4 %right.1 = (bf16[1024,512]{1,0:T(8,128)(2,1)S(1)}, bf16[640,512]{1,0:T(8,128)(2,1)S(1)}, bf16[8,96,512]{2,1,0:T(8,128)(2,1)S(1)}, bf16[8,96,512]{2,1,0:T(8,128)(2,1)}) custom-call(bf16[1024,512]{1,0:T(8,128)(2,1)S(1)} %get-tuple-element.66.grad_post_ref, bf16[1024,512]{1,0:T(8,128)(2,1)S(1)} %get-tuple-element.67.slope_ref, ...), custom_call_target="tpu_custom_call" | custom-call | flops 2147483648 | bytes 5373952 | tf_op jit(solution)/shard_map/right/pallas_call | solution.py:508
  29.4 0.6 %collective-permute-start = (bf16[8,96,512]{2,1,0:T(8,128)(2,1)}, bf16[8,96,512]{2,1,0:T(8,128)(2,1)S(1)}, u32[]{:S(2)}, u32[]{:S(2)}) collective-permute-start(bf16[8,96,512]{2,1,0:T(8,128)(2,1)} %get-tuple-element.74), channel_id=1, source_target_pairs={{0,1},{1,0},{2,3},{3,2},{4,5},{5,4},{6,7},{7,6},{8,9},{9,8},{10,11... | collective-permute-start | bytes 2359304 | tf_op jit(solution)/shard_map/ppermute | solution.py:722
  30.0 0.9 %left_fold.3 = (bf16[4,136,512]{2,1,0:T(8,128)(2,1)}, bf16[4,136,512]{2,1,0:T(8,128)(2,1)S(1)}) custom-call(bf16[8,136,512]{2,1,0:T(8,128)(2,1)S(1)} %get-tuple-element.81.kept_ref, bf16[8,136,512]{2,1,0:T(8,128)(2,1)S(1)} %collective-permute-done.4.received_ref), custom_call_target="tpu_custom_call" | custom-call | bytes 2228224 | tf_op jit(solution)/shard_map/left_fold/pallas_call | solution.py:508
  30.9 0.1 collective-permute-start.5
  31.0 1.1 %collective-permute-done.received_ref = bf16[8,96,512]{2,1,0:T(8,128)(2,1)S(1)} collective-permute-done((bf16[8,96,512]{2,1,0:T(8,128)(2,1)}, bf16[8,96,512]{2,1,0:T(8,128)(2,1)S(1)}, u32[]{:S(2)}, u32[]{:S(2)}) %collective-permute-start) | collective-permute-done | bytes 786464 | tf_op jit(solution)/shard_map/ppermute | solution.py:722
  32.1 0.8 %right_fold.3 = (bf16[4,96,512]{2,1,0:T(8,128)(2,1)}, bf16[4,96,512]{2,1,0:T(8,128)(2,1)S(1)}) custom-call(bf16[8,96,512]{2,1,0:T(8,128)(2,1)S(1)} %get-tuple-element.73.kept_ref, bf16[8,96,512]{2,1,0:T(8,128)(2,1)S(1)} %collective-permute-done.received_ref), custom_call_target="tpu_custom_call" | custom-call | bytes 1572864 | tf_op jit(solution)/shard_map/right_fold/pallas_call | solution.py:508
  33.0 0.9 %collective-permute-start.1 = (bf16[4,96,512]{2,1,0:T(8,128)(2,1)}, bf16[4,96,512]{2,1,0:T(8,128)(2,1)S(1)}, u32[]{:S(2)}, u32[]{:S(2)}) collective-permute-start(bf16[4,96,512]{2,1,0:T(8,128)(2,1)} %get-tuple-element.76), channel_id=1, source_target_pairs={{0,2},{1,9},{2,0},{3,11},{4,6},{5,13},{6,4},{7,15},{8,10},{9,1},{1... | collective-permute-start | bytes 1179656 | tf_op jit(solution)/shard_map/ppermute | solution.py:457
  33.9 3.9 %finish.1 = (bf16[16,8,512]{2,1,0:T(8,128)(2,1)}, bf16[1024,512]{1,0:T(8,128)(2,1)}, f32[256,512]{1,0:T(8,128)}) custom-call(bf16[640,512]{1,0:T(8,128)(2,1)S(1)} %get-tuple-element.68.placed_ref, bf16[1024,512]{1,0:T(8,128)(2,1)S(1)} %get-tuple-element.69.grad_pre_ref, bf16[256,512]{1,0:T(8,128)(2,1)S(1)} %get-tuple-element.63.node_grad_pre_ref, ...), custom_call_target="tpu_custom_call" | custom-call | flops 1073741824 | bytes 5898240 | tf_op jit(solution)/shard_map/finish/pallas_call | solution.py:508
  37.8 2.9 %collective-permute-done.5.received_ref = bf16[4,136,512]{2,1,0:T(8,128)(2,1)S(1)} collective-permute-done((bf16[4,136,512]{2,1,0:T(8,128)(2,1)}, bf16[4,136,512]{2,1,0:T(8,128)(2,1)S(1)}, u32[]{:S(2)}, u32[]{:S(2)}) %collective-permute-start.5) | collective-permute-done | bytes 557088 | tf_op jit(solution)/shard_map/ppermute | solution.py:457
  40.7 0.8 %left_fold.4 = (bf16[2,136,512]{2,1,0:T(8,128)(2,1)}, bf16[2,136,512]{2,1,0:T(8,128)(2,1)S(1)}) custom-call(bf16[4,136,512]{2,1,0:T(8,128)(2,1)S(1)} %get-tuple-element.83.kept_ref, bf16[4,136,512]{2,1,0:T(8,128)(2,1)S(1)} %collective-permute-done.5.received_ref, bf16[16,8,512]{2,1,0:T(8,128)(2,1)} %get-tuple-element.71.refs_0_), custom_call_target="tpu_custom_call" | custom-call | bytes 1245184 | tf_op jit(solution)/shard_map/left_fold/pallas_call | solution.py:508
  41.5 0.1 collective-permute-start.6
  41.6 3.4 %collective-permute-done.1.received_ref = bf16[4,96,512]{2,1,0:T(8,128)(2,1)S(1)} collective-permute-done((bf16[4,96,512]{2,1,0:T(8,128)(2,1)}, bf16[4,96,512]{2,1,0:T(8,128)(2,1)S(1)}, u32[]{:S(2)}, u32[]{:S(2)}) %collective-permute-start.1) | collective-permute-done | bytes 393248 | tf_op jit(solution)/shard_map/ppermute | solution.py:457
  45.0 0.7 %right_fold.4 = (bf16[2,96,512]{2,1,0:T(8,128)(2,1)}, bf16[2,96,512]{2,1,0:T(8,128)(2,1)S(1)}) custom-call(bf16[4,96,512]{2,1,0:T(8,128)(2,1)S(1)} %get-tuple-element.75.kept_ref, bf16[4,96,512]{2,1,0:T(8,128)(2,1)S(1)} %collective-permute-done.1.received_ref), custom_call_target="tpu_custom_call" | custom-call | bytes 786432 | tf_op jit(solution)/shard_map/right_fold/pallas_call | solution.py:508
  45.8 4.0 %all-to-all-start.1 = ((bf16[16,8,512]{2,1,0:T(8,128)(2,1)}), bf16[16,8,512]{2,1,0:T(8,128)(2,1)S(1)}, u32[]{:S(2)}, u32[]{:S(2)}) async-start(bf16[16,8,512]{2,1,0:T(8,128)(2,1)} %get-tuple-element.71.refs_0_), calls=%async_computation.1 | async-start | bytes 262144 | tf_op jit(solution)/shard_map/all_to_all | solution.py:749
  49.8 0.2 collective-permute-done.6.received_ref
  50.0 0.7 %left_fold.5 = (bf16[1,136,512]{2,1,0:T(8,128)(2,1)}, bf16[1,136,512]{2,1,0:T(8,128)(2,1)S(1)}) custom-call(bf16[2,136,512]{2,1,0:T(8,128)(2,1)S(1)} %get-tuple-element.85.kept_ref, bf16[2,136,512]{2,1,0:T(8,128)(2,1)S(1)} %collective-permute-done.6.received_ref), custom_call_target="tpu_custom_call" | custom-call | bytes 557056 | tf_op jit(solution)/shard_map/left_fold/pallas_call | solution.py:508
  50.7 2.7 %collective-permute-start.7 = (bf16[1,136,512]{2,1,0:T(8,128)(2,1)}, bf16[1,136,512]{2,1,0:T(8,128)(2,1)S(1)}, u32[]{:S(2)}, u32[]{:S(2)}) collective-permute-start(bf16[1,136,512]{2,1,0:T(8,128)(2,1)} %get-tuple-element.88), channel_id=1, source_target_pairs={{0,8},{1,3},{2,10},{3,1},{4,12},{5,7},{6,14},{7,5},{8,0},{9,11},{1... | collective-permute-start | bytes 417800 | tf_op jit(solution)/shard_map/ppermute | solution.py:457
  53.4 0.8 %collective-permute-done.2.received_ref = bf16[2,96,512]{2,1,0:T(8,128)(2,1)S(1)} collective-permute-done((bf16[2,96,512]{2,1,0:T(8,128)(2,1)}, bf16[2,96,512]{2,1,0:T(8,128)(2,1)S(1)}, u32[]{:S(2)}, u32[]{:S(2)}) %collective-permute-start.2) | collective-permute-done | bytes 196640 | tf_op jit(solution)/shard_map/ppermute | solution.py:457
  54.2 0.7 %right_fold.5 = (bf16[1,96,512]{2,1,0:T(8,128)(2,1)}, bf16[1,96,512]{2,1,0:T(8,128)(2,1)S(1)}) custom-call(bf16[2,96,512]{2,1,0:T(8,128)(2,1)S(1)} %get-tuple-element.77.kept_ref, bf16[2,96,512]{2,1,0:T(8,128)(2,1)S(1)} %collective-permute-done.2.received_ref), custom_call_target="tpu_custom_call" | custom-call | bytes 393216 | tf_op jit(solution)/shard_map/right_fold/pallas_call | solution.py:508
  54.9 0.1 collective-permute-start.3
  54.9 2.8 %all-to-all-done.1.returned_ref = bf16[16,8,512]{2,1,0:T(8,128)(2,1)S(1)} async-done(((bf16[16,8,512]{2,1,0:T(8,128)(2,1)}), bf16[16,8,512]{2,1,0:T(8,128)(2,1)S(1)}, u32[]{:S(2)}, u32[]{:S(2)}) %all-to-all-start.1) | async-done | bytes 131104 | tf_op jit(solution)/shard_map/all_to_all | solution.py:749
  57.7 2.1 %nodes.1 = bf16[256,512]{1,0:T(8,128)(2,1)} custom-call(f32[256,512]{1,0:T(8,128)} %get-tuple-element.70.total_hbm, bf16[16,8,512]{2,1,0:T(8,128)(2,1)S(1)} %all-to-all-done.1.returned_ref, s32[1,8,16]{2,1,0:T(8,128)} %bitcast.10), custom_call_target="tpu_custom_call" | custom-call | bytes 655872 | tf_op jit(solution)/shard_map/nodes/pallas_call | solution.py:508
  59.9 0.7 %left_shares.1 = (f32[64,512]{1,0:T(8,128)}, f32[32,512]{1,0:T(8,128)}, f32[32,512]{1,0:T(8,128)}, f32[2,512]{1,0:T(2,128)}) custom-call(bf16[1,136,512]{2,1,0:T(8,128)(2,1)S(1)} %get-tuple-element.87.kept, bf16[1,136,512]{2,1,0:T(8,128)(2,1)S(1)} %collective-permute-done.7.received), custom_call_target="tpu_custom_call" | custom-call | bytes 278528 | tf_op jit(solution)/shard_map/left_shares/pallas_call | solution.py:508
  60.6 1.2 %collective-permute-done.3.received = bf16[1,96,512]{2,1,0:T(8,128)(2,1)S(1)} collective-permute-done((bf16[1,96,512]{2,1,0:T(8,128)(2,1)}, bf16[1,96,512]{2,1,0:T(8,128)(2,1)S(1)}, u32[]{:S(2)}, u32[]{:S(2)}) %collective-permute-start.3) | collective-permute-done | bytes 98336 | tf_op jit(solution)/shard_map/ppermute | solution.py:457
  61.8 0.7 %right_shares.1 = f32[96,512]{1,0:T(8,128)} custom-call(bf16[1,96,512]{2,1,0:T(8,128)(2,1)S(1)} %get-tuple-element.79.kept, bf16[1,96,512]{2,1,0:T(8,128)(2,1)S(1)} %collective-permute-done.3.received, f32[2,512]{1,0:T(2,128)} %get-tuple-element.49.refs_0_), custom_call_target="tpu_custom_call" | custom-call | bytes 200704 | tf_op jit(solution)/shard_map/right_shares/pallas_call | solution.py:508
  (15 shorter events, 0.1 us)
Async XLA Ops:
  2.5 15.3 %all-to-all-start = ((bf16[16,8,512]{2,1,0:T(8,128)(2,1)}), bf16[16,8,512]{2,1,0:T(8,128)(2,1)S(1)}, u32[]{:S(2)}, u32[]{:S(2)}) async-start(bf16[16,8,512]{2,1,0:T(8,128)(2,1)} %bitcast.8), calls=%async_computation | async-start | bytes 262144 | tf_op jit(solution)/shard_map/all_to_all | solution.py:583
  17.8 4.1 %copy-start = (bf16[1024,512]{1,0:T(8,128)(2,1)S(1)}, bf16[1024,512]{1,0:T(8,128)(2,1)}, u32[]{:S(2)}) copy-start(bf16[1024,512]{1,0:T(8,128)(2,1)} %grad_edges_hbm.1) | copy-start | bytes 3145732
  17.8 4.1 %copy-start.3 = (bf16[1024,256]{1,0:T(8,128)(2,1)S(1)}, bf16[1024,256]{1,0:T(8,128)(2,1)}, u32[]{:S(2)}) copy-start(bf16[1024,256]{1,0:T(8,128)(2,1)} %get-tuple-element.65.receive_ref) | copy-start | bytes 1572868
  17.8 4.1 %copy-start.4 = (f32[2,512]{1,0:T(2,128)S(1)}, f32[2,512]{1,0:T(2,128)}, u32[]{:S(2)}) copy-start(f32[2,512]{1,0:T(2,128)} %gains_ref.1) | copy-start | bytes 12292
  21.9 4.1 %copy-start.1 = (bf16[640,1024]{1,0:T(8,128)(2,1)S(1)}, bf16[640,1024]{1,0:T(8,128)(2,1)}, u32[]{:S(2)}) copy-start(bf16[640,1024]{1,0:T(8,128)(2,1)} %get-tuple-element.54.place_hbm.place_ref) | copy-start | bytes 3932164
  21.9 4.1 %copy-start.2 = (bf16[256,512]{1,0:T(8,128)(2,1)S(1)}, bf16[256,512]{1,0:T(8,128)(2,1)}, u32[]{:S(2)}) copy-start(bf16[256,512]{1,0:T(8,128)(2,1)} %node_ref.1) | copy-start | bytes 786436
  21.9 4.1 %copy-start.5 = (bf16[1024,512]{1,0:T(8,128)(2,1)S(1)}, bf16[1024,512]{1,0:T(8,128)(2,1)}, u32[]{:S(2)}) copy-start(bf16[1024,512]{1,0:T(8,128)(2,1)} %edge_ref.1) | copy-start | bytes 3145732
  25.9 4.2 %collective-permute-start.4 = (bf16[8,136,512]{2,1,0:T(8,128)(2,1)}, bf16[8,136,512]{2,1,0:T(8,128)(2,1)S(1)}, u32[]{:S(2)}, u32[]{:S(2)}) collective-permute-start(bf16[8,136,512]{2,1,0:T(8,128)(2,1)} %get-tuple-element.82), channel_id=1, source_target_pairs={{0,1},{1,0},{2,3},{3,2},{4,5},{5,4},{6,7},{7,6},{8,9},{9,8},{10,11... | collective-permute-start | bytes 3342344 | tf_op jit(solution)/shard_map/ppermute | solution.py:713
  29.4 2.8 %collective-permute-start = (bf16[8,96,512]{2,1,0:T(8,128)(2,1)}, bf16[8,96,512]{2,1,0:T(8,128)(2,1)S(1)}, u32[]{:S(2)}, u32[]{:S(2)}) collective-permute-start(bf16[8,96,512]{2,1,0:T(8,128)(2,1)} %get-tuple-element.74), channel_id=1, source_target_pairs={{0,1},{1,0},{2,3},{3,2},{4,5},{5,4},{6,7},{7,6},{8,9},{9,8},{10,11... | collective-permute-start | bytes 2359304 | tf_op jit(solution)/shard_map/ppermute | solution.py:722
  30.9 9.8 %collective-permute-start.5 = (bf16[4,136,512]{2,1,0:T(8,128)(2,1)}, bf16[4,136,512]{2,1,0:T(8,128)(2,1)S(1)}, u32[]{:S(2)}, u32[]{:S(2)}) collective-permute-start(bf16[4,136,512]{2,1,0:T(8,128)(2,1)} %get-tuple-element.84), channel_id=1, source_target_pairs={{0,2},{1,5},{2,0},{3,7},{4,6},{5,1},{6,4},{7,3},{8,10},{9,13},{10,... | collective-permute-start | bytes 1671176 | tf_op jit(solution)/shard_map/ppermute | solution.py:457
  33.0 12.0 %collective-permute-start.1 = (bf16[4,96,512]{2,1,0:T(8,128)(2,1)}, bf16[4,96,512]{2,1,0:T(8,128)(2,1)S(1)}, u32[]{:S(2)}, u32[]{:S(2)}) collective-permute-start(bf16[4,96,512]{2,1,0:T(8,128)(2,1)} %get-tuple-element.76), channel_id=1, source_target_pairs={{0,2},{1,9},{2,0},{3,11},{4,6},{5,13},{6,4},{7,15},{8,10},{9,1},{1... | collective-permute-start | bytes 1179656 | tf_op jit(solution)/shard_map/ppermute | solution.py:457
  41.5 8.5 %collective-permute-start.6 = (bf16[2,136,512]{2,1,0:T(8,128)(2,1)}, bf16[2,136,512]{2,1,0:T(8,128)(2,1)S(1)}, u32[]{:S(2)}, u32[]{:S(2)}) collective-permute-start(bf16[2,136,512]{2,1,0:T(8,128)(2,1)} %get-tuple-element.86), channel_id=1, source_target_pairs={{0,4},{1,9},{2,6},{3,11},{4,0},{5,13},{6,2},{7,15},{8,12},{9,1},{1... | collective-permute-start | bytes 835592 | tf_op jit(solution)/shard_map/ppermute | solution.py:457
  45.7 8.5 %collective-permute-start.2 = (bf16[2,96,512]{2,1,0:T(8,128)(2,1)}, bf16[2,96,512]{2,1,0:T(8,128)(2,1)S(1)}, u32[]{:S(2)}, u32[]{:S(2)}) collective-permute-start(bf16[2,96,512]{2,1,0:T(8,128)(2,1)} %get-tuple-element.78), channel_id=1, source_target_pairs={{0,4},{1,3},{2,6},{3,1},{4,0},{5,7},{6,2},{7,5},{8,12},{9,11},{10,... | collective-permute-start | bytes 589832 | tf_op jit(solution)/shard_map/ppermute | solution.py:457
  45.8 12.0 %all-to-all-start.1 = ((bf16[16,8,512]{2,1,0:T(8,128)(2,1)}), bf16[16,8,512]{2,1,0:T(8,128)(2,1)S(1)}, u32[]{:S(2)}, u32[]{:S(2)}) async-start(bf16[16,8,512]{2,1,0:T(8,128)(2,1)} %get-tuple-element.71.refs_0_), calls=%async_computation.1 | async-start | bytes 262144 | tf_op jit(solution)/shard_map/all_to_all | solution.py:749
  50.7 9.1 %collective-permute-start.7 = (bf16[1,136,512]{2,1,0:T(8,128)(2,1)}, bf16[1,136,512]{2,1,0:T(8,128)(2,1)S(1)}, u32[]{:S(2)}, u32[]{:S(2)}) collective-permute-start(bf16[1,136,512]{2,1,0:T(8,128)(2,1)} %get-tuple-element.88), channel_id=1, source_target_pairs={{0,8},{1,3},{2,10},{3,1},{4,12},{5,7},{6,14},{7,5},{8,0},{9,11},{1... | collective-permute-start | bytes 417800 | tf_op jit(solution)/shard_map/ppermute | solution.py:457
  54.9 6.9 %collective-permute-start.3 = (bf16[1,96,512]{2,1,0:T(8,128)(2,1)}, bf16[1,96,512]{2,1,0:T(8,128)(2,1)S(1)}, u32[]{:S(2)}, u32[]{:S(2)}) collective-permute-start(bf16[1,96,512]{2,1,0:T(8,128)(2,1)} %get-tuple-element.80), channel_id=1, source_target_pairs={{0,8},{1,5},{2,10},{3,7},{4,12},{5,1},{6,14},{7,3},{8,0},{9,13},{1... | collective-permute-start | bytes 294920 | tf_op jit(solution)/shard_map/ppermute | solution.py:457
